TPU v7x, 256 devices: a whole 4x4x8 slice. The times are simulated.
256 devices in a mesh: row: 16 (over z_hi, y, core), col: 16 (over x, z_lo).
Axes of the slice: x: 4, y: 4, z: 8 (z_hi: 2, z_lo: 4; z = z_hi * 4 + z_lo), core: 2. Of those that a mesh axis runs over, the one named last changes fastest.
Arguments:
- output_grad: bfloat16 [1024, 8192], P('col', 'row'), may hold values from -16 to 16
- gate_preact: bfloat16 [1024, 28672], P('row', 'col'), may hold values from -6 to 6
- up_preact: bfloat16 [1024, 28672], P('row', 'col'), may hold values from -6 to 6
- gate_weight: bfloat16 [8192, 28672], P('row', 'col'), may hold values from -0.0625 to 0.0625
- up_weight: bfloat16 [8192, 28672], P('row', 'col'), may hold values from -0.0625 to 0.0625
- down_weight: bfloat16 [28672, 8192], P('col', 'row'), may hold values from -0.03125 to 0.03125
Outputs:
- input_grad: bfloat16 [1024, 8192], P('col', 'row')
- gate_factor: float32 [14336, 28672], P('row', 'col')
All inputs are finite; a program needn't handle non-finite values.
Results may differ from a plain program's by a relative error of at most 0.0049.
Values may be sent and summed in bfloat16 or wider, within the bound.
No kernel may reach another device: no remote copies, remote signals or barrier semaphores. Data moves between devices by JAX's collectives and lax.ppermute only.
A program may use at most 128 MiB of HBM per device.

v0:
```python
import jax
import jax.numpy as jnp
from jax import lax
from jax.sharding import PartitionSpec as P

TOKENS = 1024
SLAB_DEV = 896


def from_root(block, axis, holder):
    block = jnp.where(lax.axis_index(axis) == holder, block, jnp.zeros_like(block))
    return lax.psum(block, axis)


def swiglu_grads(hidden_grad, gate_preact, up_preact):
    gate_float = gate_preact.astype(jnp.float32)
    up_float = up_preact.astype(jnp.float32)
    logistic = jax.nn.sigmoid(gate_float)
    derivative = logistic * (1.0 + gate_float * (1.0 - logistic))
    grad_gate = (hidden_grad * up_float * derivative).astype(jnp.bfloat16)
    grad_up = (hidden_grad * gate_float * logistic).astype(jnp.bfloat16)
    return (grad_gate, grad_up)


def contract_last(left, right):
    return lax.dot_general(
        left, right, (((1,), (1,)), ((), ())), preferred_element_type=jnp.float32
    )


def shards(output_grad, gate_preact, up_preact, gate_weight, up_weight, down_weight):
    cotangent_all = lax.all_gather(output_grad, "col", axis=0, tiled=True)
    hidden_part = contract_last(cotangent_all, down_weight)
    hidden_grad = lax.psum(hidden_part, "row")
    gate_all, up_all = (
        lax.all_gather(gate_preact, "row", axis=0, tiled=True),
        lax.all_gather(up_preact, "row", axis=0, tiled=True),
    )
    grad_gate, grad_up = swiglu_grads(hidden_grad, gate_all, up_all)
    units_dev = grad_gate.shape[1]
    first_unit = lax.axis_index("row") * SLAB_DEV
    owner_column = first_unit // units_dev
    offset = first_unit % units_dev
    own_slab = lax.dynamic_slice_in_dim(grad_gate, offset, SLAB_DEV, 1)
    slab_grads = from_root(own_slab, "col", owner_column)
    gate_factor = (
        lax.dot_general(
            slab_grads, grad_gate, (((0,), (0,)), ((), ())), preferred_element_type=jnp.float32
        )
        / TOKENS
    )
    input_float = lax.psum_scatter(
        contract_last(grad_gate, gate_weight) + contract_last(grad_up, up_weight),
        "col",
        scatter_dimension=0,
        tiled=True,
    )
    return (input_float.astype(jnp.bfloat16), gate_factor)


def solution(mesh):
    return jax.shard_map(
        shards,
        mesh=mesh,
        in_specs=(
            P("col", "row"),
            P("row", "col"),
            P("row", "col"),
            P("row", "col"),
            P("row", "col"),
            P("col", "row"),
        ),
        out_specs=(P("col", "row"), P("row", "col")),
        check_vma=False,
    )
```

profile of v0, /device:TPU:8, one launch (start us, length us, event | category | flops | bytes accessed | tf_op | source)
XLA Modules:
  0.0 746.4 jit_solution(16275275222608679882)
XLA Ops:
  7.2 0.0 copy-start
  7.2 0.0 all-gather.4.cloned.1.call-start
  7.2 0.7 all-gather.4.cloned.1.call-update
  7.9 0.0 all-gather.8.cloned.1.call-start
  8.0 0.7 all-gather.8.cloned.1.call-update
  8.7 0.0 all-gather.6.cloned.1.call-start
  8.7 0.7 all-gather.6.cloned.1.call-update
  9.4 0.0 all-reduce.3.cloned.1.call-start
  9.4 85.3 %all-gather.4.cloned.1.call-done = bf16[1024,512]{1,0:T(8,128)(2,1)} async-done(((bf16[64,512]{1,0:T(8,128)(2,1)}), bf16[1024,512]{1,0:T(8,128)(2,1)}) %all-gather.4.cloned.1.call-update) | async-done | bytes 1048592 | tf_op jit(solution)/shard_map/all_gather | solution.py:32
  94.7 0.0 copy-done
  94.7 6.3 fusion.15
  101.0 0.0 all-reduce.3.cloned.1.call-update
  101.1 0.0 all-reduce.5.cloned.1.call-start
  101.1 68.6 %all-gather.8.cloned.1.call-done = bf16[1024,1792]{1,0:T(8,128)(2,1)} async-done(((bf16[64,1792]{1,0:T(8,128)(2,1)}), bf16[1024,1792]{1,0:T(8,128)(2,1)}) %all-gather.8.cloned.1.call-update) | async-done | bytes 3670032 | tf_op jit(solution)/shard_map/all_gather | solution.py:36
  169.7 72.1 %all-gather.6.cloned.1.call-done = bf16[1024,1792]{1,0:T(8,128)(2,1)} async-done(((bf16[64,1792]{1,0:T(8,128)(2,1)}), bf16[1024,1792]{1,0:T(8,128)(2,1)}) %all-gather.6.cloned.1.call-update) | async-done | bytes 3670032 | tf_op jit(solution)/shard_map/all_gather | solution.py:37
  241.8 214.2 %all-reduce.3.cloned.1.call-done = f32[1024,1792]{1,0:T(8,128)} async-done(((f32[1024,1792]{1,0:T(8,128)}), f32[1024,1792]{1,0:T(8,128)}) %all-reduce.3.cloned.1.call-update) | async-done | bytes 7340048 | tf_op jit(solution)/shard_map/psum | solution.py:34
  455.9 6.8 fusion.6
  462.7 0.0 copy-start.1
  462.7 1.9 copy-done.1
  464.6 2.3 dynamic-slice_select_fusion
  466.9 0.0 all-reduce.5.cloned.1.call-update
  466.9 0.0 reduce-scatter.2.cloned.1.call-start
  467.0 0.0 copy-start.2
  467.0 0.0 copy-start.3
  467.0 4.8 fusion.16
  471.9 0.0 copy-done.2
  471.9 6.7 fusion.11
  478.6 0.0 reduce-scatter.2.cloned.1.call-update
  478.6 167.0 %all-reduce.5.cloned.1.call-done = bf16[1024,896]{1,0:T(8,128)(2,1)} async-done(((bf16[1024,896]{1,0:T(8,128)(2,1)}), bf16[1024,896]{1,0:T(8,128)(2,1)}) %all-reduce.5.cloned.1.call-update) | async-done | bytes 1835024 | tf_op jit(solution)/shard_map/psum | solution.py:12
  645.6 8.9 %convolution_multiply_fusion = f32[896,1792]{1,0:T(8,128)} fusion(bf16[1024,896]{1,0:T(8,128)(2,1)} %all-reduce.5.cloned.1.call-done, bf16[1024,1792]{1,0:T(8,128)(2,1)} %copy-done.1), kind=kOutput, calls=%fused_computation.12 | convolution fusion | flops 3289939968 | bytes 11927552 | tf_op jit(solution)/shard_map/dot_general | solution.py:47
  654.5 83.5 %reduce-scatter.2.cloned.1.call-done = f32[64,512]{1,0:T(8,128)} async-done(((f32[1024,512]{1,0:T(8,128)}), f32[64,512]{1,0:T(8,128)}) %reduce-scatter.2.cloned.1.call-update) | async-done | bytes 131088 | tf_op jit(solution)/shard_map/reduce_scatter | solution.py:52
  738.0 1.5 convert_element_type.19
  (1 shorter events, 0.0 us)
Async XLA Ops:
  7.2 87.5 %copy-start = (bf16[1792,512]{1,0:T(8,128)(2,1)S(1)}, bf16[1792,512]{1,0:T(8,128)(2,1)}, u32[]{:S(2)}) copy-start(bf16[1792,512]{1,0:T(8,128)(2,1)} %param.11) | copy-start | bytes 5505028
  7.2 87.5 %all-gather.4.cloned.1.call-start = ((), (), s32[]{:S(2)}) async-start(), calls=%async_computation.1 | async-start | bytes 1114112 | tf_op jit(solution)/shard_map/all_gather | solution.py:32
  7.9 161.8 %all-gather.8.cloned.1.call-start = ((), (), s32[]{:S(2)}) async-start(), calls=%async_computation.4 | async-start | bytes 3899392 | tf_op jit(solution)/shard_map/all_gather | solution.py:36
  8.7 233.1 %all-gather.6.cloned.1.call-start = ((), (), s32[]{:S(2)}) async-start(), calls=%async_computation.3 | async-start | bytes 3899392 | tf_op jit(solution)/shard_map/all_gather | solution.py:37
  9.4 446.5 %all-reduce.3.cloned.1.call-start = ((), (), s32[]{:S(2)}) async-start(), calls=%async_computation.2 | async-start | bytes 14680064 | tf_op jit(solution)/shard_map/psum | solution.py:34
  101.1 544.6 %all-reduce.5.cloned.1.call-start = ((), (), s32[]{:S(2)}) async-start(), calls=%async_computation.6 | async-start | bytes 3670016 | tf_op jit(solution)/shard_map/psum | solution.py:12
  462.7 1.9 copy-start.1
  466.9 271.1 %reduce-scatter.2.cloned.1.call-start = ((), (), s32[]{:S(2)}) async-start(), calls=%async_computation.5 | async-start | bytes 2228224 | tf_op jit(solution)/shard_map/reduce_scatter | solution.py:52
  467.0 4.9 copy-start.2
  467.0 4.9 copy-start.3
Sparse Core Ops, SparseCore 0:
  9.8 84.8 all-gather.3
  97.4 72.2 all-gather.7
  172.4 69.2 all-gather.5
  244.3 211.5 all-reduce.2
  467.1 178.5 all-reduce.4
  648.2 89.7 reduce-scatter.1
where the time goes:
time: 747 us; the launch traced here: 746 us
  waiting for transfers between devices  693 us (93%)
  matrix products  26.8 us (4%)
  between operations  14.2 us (2%)
  other arithmetic  10.6 us (1%)
    psum x1, waiting for transfers between devices, shards(): hidden_grad = lax.psum(hidden_part, 'row')  214 us
    psum x1, waiting for transfers between devices, from_root(): return lax.psum(block, axis)  167 us
    all_gather x1, waiting for transfers between devices, shards(): cotangent_all = lax.all_gather(output_grad, 'col', axis=0, tiled=True)  85.3 us
    reduce_scatter x1, waiting for transfers between devices, shards(): lax.psum_scatter(contract_last(grad_gate, gate_weight) + contract_last(gr...  83.5 us
    all_gather x1, waiting for transfers between devices, shards(): lax.all_gather(up_preact, 'row', axis=0, tiled=True)  72.1 us
    all_gather x1, waiting for transfers between devices, shards(): lax.all_gather(gate_preact, 'row', axis=0, tiled=True)  68.6 us
    dot_general x3, matrix products, contract_last(): lax.dot_general(left, right, (((1,), (1,)), ((), ())), preferred_element_...  17.9 us
  transfers between devices with their start and end apart: 6, of which 6 were waited for; matrix products, arithmetic and copies ran while one was open for 4% of the time, Pallas kernels for 0%

commit v1 on v0

v1 whole, which is shorter than its diff:
```python
import jax
import jax.numpy as jnp
from jax import lax
from jax.sharding import Mesh
from jax.sharding import PartitionSpec as P

TOKENS = 1024
BF = jnp.bfloat16
F32 = jnp.float32
SIZES = (2, 4, 2, 4, 4)
AXES = ("zh", "y", "core", "x", "zl")
ROW = ("zh", "y", "core")
COL = ("x", "zl")


def swap(block, axis, k):
    n = SIZES[AXES.index(axis)]
    return lax.ppermute(block, axis, [(i, i ^ k) for i in range(n)])


def put(buf, block, *index):
    start = list(index) + [0] * (buf.ndim - len(index))
    lead = buf.ndim - block.ndim
    return lax.dynamic_update_slice(buf, block.reshape((1,) * lead + block.shape), start)


def pick(array, index, axis):
    return lax.dynamic_index_in_dim(array, index, axis, keepdims=False)


def swiglu_grads(hidden_grad, gate_preact, up_preact):
    gate_float = gate_preact.astype(F32)
    up_float = up_preact.astype(F32)
    logistic = jax.nn.sigmoid(gate_float)
    derivative = logistic * (1.0 + gate_float * (1.0 - logistic))
    grad_gate = (hidden_grad * up_float * derivative).astype(BF)
    grad_up = (hidden_grad * gate_float * logistic).astype(BF)
    return (grad_gate, grad_up)


def contract_last(left, right):
    return lax.dot_general(
        left, right, (((left.ndim - 1,), (1,)), ((), ())), preferred_element_type=F32
    )


def scatter_pairs(half):
    pairs = []
    for zh in range(2):
        for y in range(4):
            for core in range(2):
                for x in range(2):
                    for zl in range(4):
                        src = (((zh * 4 + y) * 2 + core) * 4 + x) * 4 + zl
                        dst = (((x * 4 + zl) * 2 + half) * 4 + y) * 4 + core * 2 + zh
                        pairs.append((src, dst))
    return pairs


def shards(output_grad, gate_preact, up_preact, gate_weight, up_weight, down_weight):
    zh, y, core, x, zl = (lax.axis_index(a) for a in AXES)
    units = gate_preact.shape[1]
    half_units = units // 2
    width = output_grad.shape[1]

    def at_zl(buf, block, which):
        return put(buf, block, (which & 1) ^ core, which >> 1)

    run = jnp.zeros((2, 2, 64, width), BF)
    run = at_zl(run, output_grad, zl)
    for k in (1, 2, 3):
        run = at_zl(run, swap(output_grad, "zl", k), zl ^ k)
    cot = jnp.zeros((2, 4, 2, 64, width), BF)
    cot = lax.dynamic_update_slice(cot, run[:, None], (0, x, 0, 0, 0))
    for k in (1, 3, 2):
        cot = lax.dynamic_update_slice(cot, swap(run, "x", k)[:, None], (0, x ^ k, 0, 0, 0))
    pre = jnp.stack([gate_preact, up_preact])
    pre_far = swap(pre, "zh", 1)

    sent = contract_last(cot[1].reshape(512, width), down_weight).astype(BF)
    kept = contract_last(cot[0].reshape(512, width), down_weight)
    part = (kept + swap(sent, "core", 1).astype(F32)).reshape(2, 4, 64, units)
    hidden = pick(part, y, 1)
    got = [swap(pick(part, y ^ k, 1).astype(BF), "y", k) for k in (1, 3, 2)]
    for block in got:
        hidden = hidden + block.astype(F32)
    hidden = hidden + swap(hidden.astype(BF), "zh", 1).astype(F32)

    low = jnp.where(zh == 0, pre, pre_far)
    high = jnp.where(zh == 0, pre_far, pre)
    grad_gate, grad_up = swiglu_grads(
        hidden, jnp.stack([low[0], high[0]]), jnp.stack([low[1], high[1]])
    )

    own = pick(grad_gate, zh, 0)
    piece0 = lax.ppermute(own[:, :half_units], AXES, scatter_pairs(0))
    piece1 = lax.ppermute(own[:, half_units:], AXES, scatter_pairs(1))
    piece = jnp.where(core == 0, piece0, piece1)
    srun = put(jnp.zeros((4, 64, half_units), BF), piece, zl)
    for k in (1, 2, 3):
        srun = put(srun, swap(piece, "zl", k), zl ^ k)
    slab = put(jnp.zeros((4, 4, 64, half_units), BF), srun, x)

    both = jnp.stack([grad_gate, grad_up])
    run2 = jnp.zeros((2, 4, 2, 64, units), BF)
    run2 = lax.dynamic_update_slice(run2, both[:, None], (0, y, 0, 0, 0))
    for k in (1, 3, 2):
        run2 = lax.dynamic_update_slice(run2, swap(both, "y", k)[:, None], (0, y ^ k, 0, 0, 0))
    full = jnp.zeros((2, 4, 2, 2, 64, units), BF)
    full = lax.dynamic_update_slice(full, run2[:, :, None], (0, 0, core, 0, 0, 0))
    full = lax.dynamic_update_slice(
        full, swap(run2, "core", 1)[:, :, None], (0, 0, 1 - core, 0, 0, 0)
    )
    for k in (1, 3, 2):
        slab = put(slab, swap(srun, "x", k), x ^ k)

    gate_all = full[0].reshape(TOKENS, units)
    up_all = full[1].reshape(TOKENS, units)
    partial = contract_last(gate_all, gate_weight) + contract_last(up_all, up_weight)
    partial = partial.reshape(2, 2, 2, 2, 64, width).transpose(3, 0, 1, 2, 4, 5)
    partial = partial.reshape(4, 4, 64, width)
    mine = pick(partial, x, 0)
    for block in [swap(pick(partial, x ^ k, 0).astype(BF), "x", k) for k in (1, 3, 2)]:
        mine = mine + block.astype(F32)
    result = pick(mine, zl, 0)
    for block in [swap(pick(mine, zl ^ k, 0).astype(BF), "zl", k) for k in (1, 2, 3)]:
        result = result + block.astype(F32)

    gate_factor = (
        lax.dot_general(
            slab.reshape(TOKENS, half_units),
            gate_all,
            (((0,), (0,)), ((), ())),
            preferred_element_type=F32,
        )
        / TOKENS
    )
    return (result.astype(BF), gate_factor)


def solution(mesh):
    fine = Mesh(mesh.devices.reshape(SIZES), AXES)
    return jax.shard_map(
        shards,
        mesh=fine,
        in_specs=(P(COL, ROW), P(ROW, COL), P(ROW, COL), P(ROW, COL), P(ROW, COL), P(COL, ROW)),
        out_specs=(P(COL, ROW), P(ROW, COL)),
        check_vma=False,
    )
```

time: 747 us -> 220 us (0.29)
  the two profiles are of different devices: /device:TPU:8 before, /device:TPU:34 now
where the time goes in v1:
time: 220 us
  waiting for transfers between devices  119 us (54%)
  starting transfers between devices  65 us (30%)
  matrix products  17.3 us (8%)
  local copies, waits for them, and re-layouts  14.1 us (6%)
  other arithmetic  3.81 us (2%)
    ppermute x28, waiting for transfers between devices, swap(): return lax.ppermute(block, axis, [(i, i ^ k) for i in range(n)])  106 us
    ppermute x28, starting transfers between devices, swap(): return lax.ppermute(block, axis, [(i, i ^ k) for i in range(n)])  61.8 us
    ppermute x1, waiting for transfers between devices, shards(): piece0 = lax.ppermute(own[:, :half_units], AXES, scatter_pairs(0))  12.3 us
    dot_general x4, matrix products, contract_last(): lax.dot_general(left, right, (((left.ndim - 1,), (1,)), ((), ())), prefer...  10.8 us
    dot_general x1, matrix products, shards(): lax.dot_general(slab.reshape(TOKENS, half_units), gate_all, (((0,), (0,))...  6.43 us
  transfers between devices with their start and end apart: 30, of which 19 were waited for; matrix products, arithmetic and copies ran while one was open for 14% of the time, Pallas kernels for 0%

profile of v1, /device:TPU:34, one launch (start us, length us, event | category | flops | bytes accessed | tf_op | source)
XLA Modules:
  0.0 219.9 jit_solution(2679774012836492196)
XLA Ops:
  0.8 3.3 %collective-permute-start.1 = (bf16[64,512]{1,0:T(8,128)(2,1)}, bf16[64,512]{1,0:T(8,128)(2,1)S(1)}, u32[]{:S(2)}, u32[]{:S(2)}) collective-permute-start(bf16[64,512]{1,0:T(8,128)(2,1)} %param.6), channel_id=1, source_target_pairs={{0,2},{1,3},{2,0},{3,1},{4,6},{5,7},{6,4},{7,5},{8,10},{9,11},{10,... | collective-permute-start | bytes 196616 | tf_op jit(solution)/shard_map/ppermute | solution.py:18
  5.5 3.8 %collective-permute-done.1 = bf16[64,512]{1,0:T(8,128)(2,1)S(1)} collective-permute-done((bf16[64,512]{1,0:T(8,128)(2,1)}, bf16[64,512]{1,0:T(8,128)(2,1)S(1)}, u32[]{:S(2)}, u32[]{:S(2)}) %collective-permute-start.1) | collective-permute-done | bytes 65568 | tf_op jit(solution)/shard_map/ppermute | solution.py:18
  10.8 2.2 collective-permute-start.4
  14.5 5.0 %collective-permute-done.3 = bf16[2,2,64,512]{3,2,1,0:T(8,128)(2,1)S(1)} collective-permute-done((bf16[2,2,64,512]{3,2,1,0:T(8,128)(2,1)S(1)}, bf16[2,2,64,512]{3,2,1,0:T(8,128)(2,1)S(1)}, u32[]{:S(2)}, u32[]{:S(2)}) %collective-permute-start.3) | collective-permute-done | bytes 262176 | tf_op jit(solution)/shard_map/ppermute | solution.py:18
  19.5 3.9 %collective-permute-done.4 = bf16[2,2,64,512]{3,2,1,0:T(8,128)(2,1)S(1)} collective-permute-done((bf16[2,2,64,512]{3,2,1,0:T(8,128)(2,1)S(1)}, bf16[2,2,64,512]{3,2,1,0:T(8,128)(2,1)S(1)}, u32[]{:S(2)}, u32[]{:S(2)}) %collective-permute-start.4) | collective-permute-done | bytes 262176 | tf_op jit(solution)/shard_map/ppermute | solution.py:18
  24.6 2.4 %convolution_convert_fusion = bf16[512,1792]{1,0:T(8,128)(2,1)} fusion(bf16[512,512]{1,0:T(8,128)(2,1)S(1)} %bitcast.146, bf16[1792,512]{1,0:T(8,128)(2,1)S(1)} %copy-done), kind=kOutput, calls=%fused_computation.4 | convolution fusion | flops 940441600 | bytes 4194304 | tf_op jit(solution)/shard_map/dot_general | solution.py:42
  27.0 5.8 %collective-permute-start.11 = (bf16[2,64,1792]{2,1,0:T(8,128)(2,1)S(1)}, bf16[2,64,1792]{2,1,0:T(8,128)(2,1)}, u32[]{:S(2)}, u32[]{:S(2)}) collective-permute-start(bf16[2,64,1792]{2,1,0:T(8,128)(2,1)S(1)} %pad_maximum_fusion.1), channel_id=1, source_target_pairs={{0,128},{128,0},{1,129},{129,1},{2,130},{130,2},{3,131},{131,3},{4... | collective-permute-start | bytes 1376264 | tf_op jit(solution)/shard_map/ppermute | solution.py:18
  32.9 2.6 %convert_add_fusion = f32[512,1792]{1,0:T(8,128)S(1)} fusion(bf16[512,1792]{1,0:T(8,128)(2,1)} %collective-permute-done.6, bf16[512,512]{1,0:T(8,128)(2,1)S(1)} %bitcast.140, bf16[1792,512]{1,0:T(8,128)(2,1)S(1)} %copy-done), kind=kOutput, calls=%fused_computation.3 | convolution fusion | flops 941359104 | bytes 7864320 | tf_op jit(solution)/shard_map/dot_general | solution.py:42
  35.7 3.3 %collective-permute-start.9 = (bf16[2,64,1792]{2,1,0:T(8,128)(2,1)S(1)}, bf16[2,64,1792]{2,1,0:T(8,128)(2,1)S(1)}, u32[]{:S(2)}, u32[]{:S(2)}) collective-permute-start(bf16[2,64,1792]{2,1,0:T(8,128)(2,1)S(1)} %get-tuple-element.10), channel_id=1, source_target_pairs={{0,64},{32,96},{64,0},{96,32},{1,65},{33,97},{65,1},{97,33},{2,66}... | collective-permute-start | bytes 1376264 | tf_op jit(solution)/shard_map/ppermute | solution.py:18
  40.0 14.1 %collective-permute-done.11 = bf16[2,64,1792]{2,1,0:T(8,128)(2,1)} collective-permute-done((bf16[2,64,1792]{2,1,0:T(8,128)(2,1)S(1)}, bf16[2,64,1792]{2,1,0:T(8,128)(2,1)}, u32[]{:S(2)}, u32[]{:S(2)}) %collective-permute-start.11) | collective-permute-done | bytes 458784 | tf_op jit(solution)/shard_map/ppermute | solution.py:18
  55.2 4.5 %collective-permute-done.8 = bf16[2,64,1792]{2,1,0:T(8,128)(2,1)S(1)} collective-permute-done((bf16[2,64,1792]{2,1,0:T(8,128)(2,1)S(1)}, bf16[2,64,1792]{2,1,0:T(8,128)(2,1)S(1)}, u32[]{:S(2)}, u32[]{:S(2)}) %collective-permute-start.8) | collective-permute-done | bytes 458784 | tf_op jit(solution)/shard_map/ppermute | solution.py:18
  60.3 4.0 %collective-permute-start.10 = (bf16[2,64,1792]{2,1,0:T(8,128)(2,1)S(1)}, bf16[2,64,1792]{2,1,0:T(8,128)(2,1)S(1)}, u32[]{:S(2)}, u32[]{:S(2)}) collective-permute-start(bf16[2,64,1792]{2,1,0:T(8,128)(2,1)S(1)} %get-tuple-element.4), channel_id=1, source_target_pairs={{0,128},{128,0},{1,129},{129,1},{2,130},{130,2},{3,131},{131,3},{4... | collective-permute-start | bytes 1376264 | tf_op jit(solution)/shard_map/ppermute | solution.py:18
  64.4 21.9 %collective-permute-done.10 = bf16[2,64,1792]{2,1,0:T(8,128)(2,1)S(1)} collective-permute-done((bf16[2,64,1792]{2,1,0:T(8,128)(2,1)S(1)}, bf16[2,64,1792]{2,1,0:T(8,128)(2,1)S(1)}, u32[]{:S(2)}, u32[]{:S(2)}) %collective-permute-start.10) | collective-permute-done | bytes 458784 | tf_op jit(solution)/shard_map/ppermute | solution.py:18
  86.9 1.7 collective-permute-start.12
  91.4 2.2 %broadcast_in_dim.49 = bf16[2,4,2,64,1792]{4,3,2,1,0:T(8,128)(2,1)} broadcast(bf16[]{:T(256)} %constant.64.clone.1), dimensions={} | broadcast | bytes 3670018 | tf_op jit(solution)/shard_map/broadcast_in_dim | solution.py:105
  94.6 15.6 %collective-permute-done.12 = bf16[2,2,64,1792]{3,2,1,0:T(8,128)(2,1)S(1)} collective-permute-done((bf16[2,2,64,1792]{3,2,1,0:T(8,128)(2,1)S(1)}, bf16[2,2,64,1792]{3,2,1,0:T(8,128)(2,1)S(1)}, u32[]{:S(2)}, u32[]{:S(2)}) %collective-permute-start.12) | collective-permute-done | bytes 917536 | tf_op jit(solution)/shard_map/ppermute | solution.py:18
  111.1 18.3 %collective-permute-done.13 = bf16[2,2,64,1792]{3,2,1,0:T(8,128)(2,1)S(1)} collective-permute-done((bf16[2,2,64,1792]{3,2,1,0:T(8,128)(2,1)S(1)}, bf16[2,2,64,1792]{3,2,1,0:T(8,128)(2,1)S(1)}, u32[]{:S(2)}, u32[]{:S(2)}) %collective-permute-start.13) | collective-permute-done | bytes 917536 | tf_op jit(solution)/shard_map/ppermute | solution.py:18
  132.4 1.9 collective-permute-start.22
  135.6 12.3 %collective-permute-done.22 = bf16[64,896]{1,0:T(8,128)(2,1)S(1)} collective-permute-done((bf16[64,896]{1,0:T(8,128)(2,1)S(1)}, bf16[64,896]{1,0:T(8,128)(2,1)S(1)}, u32[]{:S(2)}, u32[]{:S(2)}) %collective-permute-start.22) | collective-permute-done | bytes 114720 | tf_op jit(solution)/shard_map/ppermute | solution.py:96
  148.2 3.4 %collective-permute-start.26 = (bf16[64,896]{1,0:T(8,128)(2,1)S(1)}, bf16[64,896]{1,0:T(8,128)(2,1)S(1)}, u32[]{:S(2)}, u32[]{:S(2)}) collective-permute-start(bf16[64,896]{1,0:T(8,128)(2,1)S(1)} %get-tuple-element.3), channel_id=1, source_target_pairs={{0,3},{1,2},{2,1},{3,0},{4,7},{5,6},{6,5},{7,4},{8,11},{9,10},{10,... | collective-permute-start | bytes 344072 | tf_op jit(solution)/shard_map/ppermute | solution.py:18
  154.0 3.6 %collective-permute-done.26 = bf16[64,896]{1,0:T(8,128)(2,1)S(1)} collective-permute-done((bf16[64,896]{1,0:T(8,128)(2,1)S(1)}, bf16[64,896]{1,0:T(8,128)(2,1)S(1)}, u32[]{:S(2)}, u32[]{:S(2)}) %collective-permute-start.26) | collective-permute-done | bytes 114720 | tf_op jit(solution)/shard_map/ppermute | solution.py:18
  157.6 3.2 %collective-permute-start.27 = (bf16[4,64,896]{2,1,0:T(8,128)(2,1)S(1)}, bf16[4,64,896]{2,1,0:T(8,128)(2,1)S(1)}, u32[]{:S(2)}, u32[]{:S(2)}) collective-permute-start(bf16[4,64,896]{2,1,0:T(8,128)(2,1)S(1)} %bitcast_dynamic-update-slice_fusion.14), channel_id=1, source_target_pairs={{0,4},{4,0},{8,12},{12,8},{1,5},{5,1},{9,13},{13,9},{2,6},{6,2},{1... | collective-permute-start | bytes 1376264 | tf_op jit(solution)/shard_map/ppermute | solution.py:18
  160.8 10.5 %collective-permute-start.28 = (bf16[4,64,896]{2,1,0:T(8,128)(2,1)S(1)}, bf16[4,64,896]{2,1,0:T(8,128)(2,1)S(1)}, u32[]{:S(2)}, u32[]{:S(2)}) collective-permute-start(bf16[4,64,896]{2,1,0:T(8,128)(2,1)S(1)} %bitcast_dynamic-update-slice_fusion.14), channel_id=1, source_target_pairs={{0,12},{4,8},{8,4},{12,0},{1,13},{5,9},{9,5},{13,1},{2,14},{6,10},... | collective-permute-start | bytes 1376264 | tf_op jit(solution)/shard_map/ppermute | solution.py:18
  173.0 2.5 %bitcast_dynamic-update-slice_fusion = bf16[2,4,2,2,64,1792]{5,4,3,2,1,0:T(8,128)(2,1)S(1)} fusion(bf16[2,4,2,2,64,1792]{5,4,3,2,1,0:T(8,128)(2,1)S(1)} %broadcast_in_dim.48, s32[]{:T(128)S(6)} %select_n.128, bf16[2,4,2,64,1792]{4,3,2,1,0:T(8,128)(2,1)} %bitcast_dynamic-update-slice_fusion.5), kind=kLoop, calls=%fused_computation.1 | loop fusion | bytes 7340036 | tf_op jit(solution)/shard_map/dynamic_update_slice | solution.py:110
  175.5 2.5 %bitcast_dynamic-update-slice_fusion.1 = bf16[2,4,2,2,64,1792]{5,4,3,2,1,0:T(8,128)(2,1)S(1)} fusion(bf16[2,4,2,2,64,1792]{5,4,3,2,1,0:T(8,128)(2,1)S(1)} %bitcast_dynamic-update-slice_fusion, s32[]{:T(128)S(6)} %select_n.129, bf16[2,4,2,64,1792]{4,3,2,1,0:T(8,128)(2,1)} %collective-permute-done.15), kind=kLoop, calls=%fused_computation.2 | loop fusion | bytes 7340036 | tf_op jit(solution)/shard_map/dynamic_update_slice | solution.py:111
  178.8 3.7 %fusion.33 = f32[1024,512]{1,0:T(8,128)S(1)} fusion(bf16[1024,1792]{1,0:T(8,128)(2,1)S(1)} %bitcast.138, bf16[512,1792]{1,0:T(8,128)(2,1)} %param.10), kind=kOutput, calls=%fused_computation.81 | convolution fusion | flops 1879048192 | bytes 7602176 | tf_op jit(solution)/shard_map/dot_general | solution.py:42
  182.6 2.1 convolution_add_fusion
  185.0 12.1 %collective-permute-start.18 = (bf16[4,64,512]{2,1,0:T(8,128)(2,1)S(1)}, bf16[4,64,512]{2,1,0:T(8,128)(2,1)S(1)}, u32[]{:S(2)}, u32[]{:S(2)}) collective-permute-start(bf16[4,64,512]{2,1,0:T(8,128)(2,1)S(1)} %get-tuple-element.12), channel_id=1, source_target_pairs={{0,8},{4,12},{8,0},{12,4},{1,9},{5,13},{9,1},{13,5},{2,10},{6,14},... | collective-permute-start | bytes 786440 | tf_op jit(solution)/shard_map/ppermute | solution.py:18
  198.9 5.5 %collective-permute-done.18 = bf16[4,64,512]{2,1,0:T(8,128)(2,1)S(1)} collective-permute-done((bf16[4,64,512]{2,1,0:T(8,128)(2,1)S(1)}, bf16[4,64,512]{2,1,0:T(8,128)(2,1)S(1)}, u32[]{:S(2)}, u32[]{:S(2)}) %collective-permute-start.18) | collective-permute-done | bytes 262176 | tf_op jit(solution)/shard_map/ppermute | solution.py:18
  204.3 3.2 %collective-permute-done.17 = bf16[4,64,512]{2,1,0:T(8,128)(2,1)S(1)} collective-permute-done((bf16[4,64,512]{2,1,0:T(8,128)(2,1)S(1)}, bf16[4,64,512]{2,1,0:T(8,128)(2,1)S(1)}, u32[]{:S(2)}, u32[]{:S(2)}) %collective-permute-start.17) | collective-permute-done | bytes 262176 | tf_op jit(solution)/shard_map/ppermute | solution.py:18
  210.7 2.1 collective-permute-start.19
  212.8 6.4 %convolution_multiply_fusion = f32[896,1792]{1,0:T(8,128)} fusion(bf16[1024,896]{1,0:T(8,128)(2,1)S(1)} %bitcast.141, bf16[1024,1792]{1,0:T(8,128)(2,1)S(1)} %bitcast.137), kind=kOutput, calls=%fused_computation | convolution fusion | flops 3289939968 | bytes 11927552 | tf_op jit(solution)/shard_map/dot_general | solution.py:130
  (87 shorter events, 29.3 us)
Async XLA Ops:
  0.6 24.0 %copy-start = (bf16[1792,512]{1,0:T(8,128)(2,1)S(1)}, bf16[1792,512]{1,0:T(8,128)(2,1)}, u32[]{:S(2)}) copy-start(bf16[1792,512]{1,0:T(8,128)(2,1)} %param.11) | copy-start | bytes 5505028
  0.6 4.8 %collective-permute-start = (bf16[64,512]{1,0:T(8,128)(2,1)}, bf16[64,512]{1,0:T(8,128)(2,1)S(1)}, u32[]{:S(2)}, u32[]{:S(2)}) collective-permute-start(bf16[64,512]{1,0:T(8,128)(2,1)} %param.6), channel_id=1, source_target_pairs={{0,1},{1,0},{2,3},{3,2},{4,5},{5,4},{6,7},{7,6},{8,9},{9,8},{10,11... | collective-permute-start | bytes 196616 | tf_op jit(solution)/shard_map/ppermute | solution.py:18
  0.8 8.4 %collective-permute-start.1 = (bf16[64,512]{1,0:T(8,128)(2,1)}, bf16[64,512]{1,0:T(8,128)(2,1)S(1)}, u32[]{:S(2)}, u32[]{:S(2)}) collective-permute-start(bf16[64,512]{1,0:T(8,128)(2,1)} %param.6), channel_id=1, source_target_pairs={{0,2},{1,3},{2,0},{3,1},{4,6},{5,7},{6,4},{7,5},{8,10},{9,11},{10,... | collective-permute-start | bytes 196616 | tf_op jit(solution)/shard_map/ppermute | solution.py:18
  4.1 6.0 %collective-permute-start.2 = (bf16[64,512]{1,0:T(8,128)(2,1)}, bf16[64,512]{1,0:T(8,128)(2,1)S(1)}, u32[]{:S(2)}, u32[]{:S(2)}) collective-permute-start(bf16[64,512]{1,0:T(8,128)(2,1)} %param.6), channel_id=1, source_target_pairs={{0,3},{1,2},{2,1},{3,0},{4,7},{5,6},{6,5},{7,4},{8,11},{9,10},{10,... | collective-permute-start | bytes 196616 | tf_op jit(solution)/shard_map/ppermute | solution.py:18
  10.1 9.3 %collective-permute-start.3 = (bf16[2,2,64,512]{3,2,1,0:T(8,128)(2,1)S(1)}, bf16[2,2,64,512]{3,2,1,0:T(8,128)(2,1)S(1)}, u32[]{:S(2)}, u32[]{:S(2)}) collective-permute-start(bf16[2,2,64,512]{3,2,1,0:T(8,128)(2,1)S(1)} %bitcast_dynamic-update-slice_fusion.18), channel_id=1, source_target_pairs={{0,4},{4,0},{8,12},{12,8},{1,5},{5,1},{9,13},{13,9},{2,6},{6,2},{1... | collective-permute-start | bytes 786440 | tf_op jit(solution)/shard_map/ppermute | solution.py:18
  10.8 12.7 %collective-permute-start.4 = (bf16[2,2,64,512]{3,2,1,0:T(8,128)(2,1)S(1)}, bf16[2,2,64,512]{3,2,1,0:T(8,128)(2,1)S(1)}, u32[]{:S(2)}, u32[]{:S(2)}) collective-permute-start(bf16[2,2,64,512]{3,2,1,0:T(8,128)(2,1)S(1)} %bitcast_dynamic-update-slice_fusion.18), channel_id=1, source_target_pairs={{0,12},{4,8},{8,4},{12,0},{1,13},{5,9},{9,5},{13,1},{2,14},{6,10},... | collective-permute-start | bytes 786440 | tf_op jit(solution)/shard_map/ppermute | solution.py:18
  12.9 11.5 %collective-permute-start.5 = (bf16[2,2,64,512]{3,2,1,0:T(8,128)(2,1)S(1)}, bf16[2,2,64,512]{3,2,1,0:T(8,128)(2,1)S(1)}, u32[]{:S(2)}, u32[]{:S(2)}) collective-permute-start(bf16[2,2,64,512]{3,2,1,0:T(8,128)(2,1)S(1)} %bitcast_dynamic-update-slice_fusion.18), channel_id=1, source_target_pairs={{0,8},{4,12},{8,0},{12,4},{1,9},{5,13},{9,1},{13,5},{2,10},{6,14},... | collective-permute-start | bytes 786440 | tf_op jit(solution)/shard_map/ppermute | solution.py:18
  27.0 5.9 %collective-permute-start.6 = (bf16[512,1792]{1,0:T(8,128)(2,1)}, bf16[512,1792]{1,0:T(8,128)(2,1)}, u32[]{:S(2)}, u32[]{:S(2)}) collective-permute-start(bf16[512,1792]{1,0:T(8,128)(2,1)} %convolution_convert_fusion), channel_id=1, source_target_pairs={{0,16},{16,0},{1,17},{17,1},{2,18},{18,2},{3,19},{19,3},{4,20},{20... | collective-permute-start | bytes 5505032 | tf_op jit(solution)/shard_map/ppermute | solution.py:18
  27.0 27.1 %collective-permute-start.11 = (bf16[2,64,1792]{2,1,0:T(8,128)(2,1)S(1)}, bf16[2,64,1792]{2,1,0:T(8,128)(2,1)}, u32[]{:S(2)}, u32[]{:S(2)}) collective-permute-start(bf16[2,64,1792]{2,1,0:T(8,128)(2,1)S(1)} %pad_maximum_fusion.1), channel_id=1, source_target_pairs={{0,128},{128,0},{1,129},{129,1},{2,130},{130,2},{3,131},{131,3},{4... | collective-permute-start | bytes 1376264 | tf_op jit(solution)/shard_map/ppermute | solution.py:18
  35.7 19.6 %collective-permute-start.9 = (bf16[2,64,1792]{2,1,0:T(8,128)(2,1)S(1)}, bf16[2,64,1792]{2,1,0:T(8,128)(2,1)S(1)}, u32[]{:S(2)}, u32[]{:S(2)}) collective-permute-start(bf16[2,64,1792]{2,1,0:T(8,128)(2,1)S(1)} %get-tuple-element.10), channel_id=1, source_target_pairs={{0,64},{32,96},{64,0},{96,32},{1,65},{33,97},{65,1},{97,33},{2,66}... | collective-permute-start | bytes 1376264 | tf_op jit(solution)/shard_map/ppermute | solution.py:18
  38.9 20.8 %collective-permute-start.8 = (bf16[2,64,1792]{2,1,0:T(8,128)(2,1)S(1)}, bf16[2,64,1792]{2,1,0:T(8,128)(2,1)S(1)}, u32[]{:S(2)}, u32[]{:S(2)}) collective-permute-start(bf16[2,64,1792]{2,1,0:T(8,128)(2,1)S(1)} %get-tuple-element.9), channel_id=1, source_target_pairs={{0,96},{32,64},{64,32},{96,0},{1,97},{33,65},{65,33},{97,1},{2,98}... | collective-permute-start | bytes 1376264 | tf_op jit(solution)/shard_map/ppermute | solution.py:18
  40.0 20.1 %collective-permute-start.7 = (bf16[2,64,1792]{2,1,0:T(8,128)(2,1)S(1)}, bf16[2,64,1792]{2,1,0:T(8,128)(2,1)S(1)}, u32[]{:S(2)}, u32[]{:S(2)}) collective-permute-start(bf16[2,64,1792]{2,1,0:T(8,128)(2,1)S(1)} %get-tuple-element.8), channel_id=1, source_target_pairs={{0,32},{32,0},{64,96},{96,64},{1,33},{33,1},{65,97},{97,65},{2,34}... | collective-permute-start | bytes 1376264 | tf_op jit(solution)/shard_map/ppermute | solution.py:18
  60.3 25.9 %collective-permute-start.10 = (bf16[2,64,1792]{2,1,0:T(8,128)(2,1)S(1)}, bf16[2,64,1792]{2,1,0:T(8,128)(2,1)S(1)}, u32[]{:S(2)}, u32[]{:S(2)}) collective-permute-start(bf16[2,64,1792]{2,1,0:T(8,128)(2,1)S(1)} %get-tuple-element.4), channel_id=1, source_target_pairs={{0,128},{128,0},{1,129},{129,1},{2,130},{130,2},{3,131},{131,3},{4... | collective-permute-start | bytes 1376264 | tf_op jit(solution)/shard_map/ppermute | solution.py:18
  86.9 23.3 %collective-permute-start.12 = (bf16[2,2,64,1792]{3,2,1,0:T(8,128)(2,1)S(1)}, bf16[2,2,64,1792]{3,2,1,0:T(8,128)(2,1)S(1)}, u32[]{:S(2)}, u32[]{:S(2)}) collective-permute-start(bf16[2,2,64,1792]{3,2,1,0:T(8,128)(2,1)S(1)} %pad_maximum_fusion), channel_id=1, source_target_pairs={{0,32},{32,0},{64,96},{96,64},{1,33},{33,1},{65,97},{97,65},{2,34}... | collective-permute-start | bytes 2752520 | tf_op jit(solution)/shard_map/ppermute | solution.py:18
  88.5 41.0 %collective-permute-start.13 = (bf16[2,2,64,1792]{3,2,1,0:T(8,128)(2,1)S(1)}, bf16[2,2,64,1792]{3,2,1,0:T(8,128)(2,1)S(1)}, u32[]{:S(2)}, u32[]{:S(2)}) collective-permute-start(bf16[2,2,64,1792]{3,2,1,0:T(8,128)(2,1)S(1)} %pad_maximum_fusion), channel_id=1, source_target_pairs={{0,96},{32,64},{64,32},{96,0},{1,97},{33,65},{65,33},{97,1},{2,98}... | collective-permute-start | bytes 2752520 | tf_op jit(solution)/shard_map/ppermute | solution.py:18
  90.0 41.3 %collective-permute-start.14 = (bf16[2,2,64,1792]{3,2,1,0:T(8,128)(2,1)S(1)}, bf16[2,2,64,1792]{3,2,1,0:T(8,128)(2,1)S(1)}, u32[]{:S(2)}, u32[]{:S(2)}) collective-permute-start(bf16[2,2,64,1792]{3,2,1,0:T(8,128)(2,1)S(1)} %pad_maximum_fusion), channel_id=1, source_target_pairs={{0,64},{32,96},{64,0},{96,32},{1,65},{33,97},{65,1},{97,33},{2,66}... | collective-permute-start | bytes 2752520 | tf_op jit(solution)/shard_map/ppermute | solution.py:18
  132.3 43.2 %collective-permute-start.15 = (bf16[2,4,2,64,1792]{4,3,2,1,0:T(8,128)(2,1)}, bf16[2,4,2,64,1792]{4,3,2,1,0:T(8,128)(2,1)}, u32[]{:S(2)}, u32[]{:S(2)}) collective-permute-start(bf16[2,4,2,64,1792]{4,3,2,1,0:T(8,128)(2,1)} %bitcast_dynamic-update-slice_fusion.5), channel_id=1, source_target_pairs={{0,16},{16,0},{1,17},{17,1},{2,18},{18,2},{3,19},{19,3},{4,20},{20... | collective-permute-start | bytes 11010056 | tf_op jit(solution)/shard_map/ppermute | solution.py:18
  132.4 15.5 %collective-permute-start.22 = (bf16[64,896]{1,0:T(8,128)(2,1)S(1)}, bf16[64,896]{1,0:T(8,128)(2,1)S(1)}, u32[]{:S(2)}, u32[]{:S(2)}) collective-permute-start(bf16[64,896]{1,0:T(8,128)(2,1)S(1)} %get-tuple-element.28), channel_id=1, source_target_pairs={{0,0},{1,32},{2,64},{3,96},{4,128},{5,160},{6,192},{7,224},{16,2},... | collective-permute-start | bytes 344072 | tf_op jit(solution)/shard_map/ppermute | solution.py:96
  134.3 13.6 %collective-permute-start.23 = (bf16[64,896]{1,0:T(8,128)(2,1)S(1)}, bf16[64,896]{1,0:T(8,128)(2,1)S(1)}, u32[]{:S(2)}, u32[]{:S(2)}) collective-permute-start(bf16[64,896]{1,0:T(8,128)(2,1)S(1)} %get-tuple-element.27), channel_id=1, source_target_pairs={{0,16},{1,48},{2,80},{3,112},{4,144},{5,176},{6,208},{7,240},{16,1... | collective-permute-start | bytes 344072 | tf_op jit(solution)/shard_map/ppermute | solution.py:97
  148.0 4.9 %collective-permute-start.24 = (bf16[64,896]{1,0:T(8,128)(2,1)S(1)}, bf16[64,896]{1,0:T(8,128)(2,1)S(1)}, u32[]{:S(2)}, u32[]{:S(2)}) collective-permute-start(bf16[64,896]{1,0:T(8,128)(2,1)S(1)} %get-tuple-element.3), channel_id=1, source_target_pairs={{0,1},{1,0},{2,3},{3,2},{4,5},{5,4},{6,7},{7,6},{8,9},{9,8},{10,11... | collective-permute-start | bytes 344072 | tf_op jit(solution)/shard_map/ppermute | solution.py:18
  148.1 5.9 %collective-permute-start.25 = (bf16[64,896]{1,0:T(8,128)(2,1)S(1)}, bf16[64,896]{1,0:T(8,128)(2,1)S(1)}, u32[]{:S(2)}, u32[]{:S(2)}) collective-permute-start(bf16[64,896]{1,0:T(8,128)(2,1)S(1)} %get-tuple-element.3), channel_id=1, source_target_pairs={{0,2},{1,3},{2,0},{3,1},{4,6},{5,7},{6,4},{7,5},{8,10},{9,11},{10,... | collective-permute-start | bytes 344072 | tf_op jit(solution)/shard_map/ppermute | solution.py:18
  148.2 9.4 %collective-permute-start.26 = (bf16[64,896]{1,0:T(8,128)(2,1)S(1)}, bf16[64,896]{1,0:T(8,128)(2,1)S(1)}, u32[]{:S(2)}, u32[]{:S(2)}) collective-permute-start(bf16[64,896]{1,0:T(8,128)(2,1)S(1)} %get-tuple-element.3), channel_id=1, source_target_pairs={{0,3},{1,2},{2,1},{3,0},{4,7},{5,6},{6,5},{7,4},{8,11},{9,10},{10,... | collective-permute-start | bytes 344072 | tf_op jit(solution)/shard_map/ppermute | solution.py:18
  157.6 14.5 %collective-permute-start.27 = (bf16[4,64,896]{2,1,0:T(8,128)(2,1)S(1)}, bf16[4,64,896]{2,1,0:T(8,128)(2,1)S(1)}, u32[]{:S(2)}, u32[]{:S(2)}) collective-permute-start(bf16[4,64,896]{2,1,0:T(8,128)(2,1)S(1)} %bitcast_dynamic-update-slice_fusion.14), channel_id=1, source_target_pairs={{0,4},{4,0},{8,12},{12,8},{1,5},{5,1},{9,13},{13,9},{2,6},{6,2},{1... | collective-permute-start | bytes 1376264 | tf_op jit(solution)/shard_map/ppermute | solution.py:18
  160.8 37.9 %collective-permute-start.28 = (bf16[4,64,896]{2,1,0:T(8,128)(2,1)S(1)}, bf16[4,64,896]{2,1,0:T(8,128)(2,1)S(1)}, u32[]{:S(2)}, u32[]{:S(2)}) collective-permute-start(bf16[4,64,896]{2,1,0:T(8,128)(2,1)S(1)} %bitcast_dynamic-update-slice_fusion.14), channel_id=1, source_target_pairs={{0,12},{4,8},{8,4},{12,0},{1,13},{5,9},{9,5},{13,1},{2,14},{6,10},... | collective-permute-start | bytes 1376264 | tf_op jit(solution)/shard_map/ppermute | solution.py:18
  171.3 27.5 %collective-permute-start.29 = (bf16[4,64,896]{2,1,0:T(8,128)(2,1)S(1)}, bf16[4,64,896]{2,1,0:T(8,128)(2,1)S(1)}, u32[]{:S(2)}, u32[]{:S(2)}) collective-permute-start(bf16[4,64,896]{2,1,0:T(8,128)(2,1)S(1)} %bitcast_dynamic-update-slice_fusion.14), channel_id=1, source_target_pairs={{0,8},{4,12},{8,0},{12,4},{1,9},{5,13},{9,1},{13,5},{2,10},{6,14},... | collective-permute-start | bytes 1376264 | tf_op jit(solution)/shard_map/ppermute | solution.py:18
  185.0 19.4 %collective-permute-start.18 = (bf16[4,64,512]{2,1,0:T(8,128)(2,1)S(1)}, bf16[4,64,512]{2,1,0:T(8,128)(2,1)S(1)}, u32[]{:S(2)}, u32[]{:S(2)}) collective-permute-start(bf16[4,64,512]{2,1,0:T(8,128)(2,1)S(1)} %get-tuple-element.12), channel_id=1, source_target_pairs={{0,8},{4,12},{8,0},{12,4},{1,9},{5,13},{9,1},{13,5},{2,10},{6,14},... | collective-permute-start | bytes 786440 | tf_op jit(solution)/shard_map/ppermute | solution.py:18
  197.1 10.5 %collective-permute-start.17 = (bf16[4,64,512]{2,1,0:T(8,128)(2,1)S(1)}, bf16[4,64,512]{2,1,0:T(8,128)(2,1)S(1)}, u32[]{:S(2)}, u32[]{:S(2)}) collective-permute-start(bf16[4,64,512]{2,1,0:T(8,128)(2,1)S(1)} %get-tuple-element.13), channel_id=1, source_target_pairs={{0,12},{4,8},{8,4},{12,0},{1,13},{5,9},{9,5},{13,1},{2,14},{6,10},... | collective-permute-start | bytes 786440 | tf_op jit(solution)/shard_map/ppermute | solution.py:18
  197.1 11.9 %collective-permute-start.16 = (bf16[4,64,512]{2,1,0:T(8,128)(2,1)S(1)}, bf16[4,64,512]{2,1,0:T(8,128)(2,1)S(1)}, u32[]{:S(2)}, u32[]{:S(2)}) collective-permute-start(bf16[4,64,512]{2,1,0:T(8,128)(2,1)S(1)} %get-tuple-element.11), channel_id=1, source_target_pairs={{0,4},{4,0},{8,12},{12,8},{1,5},{5,1},{9,13},{13,9},{2,6},{6,2},{1... | collective-permute-start | bytes 786440 | tf_op jit(solution)/shard_map/ppermute | solution.py:18
  209.2 10.0 %collective-permute-start.21 = (bf16[64,512]{1,0:T(8,128)(2,1)S(1)}, bf16[64,512]{1,0:T(8,128)(2,1)S(1)}, u32[]{:S(2)}, u32[]{:S(2)}) collective-permute-start(bf16[64,512]{1,0:T(8,128)(2,1)S(1)} %get-tuple-element.21), channel_id=1, source_target_pairs={{0,3},{1,2},{2,1},{3,0},{4,7},{5,6},{6,5},{7,4},{8,11},{9,10},{10,... | collective-permute-start | bytes 196616 | tf_op jit(solution)/shard_map/ppermute | solution.py:18
  209.3 9.9 %collective-permute-start.20 = (bf16[64,512]{1,0:T(8,128)(2,1)S(1)}, bf16[64,512]{1,0:T(8,128)(2,1)S(1)}, u32[]{:S(2)}, u32[]{:S(2)}) collective-permute-start(bf16[64,512]{1,0:T(8,128)(2,1)S(1)} %get-tuple-element.22), channel_id=1, source_target_pairs={{0,2},{1,3},{2,0},{3,1},{4,6},{5,7},{6,4},{7,5},{8,10},{9,11},{10,... | collective-permute-start | bytes 196616 | tf_op jit(solution)/shard_map/ppermute | solution.py:18
  210.7 8.5 %collective-permute-start.19 = (bf16[64,512]{1,0:T(8,128)(2,1)S(1)}, bf16[64,512]{1,0:T(8,128)(2,1)S(1)}, u32[]{:S(2)}, u32[]{:S(2)}) collective-permute-start(bf16[64,512]{1,0:T(8,128)(2,1)S(1)} %get-tuple-element.20), channel_id=1, source_target_pairs={{0,1},{1,0},{2,3},{3,2},{4,5},{5,4},{6,7},{7,6},{8,9},{9,8},{10,11... | collective-permute-start | bytes 196616 | tf_op jit(solution)/shard_map/ppermute | solution.py:18
  212.8 7.1 %copy-start.1 = (bf16[1792,512]{1,0:T(8,128)(2,1)S(1)}, bf16[1792,512]{1,0:T(8,128)(2,1)}, u32[]{:S(2)}) copy-start(bf16[1792,512]{1,0:T(8,128)(2,1)} %param.11) | copy-start | bytes 5505028
  (3 other events, 8.8 us)

commit v2 on v1

v2 whole, which is shorter than its diff:
```python
import jax
import jax.numpy as jnp
from jax import lax
from jax.sharding import Mesh
from jax.sharding import PartitionSpec as P

TOKENS = 1024
ROWS = 32
BF = jnp.bfloat16
F32 = jnp.float32
SIZES = (2, 4, 2, 4, 4)
AXES = ("zh", "y", "core", "x", "zl")
ROW = ("zh", "y", "core")
COL = ("x", "zl")


def swap(block, axis, k):
    n = SIZES[AXES.index(axis)]
    return lax.ppermute(block, axis, [(i, i ^ k) for i in range(n)])


def after(block, *deps):
    return lax.optimization_barrier((block, deps))[0]


def put(buf, block, index, axis):
    start = [0] * buf.ndim
    start[axis] = index
    return lax.dynamic_update_slice(buf, jnp.expand_dims(block, axis), start)


def pick(array, index, axis):
    return lax.dynamic_index_in_dim(array, index, axis, keepdims=False)


def swiglu_grads(hidden_grad, gate_preact, up_preact):
    gate_float = gate_preact.astype(F32)
    up_float = up_preact.astype(F32)
    logistic = jax.nn.sigmoid(gate_float)
    derivative = logistic * (1.0 + gate_float * (1.0 - logistic))
    grad_gate = (hidden_grad * up_float * derivative).astype(BF)
    grad_up = (hidden_grad * gate_float * logistic).astype(BF)
    return (grad_gate, grad_up)


def contract_last(left, right):
    return lax.dot_general(left, right, (((1,), (1,)), ((), ())), preferred_element_type=F32)


def device(zh, y, core, x, zl):
    return (((zh * 4 + y) * 2 + core) * 4 + x) * 4 + zl


def scatter_pairs(half):
    pairs = []
    for zh in range(2):
        for y in range(4):
            for core in range(2):
                for x in range(2):
                    for zl in range(4):
                        dst = device(
                            x, zl, half, (core ^ half) * 2 + (y >> 1), (y & 1) * 2 + zh
                        )
                        pairs.append((device(zh, y, core, x, zl), dst))
    return pairs


def home_pairs(k):
    return [
        (core * 4 + zl, core * 4 + (zl ^ k))
        for core in range(2)
        for zl in range(4)
        if ((zl ^ k) & 1) == core
    ]


def shards(output_grad, gate_preact, up_preact, gate_weight, up_weight, down_weight):
    zh, y, core, x, zl = (lax.axis_index(a) for a in AXES)
    units = gate_preact.shape[1]
    half_units = units // 2
    width = output_grad.shape[1]

    def at_zl(buf, block, which):
        start = ((which & 1) ^ core, which >> 1, 0, 0)
        return lax.dynamic_update_slice(buf, block[None, None], start)

    down_far = swap(down_weight, "core", 1)
    run = at_zl(jnp.zeros((2, 2, 64, width), BF), output_grad, zl)
    for k in (1, 2, 3):
        run = at_zl(run, swap(output_grad, "zl", k), zl ^ k)
    pre = after(jnp.stack([gate_preact, up_preact]), run)
    pre_far = swap(pre, "zh", 1)
    cot = put(jnp.zeros((2, 4, 2, 64, width), BF), run, x, 1)
    for k in (1, 3, 2):
        cot = put(cot, swap(run, "x", k), x ^ k, 1)
    near = cot[0]
    far = swap(cot[1], "core", 1)
    gate_far = swap(after(gate_weight, cot), "core", 1)
    up_far = swap(after(up_weight, cot), "core", 1)

    low = jnp.where(zh == 0, pre, pre_far)
    high = jnp.where(zh == 0, pre_far, pre)
    gate_tok = jnp.stack([low[0], high[0]])
    up_tok = jnp.stack([low[1], high[1]])

    def part_of(c):
        rows = slice(c * ROWS, (c + 1) * ROWS)
        part = contract_last(near[:, :, rows].reshape(8 * ROWS, width), down_weight)
        part = part + contract_last(far[:, :, rows].reshape(8 * ROWS, width), down_far)
        return part.reshape(2, 4, ROWS, units)

    def over_y(part, *deps):
        sends = tuple(pick(part, y ^ k, 1).astype(BF) for k in (1, 3, 2))
        sends = after(sends, *deps)
        return [swap(s, "y", k) for s, k in zip(sends, (1, 3, 2))]

    def add_up(part, got):
        hidden = pick(part, y, 1)
        for block in got:
            hidden = hidden + block.astype(F32)
        return hidden

    def grads(c, hidden, far_hidden):
        rows = slice(c * ROWS, (c + 1) * ROWS)
        hidden = hidden + far_hidden.astype(F32)
        return swiglu_grads(hidden, gate_tok[:, rows], up_tok[:, rows])

    part_a = part_of(0)
    part_b = part_of(1)
    got_a = over_y(part_a)
    hidden_a = add_up(part_a, got_a)
    got_b = over_y(part_b, *got_a)
    hfar_a = swap(hidden_a.astype(BF), "zh", 1)
    gate_a, up_a = grads(0, hidden_a, hfar_a)
    both_a = jnp.stack([gate_a, up_a])
    hidden_b = add_up(part_b, got_b)
    hfar_b = swap(hidden_b.astype(BF), "zh", 1)
    both_a = after(both_a, *got_b)
    one_a = swap(both_a, "y", 1)
    three_a = swap(both_a, "y", 3)
    hfar_b, one_a, three_a = lax.optimization_barrier((hfar_b, one_a, three_a))
    gate_b, up_b = grads(1, hidden_b, hfar_b)
    both_b = jnp.stack([gate_b, up_b])

    own = jnp.concatenate([pick(gate_a, zh, 0), pick(gate_b, zh, 0)], 0)
    piece0 = lax.ppermute(own[:, :half_units], AXES, scatter_pairs(0))
    piece1 = lax.ppermute(own[:, half_units:], AXES, scatter_pairs(1))

    def forward(one, three):
        return swap(one[:, 0], "y", 3), swap(three[:, 1], "y", 1)

    def assemble(both, one, three, two):
        full = jnp.zeros((2, 4, 2, ROWS, units), BF)
        full = put(full, both, y, 1)
        full = put(full, one, y ^ 1, 1)
        full = put(full, three, y ^ 3, 1)
        return put(full, jnp.stack(two, 1), y ^ 2, 1)

    def project(full):
        gate_mine = full[0].reshape(8 * ROWS, units)
        up_mine = full[1].reshape(8 * ROWS, units)
        near_sum = contract_last(gate_mine, gate_weight) + contract_last(up_mine, up_weight)
        far_sum = contract_last(gate_mine, gate_far) + contract_last(up_mine, up_far)
        sums = jnp.stack([near_sum, far_sum]).reshape(2, 2, 2, 2, ROWS, width)
        return sums.transpose(3, 1, 2, 0, 4, 5).reshape(4, 2, 2, ROWS, width)

    two_a = forward(one_a, three_a)
    both_b, piece0, piece1, *two_a = lax.optimization_barrier((both_b, piece0, piece1, *two_a))
    piece = jnp.where(core == 0, piece0, piece1)
    one_b = swap(both_b, "y", 1)
    three_b = swap(both_b, "y", 3)
    got = [swap(piece, "zl", k) for k in (1, 2, 3)]
    one_b, three_b, *got = lax.optimization_barrier((one_b, three_b, *got))
    srun = put(jnp.zeros((4, 64, half_units), BF), piece, zl, 0)
    for k in (1, 2, 3):
        srun = put(srun, got[k - 1], zl ^ k, 0)
    two_b = forward(one_b, three_b)
    got = [swap(srun, "x", k) for k in (1, 3, 2)]
    full_a = assemble(both_a, one_a, three_a, two_a)
    full_b = assemble(both_b, one_b, three_b, two_b)
    partial = jnp.concatenate([project(full_a), project(full_b)], 3)
    gate_near = jnp.concatenate([full_a[0], full_b[0]], 2)
    gate_other = swap(gate_near, "core", 1)
    slab = put(jnp.zeros((4, 4, 64, half_units), BF), srun, x, 0)
    for block, k in zip(got, (1, 3, 2)):
        slab = put(slab, block, x ^ k, 0)
    gate_all = jnp.stack([gate_near, gate_other])
    gate_factor = (
        lax.dot_general(
            slab.reshape(TOKENS, half_units),
            gate_all.reshape(TOKENS, units),
            (((0,), (0,)), ((), ())),
            preferred_element_type=F32,
        )
        / TOKENS
    )

    mine = pick(partial, x, 0)
    got = [swap(pick(partial, x ^ k, 0).astype(BF), "x", k) for k in (1, 3, 2)]
    for block in got:
        mine = mine + block.astype(F32)
    mine = after(mine, gate_factor)
    result = pick(mine, zl >> 1, 0)
    for k in (1, 2, 3):
        send = pick(mine, (zl ^ k) >> 1, 0).astype(BF)
        result = result + lax.ppermute(send, ("core", "zl"), home_pairs(k)).astype(F32)
    result = result.astype(BF)
    other_half = swap(result[1], "core", 1)
    input_grad = jnp.where((zl & 1) == core, result[0], other_half)
    return (input_grad, gate_factor)


def solution(mesh):
    fine = Mesh(mesh.devices.reshape(SIZES), AXES)
    return jax.shard_map(
        shards,
        mesh=fine,
        in_specs=(P(COL, ROW), P(ROW, COL), P(ROW, COL), P(ROW, COL), P(ROW, COL), P(COL, ROW)),
        out_specs=(P(COL, ROW), P(ROW, COL)),
        check_vma=False,
    )
```

time: 220 us -> 193 us (0.88)
  the two profiles are of different devices: /device:TPU:34 before, /device:TPU:8 now
where the time goes in v2:
time: 193 us; the launch traced here: 190 us
  starting transfers between devices  84.1 us (44%)
  waiting for transfers between devices  80.7 us (42%)
  matrix products  14.4 us (7%)
  local copies, waits for them, and re-layouts  5.75 us (3%)
  other arithmetic  4.01 us (2%)
    ppermute x38, waiting for transfers between devices, swap(): return lax.ppermute(block, axis, [(i, i ^ k) for i in range(n)])  70.1 us
    ppermute x38, starting transfers between devices, swap(): return lax.ppermute(block, axis, [(i, i ^ k) for i in range(n)])  63.9 us
    ppermute x1, starting transfers between devices, shards(): piece0 = lax.ppermute(own[:, :half_units], AXES, scatter_pairs(0))  14.2 us
    dot_general x12, matrix products, contract_last(): lax.dot_general(left, right, (((1,), (1,)), ((), ())), preferred_element_...  8.13 us
    ppermute x3, waiting for transfers between devices, shards(): lax.ppermute(send, ('core', 'zl'), home_pairs(k)).astype(F32)  6.68 us
    dot_general x1, matrix products, shards(): lax.dot_general(slab.reshape(TOKENS, half_units), gate_all.reshape(TOKENS...  6.29 us
    ppermute x3, starting transfers between devices, shards(): lax.ppermute(send, ('core', 'zl'), home_pairs(k)).astype(F32)  4.77 us
    ppermute x1, waiting for transfers between devices, shards(): piece0 = lax.ppermute(own[:, :half_units], AXES, scatter_pairs(0))  3.92 us
  transfers between devices with their start and end apart: 43, of which 24 were waited for; matrix products, arithmetic and copies ran while one was open for 8% of the time, Pallas kernels for 0%

profile of v2, /device:TPU:8, one launch (start us, length us, event | category | flops | bytes accessed | tf_op | source)
XLA Modules:
  0.0 190.4 jit_solution(13605428710460569670)
XLA Ops:
  2.6 3.3 %collective-permute-start.1 = (bf16[64,512]{1,0:T(8,128)(2,1)}, bf16[64,512]{1,0:T(8,128)(2,1)S(1)}, u32[]{:S(2)}, u32[]{:S(2)}) collective-permute-start(bf16[64,512]{1,0:T(8,128)(2,1)} %param.6), channel_id=1, source_target_pairs={{0,2},{1,3},{2,0},{3,1},{4,6},{5,7},{6,4},{7,5},{8,10},{9,11},{10,... | collective-permute-start | bytes 196616 | tf_op jit(solution)/shard_map/ppermute | solution.py:19
  6.8 3.9 %collective-permute-done.1 = bf16[64,512]{1,0:T(8,128)(2,1)S(1)} collective-permute-done((bf16[64,512]{1,0:T(8,128)(2,1)}, bf16[64,512]{1,0:T(8,128)(2,1)S(1)}, u32[]{:S(2)}, u32[]{:S(2)}) %collective-permute-start.1) | collective-permute-done | bytes 65568 | tf_op jit(solution)/shard_map/ppermute | solution.py:19
  14.9 2.2 %collective-permute-start.4 = (bf16[2,2,64,512]{3,2,1,0:T(8,128)(2,1)S(1)}, bf16[2,2,64,512]{3,2,1,0:T(8,128)(2,1)S(1)}, u32[]{:S(2)}, u32[]{:S(2)}) collective-permute-start(bf16[2,2,64,512]{3,2,1,0:T(8,128)(2,1)S(1)} %bitcast_dynamic-update-slice_fusion.16), channel_id=1, source_target_pairs={{0,12},{4,8},{8,4},{12,0},{1,13},{5,9},{9,5},{13,1},{2,14},{6,10},... | collective-permute-start | bytes 786440 | tf_op jit(solution)/shard_map/ppermute | solution.py:19
  17.9 5.0 %collective-permute-start.12 = (bf16[2,64,1792]{2,1,0:T(8,128)(2,1)S(1)}, bf16[2,64,1792]{2,1,0:T(8,128)(2,1)S(1)}, u32[]{:S(2)}, u32[]{:S(2)}) collective-permute-start(bf16[2,64,1792]{2,1,0:T(8,128)(2,1)S(1)} %pad_maximum_fusion.2), channel_id=1, source_target_pairs={{0,128},{128,0},{1,129},{129,1},{2,130},{130,2},{3,131},{131,3},{4... | collective-permute-start | bytes 1376264 | tf_op jit(solution)/shard_map/ppermute | solution.py:19
  23.0 5.0 %collective-permute-done.4 = bf16[2,2,64,512]{3,2,1,0:T(8,128)(2,1)S(1)} collective-permute-done((bf16[2,2,64,512]{3,2,1,0:T(8,128)(2,1)S(1)}, bf16[2,2,64,512]{3,2,1,0:T(8,128)(2,1)S(1)}, u32[]{:S(2)}, u32[]{:S(2)}) %collective-permute-start.4) | collective-permute-done | bytes 262176 | tf_op jit(solution)/shard_map/ppermute | solution.py:19
  34.1 2.4 %collective-permute-start.10 = (bf16[2,32,1792]{2,1,0:T(8,128)(2,1)S(1)}, bf16[2,32,1792]{2,1,0:T(8,128)(2,1)S(1)}, u32[]{:S(2)}, u32[]{:S(2)}) collective-permute-start(bf16[2,32,1792]{2,1,0:T(8,128)(2,1)S(1)} %get-tuple-element.28), channel_id=1, source_target_pairs={{0,64},{32,96},{64,0},{96,32},{1,65},{33,97},{65,1},{97,33},{2,66}... | collective-permute-start | bytes 688136 | tf_op jit(solution)/shard_map/ppermute | solution.py:19
  36.5 2.4 %collective-permute-start.8 = (bf16[2,32,1792]{2,1,0:T(8,128)(2,1)S(1)}, bf16[2,32,1792]{2,1,0:T(8,128)(2,1)S(1)}, u32[]{:S(2)}, u32[]{:S(2)}) collective-permute-start(bf16[2,32,1792]{2,1,0:T(8,128)(2,1)S(1)} %get-tuple-element.26), channel_id=1, source_target_pairs={{0,32},{32,0},{64,96},{96,64},{1,33},{33,1},{65,97},{97,65},{2,34}... | collective-permute-start | bytes 688136 | tf_op jit(solution)/shard_map/ppermute | solution.py:19
  39.6 4.6 %collective-permute-done.10 = bf16[2,32,1792]{2,1,0:T(8,128)(2,1)S(1)} collective-permute-done((bf16[2,32,1792]{2,1,0:T(8,128)(2,1)S(1)}, bf16[2,32,1792]{2,1,0:T(8,128)(2,1)S(1)}, u32[]{:S(2)}, u32[]{:S(2)}) %collective-permute-start.10) | collective-permute-done | bytes 229408 | tf_op jit(solution)/shard_map/ppermute | solution.py:19
  44.2 3.0 %collective-permute-done.9 = bf16[2,32,1792]{2,1,0:T(8,128)(2,1)S(1)} collective-permute-done((bf16[2,32,1792]{2,1,0:T(8,128)(2,1)S(1)}, bf16[2,32,1792]{2,1,0:T(8,128)(2,1)S(1)}, u32[]{:S(2)}, u32[]{:S(2)}) %collective-permute-start.9) | collective-permute-done | bytes 229408 | tf_op jit(solution)/shard_map/ppermute | solution.py:19
  47.6 5.0 %collective-permute-start.11 = (bf16[2,32,1792]{2,1,0:T(8,128)(2,1)S(1)}, bf16[2,32,1792]{2,1,0:T(8,128)(2,1)S(1)}, u32[]{:S(2)}, u32[]{:S(2)}) collective-permute-start(bf16[2,32,1792]{2,1,0:T(8,128)(2,1)S(1)} %get-tuple-element.54), channel_id=1, source_target_pairs={{0,128},{128,0},{1,129},{129,1},{2,130},{130,2},{3,131},{131,3},{4... | collective-permute-start | bytes 688136 | tf_op jit(solution)/shard_map/ppermute | solution.py:19
  61.3 4.1 %collective-permute-done.14 = bf16[2,32,1792]{2,1,0:T(8,128)(2,1)S(1)} collective-permute-done((bf16[2,32,1792]{2,1,0:T(8,128)(2,1)S(1)}, bf16[2,32,1792]{2,1,0:T(8,128)(2,1)S(1)}, u32[]{:S(2)}, u32[]{:S(2)}) %collective-permute-start.14) | collective-permute-done | bytes 229408 | tf_op jit(solution)/shard_map/ppermute | solution.py:19
  68.7 2.2 %collective-permute-start.17 = (bf16[2,2,32,1792]{3,2,0,1:T(8,128)(2,1)S(1)}, bf16[2,2,32,1792]{3,2,0,1:T(8,128)(2,1)S(1)}, u32[]{:S(2)}, u32[]{:S(2)}) collective-permute-start(bf16[2,2,32,1792]{3,2,0,1:T(8,128)(2,1)S(1)} %copy.15), channel_id=1, source_target_pairs={{0,32},{32,0},{64,96},{96,64},{1,33},{33,1},{65,97},{97,65},{2,34}... | collective-permute-start | bytes 1376264 | tf_op jit(solution)/shard_map/ppermute | solution.py:19
  71.1 6.3 %collective-permute-done.16 = bf16[2,32,1792]{2,1,0:T(8,128)(2,1)S(1)} collective-permute-done((bf16[2,32,1792]{2,1,0:T(8,128)(2,1)S(1)}, bf16[2,32,1792]{2,1,0:T(8,128)(2,1)S(1)}, u32[]{:S(2)}, u32[]{:S(2)}) %collective-permute-start.16) | collective-permute-done | bytes 229408 | tf_op jit(solution)/shard_map/ppermute | solution.py:19
  77.4 2.5 %collective-permute-done.17 = bf16[2,2,32,1792]{3,2,0,1:T(8,128)(2,1)S(1)} collective-permute-done((bf16[2,2,32,1792]{3,2,0,1:T(8,128)(2,1)S(1)}, bf16[2,2,32,1792]{3,2,0,1:T(8,128)(2,1)S(1)}, u32[]{:S(2)}, u32[]{:S(2)}) %collective-permute-start.17) | collective-permute-done | bytes 458784 | tf_op jit(solution)/shard_map/ppermute | solution.py:19
  80.2 14.2 %collective-permute-start.19 = (bf16[64,896]{1,0:T(8,128)(2,1)S(1)}, bf16[64,896]{1,0:T(8,128)(2,1)S(1)}, u32[]{:S(2)}, u32[]{:S(2)}) collective-permute-start(bf16[64,896]{1,0:T(8,128)(2,1)S(1)} %get-tuple-element.93), channel_id=1, source_target_pairs={{0,0},{1,32},{2,64},{3,96},{4,128},{5,160},{6,192},{7,224},{16,8},... | collective-permute-start | bytes 344072 | tf_op jit(solution)/shard_map/ppermute | solution.py:146
  95.8 3.7 %collective-permute-start.22 = (bf16[2,32,1792]{2,1,0:T(8,128)(2,1)S(1)}, bf16[2,32,1792]{2,1,0:T(8,128)(2,1)S(1)}, u32[]{:S(2)}, u32[]{:S(2)}) collective-permute-start(bf16[2,32,1792]{2,1,0:T(8,128)(2,1)S(1)} %slice_bitcast_fusion.4), channel_id=1, source_target_pairs={{0,32},{32,0},{64,96},{96,64},{1,33},{33,1},{65,97},{97,65},{2,34}... | collective-permute-start | bytes 688136 | tf_op jit(solution)/shard_map/ppermute | solution.py:19
  99.6 3.9 %collective-permute-done.19 = bf16[64,896]{1,0:T(8,128)(2,1)S(1)} collective-permute-done((bf16[64,896]{1,0:T(8,128)(2,1)S(1)}, bf16[64,896]{1,0:T(8,128)(2,1)S(1)}, u32[]{:S(2)}, u32[]{:S(2)}) %collective-permute-start.19) | collective-permute-done | bytes 114720 | tf_op jit(solution)/shard_map/ppermute | solution.py:146
  103.6 4.3 %collective-permute-done.22 = bf16[2,32,1792]{2,1,0:T(8,128)(2,1)S(1)} collective-permute-done((bf16[2,32,1792]{2,1,0:T(8,128)(2,1)S(1)}, bf16[2,32,1792]{2,1,0:T(8,128)(2,1)S(1)}, u32[]{:S(2)}, u32[]{:S(2)}) %collective-permute-start.22) | collective-permute-done | bytes 229408 | tf_op jit(solution)/shard_map/ppermute | solution.py:19
  108.2 2.3 %collective-permute-start.28 = (bf16[64,896]{1,0:T(8,128)(2,1)S(1)}, bf16[64,896]{1,0:T(8,128)(2,1)S(1)}, u32[]{:S(2)}, u32[]{:S(2)}) collective-permute-start(bf16[64,896]{1,0:T(8,128)(2,1)S(1)} %get-tuple-element.51), channel_id=1, source_target_pairs={{0,2},{1,3},{2,0},{3,1},{4,6},{5,7},{6,4},{7,5},{8,10},{9,11},{10,... | collective-permute-start | bytes 344072 | tf_op jit(solution)/shard_map/ppermute | solution.py:19
  115.3 4.2 %collective-permute-start.25 = (bf16[2,2,32,1792]{3,2,0,1:T(8,128)(2,1)S(1)}, bf16[2,2,32,1792]{3,2,0,1:T(8,128)(2,1)S(1)}, u32[]{:S(2)}, u32[]{:S(2)}) collective-permute-start(bf16[2,2,32,1792]{3,2,0,1:T(8,128)(2,1)S(1)} %copy.21), channel_id=1, source_target_pairs={{0,32},{32,0},{64,96},{96,64},{1,33},{33,1},{65,97},{97,65},{2,34}... | collective-permute-start | bytes 1376264 | tf_op jit(solution)/shard_map/ppermute | solution.py:19
  120.4 7.2 %collective-permute-done.25 = bf16[2,2,32,1792]{3,2,0,1:T(8,128)(2,1)S(1)} collective-permute-done((bf16[2,2,32,1792]{3,2,0,1:T(8,128)(2,1)S(1)}, bf16[2,2,32,1792]{3,2,0,1:T(8,128)(2,1)S(1)}, u32[]{:S(2)}, u32[]{:S(2)}) %collective-permute-start.25) | collective-permute-done | bytes 458784 | tf_op jit(solution)/shard_map/ppermute | solution.py:19
  127.6 2.3 %collective-permute-start.35 = (bf16[4,64,896]{2,1,0:T(8,128)(2,1)S(1)}, bf16[4,64,896]{2,1,0:T(8,128)(2,1)S(1)}, u32[]{:S(2)}, u32[]{:S(2)}) collective-permute-start(bf16[4,64,896]{2,1,0:T(8,128)(2,1)S(1)} %bitcast_dynamic-update-slice_fusion.12), channel_id=1, source_target_pairs={{0,4},{4,0},{8,12},{12,8},{1,5},{5,1},{9,13},{13,9},{2,6},{6,2},{1... | collective-permute-start | bytes 1376264 | tf_op jit(solution)/shard_map/ppermute | solution.py:19
  129.9 7.3 %collective-permute-start.36 = (bf16[4,64,896]{2,1,0:T(8,128)(2,1)S(1)}, bf16[4,64,896]{2,1,0:T(8,128)(2,1)S(1)}, u32[]{:S(2)}, u32[]{:S(2)}) collective-permute-start(bf16[4,64,896]{2,1,0:T(8,128)(2,1)S(1)} %bitcast_dynamic-update-slice_fusion.12), channel_id=1, source_target_pairs={{0,12},{4,8},{8,4},{12,0},{1,13},{5,9},{9,5},{13,1},{2,14},{6,10},... | collective-permute-start | bytes 1376264 | tf_op jit(solution)/shard_map/ppermute | solution.py:19
  141.2 2.5 %collective-permute-done.31 = bf16[2,32,1792]{2,1,0:T(8,128)(2,1)S(1)} collective-permute-done((bf16[2,32,1792]{2,1,0:T(8,128)(2,1)S(1)}, bf16[2,32,1792]{2,1,0:T(8,128)(2,1)S(1)}, u32[]{:S(2)}, u32[]{:S(2)}) %collective-permute-start.31) | collective-permute-done | bytes 229408 | tf_op jit(solution)/shard_map/ppermute | solution.py:19
  143.6 2.3 %collective-permute-done.30 = bf16[2,32,1792]{2,1,0:T(8,128)(2,1)S(1)} collective-permute-done((bf16[2,32,1792]{2,1,0:T(8,128)(2,1)S(1)}, bf16[2,32,1792]{2,1,0:T(8,128)(2,1)S(1)}, u32[]{:S(2)}, u32[]{:S(2)}) %collective-permute-start.30) | collective-permute-done | bytes 229408 | tf_op jit(solution)/shard_map/ppermute | solution.py:19
  149.8 3.0 %collective-permute-start.34 = (bf16[2,2,64,512]{3,2,1,0:T(8,128)(2,1)S(1)}, bf16[2,2,64,512]{3,2,1,0:T(8,128)(2,1)S(1)}, u32[]{:S(2)}, u32[]{:S(2)}) collective-permute-start(bf16[2,2,64,512]{3,2,1,0:T(8,128)(2,1)S(1)} %get-tuple-element.58), channel_id=1, source_target_pairs={{0,8},{4,12},{8,0},{12,4},{1,9},{5,13},{9,1},{13,5},{2,10},{6,14},... | collective-permute-start | bytes 786440 | tf_op jit(solution)/shard_map/ppermute | solution.py:19
  153.8 9.8 %collective-permute-done.36 = bf16[4,64,896]{2,1,0:T(8,128)(2,1)S(1)} collective-permute-done((bf16[4,64,896]{2,1,0:T(8,128)(2,1)S(1)}, bf16[4,64,896]{2,1,0:T(8,128)(2,1)S(1)}, u32[]{:S(2)}, u32[]{:S(2)}) %collective-permute-start.36) | collective-permute-done | bytes 458784 | tf_op jit(solution)/shard_map/ppermute | solution.py:19
  163.8 4.1 %collective-permute-done.33 = bf16[2,2,64,512]{3,2,1,0:T(8,128)(2,1)S(1)} collective-permute-done((bf16[2,2,64,512]{3,2,1,0:T(8,128)(2,1)S(1)}, bf16[2,2,64,512]{3,2,1,0:T(8,128)(2,1)S(1)}, u32[]{:S(2)}, u32[]{:S(2)}) %collective-permute-start.33) | collective-permute-done | bytes 262176 | tf_op jit(solution)/shard_map/ppermute | solution.py:19
  167.8 2.2 %collective-permute-done.32 = bf16[2,2,64,512]{3,2,1,0:T(8,128)(2,1)S(1)} collective-permute-done((bf16[2,2,64,512]{3,2,1,0:T(8,128)(2,1)S(1)}, bf16[2,2,64,512]{3,2,1,0:T(8,128)(2,1)S(1)}, u32[]{:S(2)}, u32[]{:S(2)}) %collective-permute-start.32) | collective-permute-done | bytes 262176 | tf_op jit(solution)/shard_map/ppermute | solution.py:19
  170.5 6.3 %convolution_multiply_fusion = f32[896,1792]{1,0:T(8,128)} fusion(bf16[1024,896]{1,0:T(8,128)(2,1)S(1)} %bitcast.250, bf16[1024,1792]{1,0:T(8,128)(2,1)S(1)} %bitcast.244), kind=kOutput, calls=%fused_computation | convolution fusion | flops 3289939968 | bytes 11927552 | tf_op jit(solution)/shard_map/dot_general | solution.py:189
  178.1 2.2 %collective-permute-start.40 = (bf16[2,64,512]{2,1,0:T(8,128)(2,1)S(1)}, bf16[2,64,512]{2,1,0:T(8,128)(2,1)S(1)}, u32[]{:S(2)}, u32[]{:S(2)}) collective-permute-start(bf16[2,64,512]{2,1,0:T(8,128)(2,1)S(1)} %get-tuple-element.83), channel_id=1, source_target_pairs={{0,2},{2,0},{17,19},{19,17},{4,6},{6,4},{21,23},{23,21},{8,10},{10... | collective-permute-start | bytes 393224 | tf_op jit(solution)/shard_map/ppermute | solution.py:206
  181.6 4.0 %collective-permute-done.41 = bf16[2,64,512]{2,1,0:T(8,128)(2,1)S(1)} collective-permute-done((bf16[2,64,512]{2,1,0:T(8,128)(2,1)S(1)}, bf16[2,64,512]{2,1,0:T(8,128)(2,1)S(1)}, u32[]{:S(2)}, u32[]{:S(2)}) %collective-permute-start.41) | collective-permute-done | bytes 131104 | tf_op jit(solution)/shard_map/ppermute | solution.py:206
  (141 shorter events, 51.5 us)
Async XLA Ops:
  5.9 27.3 %collective-permute-start.7 = (bf16[1792,512]{1,0:T(8,128)(2,1)}, bf16[1792,512]{1,0:T(8,128)(2,1)S(1)}, u32[]{:S(2)}, u32[]{:S(2)}) collective-permute-start(bf16[1792,512]{1,0:T(8,128)(2,1)} %param.11), channel_id=1, source_target_pairs={{0,16},{16,0},{1,17},{17,1},{2,18},{18,2},{3,19},{19,3},{4,20},{20... | collective-permute-start | bytes 5505032 | tf_op jit(solution)/shard_map/ppermute | solution.py:19
  12.2 10.8 %collective-permute-start.3 = (bf16[2,2,64,512]{3,2,1,0:T(8,128)(2,1)S(1)}, bf16[2,2,64,512]{3,2,1,0:T(8,128)(2,1)S(1)}, u32[]{:S(2)}, u32[]{:S(2)}) collective-permute-start(bf16[2,2,64,512]{3,2,1,0:T(8,128)(2,1)S(1)} %bitcast_dynamic-update-slice_fusion.16), channel_id=1, source_target_pairs={{0,4},{4,0},{8,12},{12,8},{1,5},{5,1},{9,13},{13,9},{2,6},{6,2},{1... | collective-permute-start | bytes 786440 | tf_op jit(solution)/shard_map/ppermute | solution.py:19
  14.9 13.1 %collective-permute-start.4 = (bf16[2,2,64,512]{3,2,1,0:T(8,128)(2,1)S(1)}, bf16[2,2,64,512]{3,2,1,0:T(8,128)(2,1)S(1)}, u32[]{:S(2)}, u32[]{:S(2)}) collective-permute-start(bf16[2,2,64,512]{3,2,1,0:T(8,128)(2,1)S(1)} %bitcast_dynamic-update-slice_fusion.16), channel_id=1, source_target_pairs={{0,12},{4,8},{8,4},{12,0},{1,13},{5,9},{9,5},{13,1},{2,14},{6,10},... | collective-permute-start | bytes 786440 | tf_op jit(solution)/shard_map/ppermute | solution.py:19
  17.1 10.9 %collective-permute-start.5 = (bf16[2,2,64,512]{3,2,1,0:T(8,128)(2,1)S(1)}, bf16[2,2,64,512]{3,2,1,0:T(8,128)(2,1)S(1)}, u32[]{:S(2)}, u32[]{:S(2)}) collective-permute-start(bf16[2,2,64,512]{3,2,1,0:T(8,128)(2,1)S(1)} %bitcast_dynamic-update-slice_fusion.16), channel_id=1, source_target_pairs={{0,8},{4,12},{8,0},{12,4},{1,9},{5,13},{9,1},{13,5},{2,10},{6,14},... | collective-permute-start | bytes 786440 | tf_op jit(solution)/shard_map/ppermute | solution.py:19
  17.9 15.2 %collective-permute-start.12 = (bf16[2,64,1792]{2,1,0:T(8,128)(2,1)S(1)}, bf16[2,64,1792]{2,1,0:T(8,128)(2,1)S(1)}, u32[]{:S(2)}, u32[]{:S(2)}) collective-permute-start(bf16[2,64,1792]{2,1,0:T(8,128)(2,1)S(1)} %pad_maximum_fusion.2), channel_id=1, source_target_pairs={{0,128},{128,0},{1,129},{129,1},{2,130},{130,2},{3,131},{131,3},{4... | collective-permute-start | bytes 1376264 | tf_op jit(solution)/shard_map/ppermute | solution.py:19
  31.0 80.5 %collective-permute-start.24 = (bf16[512,1792]{1,0:T(8,128)(2,1)S(1)}, bf16[512,1792]{1,0:T(8,128)(2,1)S(1)}, u32[]{:S(2)}, u32[]{:S(2)}) collective-permute-start(bf16[512,1792]{1,0:T(8,128)(2,1)S(1)} %copy-done.2), channel_id=1, source_target_pairs={{0,16},{16,0},{1,17},{17,1},{2,18},{18,2},{3,19},{19,3},{4,20},{20... | collective-permute-start | bytes 5505032 | tf_op jit(solution)/shard_map/ppermute | solution.py:19
  34.1 10.2 %collective-permute-start.10 = (bf16[2,32,1792]{2,1,0:T(8,128)(2,1)S(1)}, bf16[2,32,1792]{2,1,0:T(8,128)(2,1)S(1)}, u32[]{:S(2)}, u32[]{:S(2)}) collective-permute-start(bf16[2,32,1792]{2,1,0:T(8,128)(2,1)S(1)} %get-tuple-element.28), channel_id=1, source_target_pairs={{0,64},{32,96},{64,0},{96,32},{1,65},{33,97},{65,1},{97,33},{2,66}... | collective-permute-start | bytes 688136 | tf_op jit(solution)/shard_map/ppermute | solution.py:19
  36.5 10.8 %collective-permute-start.9 = (bf16[2,32,1792]{2,1,0:T(8,128)(2,1)S(1)}, bf16[2,32,1792]{2,1,0:T(8,128)(2,1)S(1)}, u32[]{:S(2)}, u32[]{:S(2)}) collective-permute-start(bf16[2,32,1792]{2,1,0:T(8,128)(2,1)S(1)} %get-tuple-element.27), channel_id=1, source_target_pairs={{0,96},{32,64},{64,32},{96,0},{1,97},{33,65},{65,33},{97,1},{2,98}... | collective-permute-start | bytes 688136 | tf_op jit(solution)/shard_map/ppermute | solution.py:19
  36.5 11.0 %collective-permute-start.8 = (bf16[2,32,1792]{2,1,0:T(8,128)(2,1)S(1)}, bf16[2,32,1792]{2,1,0:T(8,128)(2,1)S(1)}, u32[]{:S(2)}, u32[]{:S(2)}) collective-permute-start(bf16[2,32,1792]{2,1,0:T(8,128)(2,1)S(1)} %get-tuple-element.26), channel_id=1, source_target_pairs={{0,32},{32,0},{64,96},{96,64},{1,33},{33,1},{65,97},{97,65},{2,34}... | collective-permute-start | bytes 688136 | tf_op jit(solution)/shard_map/ppermute | solution.py:19
  47.6 11.3 %collective-permute-start.11 = (bf16[2,32,1792]{2,1,0:T(8,128)(2,1)S(1)}, bf16[2,32,1792]{2,1,0:T(8,128)(2,1)S(1)}, u32[]{:S(2)}, u32[]{:S(2)}) collective-permute-start(bf16[2,32,1792]{2,1,0:T(8,128)(2,1)S(1)} %get-tuple-element.54), channel_id=1, source_target_pairs={{0,128},{128,0},{1,129},{129,1},{2,130},{130,2},{3,131},{131,3},{4... | collective-permute-start | bytes 688136 | tf_op jit(solution)/shard_map/ppermute | solution.py:19
  53.4 12.0 %collective-permute-start.14 = (bf16[2,32,1792]{2,1,0:T(8,128)(2,1)S(1)}, bf16[2,32,1792]{2,1,0:T(8,128)(2,1)S(1)}, u32[]{:S(2)}, u32[]{:S(2)}) collective-permute-start(bf16[2,32,1792]{2,1,0:T(8,128)(2,1)S(1)} %get-tuple-element.31), channel_id=1, source_target_pairs={{0,96},{32,64},{64,32},{96,0},{1,97},{33,65},{65,33},{97,1},{2,98}... | collective-permute-start | bytes 688136 | tf_op jit(solution)/shard_map/ppermute | solution.py:19
  55.4 10.0 %collective-permute-start.15 = (bf16[2,32,1792]{2,1,0:T(8,128)(2,1)S(1)}, bf16[2,32,1792]{2,1,0:T(8,128)(2,1)S(1)}, u32[]{:S(2)}, u32[]{:S(2)}) collective-permute-start(bf16[2,32,1792]{2,1,0:T(8,128)(2,1)S(1)} %get-tuple-element.32), channel_id=1, source_target_pairs={{0,64},{32,96},{64,0},{96,32},{1,65},{33,97},{65,1},{97,33},{2,66}... | collective-permute-start | bytes 688136 | tf_op jit(solution)/shard_map/ppermute | solution.py:19
  65.4 14.4 %collective-permute-start.18 = (bf16[2,2,32,1792]{3,2,1,0:T(8,128)(2,1)S(1)}, bf16[2,2,32,1792]{3,2,1,0:T(8,128)(2,1)S(1)}, u32[]{:S(2)}, u32[]{:S(2)}) collective-permute-start(bf16[2,2,32,1792]{3,2,1,0:T(8,128)(2,1)S(1)} %pad_maximum_fusion.3), channel_id=1, source_target_pairs={{0,96},{32,64},{64,32},{96,0},{1,97},{33,65},{65,33},{97,1},{2,98}... | collective-permute-start | bytes 1376264 | tf_op jit(solution)/shard_map/ppermute | solution.py:19
  67.4 10.0 %collective-permute-start.16 = (bf16[2,32,1792]{2,1,0:T(8,128)(2,1)S(1)}, bf16[2,32,1792]{2,1,0:T(8,128)(2,1)S(1)}, u32[]{:S(2)}, u32[]{:S(2)}) collective-permute-start(bf16[2,32,1792]{2,1,0:T(8,128)(2,1)S(1)} %get-tuple-element.52), channel_id=1, source_target_pairs={{0,128},{128,0},{1,129},{129,1},{2,130},{130,2},{3,131},{131,3},{4... | collective-permute-start | bytes 688136 | tf_op jit(solution)/shard_map/ppermute | solution.py:19
  68.7 11.2 %collective-permute-start.17 = (bf16[2,2,32,1792]{3,2,0,1:T(8,128)(2,1)S(1)}, bf16[2,2,32,1792]{3,2,0,1:T(8,128)(2,1)S(1)}, u32[]{:S(2)}, u32[]{:S(2)}) collective-permute-start(bf16[2,2,32,1792]{3,2,0,1:T(8,128)(2,1)S(1)} %copy.15), channel_id=1, source_target_pairs={{0,32},{32,0},{64,96},{96,64},{1,33},{33,1},{65,97},{97,65},{2,34}... | collective-permute-start | bytes 1376264 | tf_op jit(solution)/shard_map/ppermute | solution.py:19
  80.2 23.3 %collective-permute-start.19 = (bf16[64,896]{1,0:T(8,128)(2,1)S(1)}, bf16[64,896]{1,0:T(8,128)(2,1)S(1)}, u32[]{:S(2)}, u32[]{:S(2)}) collective-permute-start(bf16[64,896]{1,0:T(8,128)(2,1)S(1)} %get-tuple-element.93), channel_id=1, source_target_pairs={{0,0},{1,32},{2,64},{3,96},{4,128},{5,160},{6,192},{7,224},{16,8},... | collective-permute-start | bytes 344072 | tf_op jit(solution)/shard_map/ppermute | solution.py:146
  94.4 9.2 %collective-permute-start.20 = (bf16[64,896]{1,0:T(8,128)(2,1)S(1)}, bf16[64,896]{1,0:T(8,128)(2,1)S(1)}, u32[]{:S(2)}, u32[]{:S(2)}) collective-permute-start(bf16[64,896]{1,0:T(8,128)(2,1)S(1)} %get-tuple-element.92), channel_id=1, source_target_pairs={{0,24},{1,56},{2,88},{3,120},{4,152},{5,184},{6,216},{7,248},{16,1... | collective-permute-start | bytes 344072 | tf_op jit(solution)/shard_map/ppermute | solution.py:147
  95.8 12.1 %collective-permute-start.22 = (bf16[2,32,1792]{2,1,0:T(8,128)(2,1)S(1)}, bf16[2,32,1792]{2,1,0:T(8,128)(2,1)S(1)}, u32[]{:S(2)}, u32[]{:S(2)}) collective-permute-start(bf16[2,32,1792]{2,1,0:T(8,128)(2,1)S(1)} %slice_bitcast_fusion.4), channel_id=1, source_target_pairs={{0,32},{32,0},{64,96},{96,64},{1,33},{33,1},{65,97},{97,65},{2,34}... | collective-permute-start | bytes 688136 | tf_op jit(solution)/shard_map/ppermute | solution.py:19
  103.6 11.7 %collective-permute-start.23 = (bf16[512,1792]{1,0:T(8,128)(2,1)S(1)}, bf16[512,1792]{1,0:T(8,128)(2,1)S(1)}, u32[]{:S(2)}, u32[]{:S(2)}) collective-permute-start(bf16[512,1792]{1,0:T(8,128)(2,1)S(1)} %copy-done), channel_id=1, source_target_pairs={{0,16},{16,0},{1,17},{17,1},{2,18},{18,2},{3,19},{19,3},{4,20},{20... | collective-permute-start | bytes 5505032 | tf_op jit(solution)/shard_map/ppermute | solution.py:19
  107.9 19.6 %collective-permute-start.26 = (bf16[2,2,32,1792]{3,2,1,0:T(8,128)(2,1)S(1)}, bf16[2,2,32,1792]{3,2,1,0:T(8,128)(2,1)S(1)}, u32[]{:S(2)}, u32[]{:S(2)}) collective-permute-start(bf16[2,2,32,1792]{3,2,1,0:T(8,128)(2,1)S(1)} %pad_maximum_fusion.4), channel_id=1, source_target_pairs={{0,96},{32,64},{64,32},{96,0},{1,97},{33,65},{65,33},{97,1},{2,98}... | collective-permute-start | bytes 1376264 | tf_op jit(solution)/shard_map/ppermute | solution.py:19
  108.1 12.2 %collective-permute-start.27 = (bf16[64,896]{1,0:T(8,128)(2,1)S(1)}, bf16[64,896]{1,0:T(8,128)(2,1)S(1)}, u32[]{:S(2)}, u32[]{:S(2)}) collective-permute-start(bf16[64,896]{1,0:T(8,128)(2,1)S(1)} %get-tuple-element.51), channel_id=1, source_target_pairs={{0,1},{1,0},{2,3},{3,2},{4,5},{5,4},{6,7},{7,6},{8,9},{9,8},{10,11... | collective-permute-start | bytes 344072 | tf_op jit(solution)/shard_map/ppermute | solution.py:19
  108.2 12.1 %collective-permute-start.28 = (bf16[64,896]{1,0:T(8,128)(2,1)S(1)}, bf16[64,896]{1,0:T(8,128)(2,1)S(1)}, u32[]{:S(2)}, u32[]{:S(2)}) collective-permute-start(bf16[64,896]{1,0:T(8,128)(2,1)S(1)} %get-tuple-element.51), channel_id=1, source_target_pairs={{0,2},{1,3},{2,0},{3,1},{4,6},{5,7},{6,4},{7,5},{8,10},{9,11},{10,... | collective-permute-start | bytes 344072 | tf_op jit(solution)/shard_map/ppermute | solution.py:19
  111.5 8.8 %collective-permute-start.29 = (bf16[64,896]{1,0:T(8,128)(2,1)S(1)}, bf16[64,896]{1,0:T(8,128)(2,1)S(1)}, u32[]{:S(2)}, u32[]{:S(2)}) collective-permute-start(bf16[64,896]{1,0:T(8,128)(2,1)S(1)} %get-tuple-element.51), channel_id=1, source_target_pairs={{0,3},{1,2},{2,1},{3,0},{4,7},{5,6},{6,5},{7,4},{8,11},{9,10},{10,... | collective-permute-start | bytes 344072 | tf_op jit(solution)/shard_map/ppermute | solution.py:19
  115.3 12.3 %collective-permute-start.25 = (bf16[2,2,32,1792]{3,2,0,1:T(8,128)(2,1)S(1)}, bf16[2,2,32,1792]{3,2,0,1:T(8,128)(2,1)S(1)}, u32[]{:S(2)}, u32[]{:S(2)}) collective-permute-start(bf16[2,2,32,1792]{3,2,0,1:T(8,128)(2,1)S(1)} %copy.21), channel_id=1, source_target_pairs={{0,32},{32,0},{64,96},{96,64},{1,33},{33,1},{65,97},{97,65},{2,34}... | collective-permute-start | bytes 1376264 | tf_op jit(solution)/shard_map/ppermute | solution.py:19
  127.6 25.2 %collective-permute-start.35 = (bf16[4,64,896]{2,1,0:T(8,128)(2,1)S(1)}, bf16[4,64,896]{2,1,0:T(8,128)(2,1)S(1)}, u32[]{:S(2)}, u32[]{:S(2)}) collective-permute-start(bf16[4,64,896]{2,1,0:T(8,128)(2,1)S(1)} %bitcast_dynamic-update-slice_fusion.12), channel_id=1, source_target_pairs={{0,4},{4,0},{8,12},{12,8},{1,5},{5,1},{9,13},{13,9},{2,6},{6,2},{1... | collective-permute-start | bytes 1376264 | tf_op jit(solution)/shard_map/ppermute | solution.py:19
  129.9 33.7 %collective-permute-start.36 = (bf16[4,64,896]{2,1,0:T(8,128)(2,1)S(1)}, bf16[4,64,896]{2,1,0:T(8,128)(2,1)S(1)}, u32[]{:S(2)}, u32[]{:S(2)}) collective-permute-start(bf16[4,64,896]{2,1,0:T(8,128)(2,1)S(1)} %bitcast_dynamic-update-slice_fusion.12), channel_id=1, source_target_pairs={{0,12},{4,8},{8,4},{12,0},{1,13},{5,9},{9,5},{13,1},{2,14},{6,10},... | collective-permute-start | bytes 1376264 | tf_op jit(solution)/shard_map/ppermute | solution.py:19
  137.2 26.5 %collective-permute-start.37 = (bf16[4,64,896]{2,1,0:T(8,128)(2,1)S(1)}, bf16[4,64,896]{2,1,0:T(8,128)(2,1)S(1)}, u32[]{:S(2)}, u32[]{:S(2)}) collective-permute-start(bf16[4,64,896]{2,1,0:T(8,128)(2,1)S(1)} %bitcast_dynamic-update-slice_fusion.12), channel_id=1, source_target_pairs={{0,8},{4,12},{8,0},{12,4},{1,9},{5,13},{9,1},{13,5},{2,10},{6,14},... | collective-permute-start | bytes 1376264 | tf_op jit(solution)/shard_map/ppermute | solution.py:19
  147.4 22.8 %collective-permute-start.38 = (bf16[4,2,64,1792]{3,2,1,0:T(8,128)(2,1)S(1)}, bf16[4,2,64,1792]{3,2,1,0:T(8,128)(2,1)S(1)}, u32[]{:S(2)}, u32[]{:S(2)}) collective-permute-start(bf16[4,2,64,1792]{3,2,1,0:T(8,128)(2,1)S(1)} %get-tuple-element.60), channel_id=1, source_target_pairs={{0,16},{16,0},{1,17},{17,1},{2,18},{18,2},{3,19},{19,3},{4,20},{20... | collective-permute-start | bytes 5505032 | tf_op jit(solution)/shard_map/ppermute | solution.py:19
  149.8 13.9 %collective-permute-start.34 = (bf16[2,2,64,512]{3,2,1,0:T(8,128)(2,1)S(1)}, bf16[2,2,64,512]{3,2,1,0:T(8,128)(2,1)S(1)}, u32[]{:S(2)}, u32[]{:S(2)}) collective-permute-start(bf16[2,2,64,512]{3,2,1,0:T(8,128)(2,1)S(1)} %get-tuple-element.58), channel_id=1, source_target_pairs={{0,8},{4,12},{8,0},{12,4},{1,9},{5,13},{9,1},{13,5},{2,10},{6,14},... | collective-permute-start | bytes 786440 | tf_op jit(solution)/shard_map/ppermute | solution.py:19
  152.8 15.0 %collective-permute-start.33 = (bf16[2,2,64,512]{3,2,1,0:T(8,128)(2,1)S(1)}, bf16[2,2,64,512]{3,2,1,0:T(8,128)(2,1)S(1)}, u32[]{:S(2)}, u32[]{:S(2)}) collective-permute-start(bf16[2,2,64,512]{3,2,1,0:T(8,128)(2,1)S(1)} %get-tuple-element.57), channel_id=1, source_target_pairs={{0,12},{4,8},{8,4},{12,0},{1,13},{5,9},{9,5},{13,1},{2,14},{6,10},... | collective-permute-start | bytes 786440 | tf_op jit(solution)/shard_map/ppermute | solution.py:19
  176.8 8.8 %collective-permute-start.41 = (bf16[2,64,512]{2,1,0:T(8,128)(2,1)S(1)}, bf16[2,64,512]{2,1,0:T(8,128)(2,1)S(1)}, u32[]{:S(2)}, u32[]{:S(2)}) collective-permute-start(bf16[2,64,512]{2,1,0:T(8,128)(2,1)S(1)} %get-tuple-element.82), channel_id=1, source_target_pairs={{1,2},{3,0},{16,19},{18,17},{5,6},{7,4},{20,23},{22,21},{9,10},{11... | collective-permute-start | bytes 393224 | tf_op jit(solution)/shard_map/ppermute | solution.py:206
  178.1 8.9 %collective-permute-start.40 = (bf16[2,64,512]{2,1,0:T(8,128)(2,1)S(1)}, bf16[2,64,512]{2,1,0:T(8,128)(2,1)S(1)}, u32[]{:S(2)}, u32[]{:S(2)}) collective-permute-start(bf16[2,64,512]{2,1,0:T(8,128)(2,1)S(1)} %get-tuple-element.83), channel_id=1, source_target_pairs={{0,2},{2,0},{17,19},{19,17},{4,6},{6,4},{21,23},{23,21},{8,10},{10... | collective-permute-start | bytes 393224 | tf_op jit(solution)/shard_map/ppermute | solution.py:206
  (14 other events, 94.9 us)

commit v3 on v2

v3 whole, which is shorter than its diff:
```python
import jax
import jax.numpy as jnp
from jax import lax
from jax.sharding import Mesh
from jax.sharding import PartitionSpec as P

TOKENS = 1024
ROWS = 32
BF = jnp.bfloat16
F32 = jnp.float32
SIZES = (2, 4, 2, 4, 4)
AXES = ("zh", "y", "core", "x", "zl")
ROW = ("zh", "y", "core")
COL = ("x", "zl")


def swap(block, axis, k):
    n = SIZES[AXES.index(axis)]
    return lax.ppermute(block, axis, [(i, i ^ k) for i in range(n)])


def after(block, *deps):
    return lax.optimization_barrier((block, deps))[0]


def put(buf, block, index, axis):
    start = [0] * buf.ndim
    start[axis] = index
    return lax.dynamic_update_slice(buf, jnp.expand_dims(block, axis), start)


def pick(array, index, axis):
    return lax.dynamic_index_in_dim(array, index, axis, keepdims=False)


def swiglu_grads(hidden_grad, gate_preact, up_preact):
    gate_float = gate_preact.astype(F32)
    up_float = up_preact.astype(F32)
    logistic = jax.nn.sigmoid(gate_float)
    derivative = logistic * (1.0 + gate_float * (1.0 - logistic))
    grad_gate = (hidden_grad * up_float * derivative).astype(BF)
    grad_up = (hidden_grad * gate_float * logistic).astype(BF)
    return (grad_gate, grad_up)


def contract_last(left, right):
    return lax.dot_general(left, right, (((1,), (1,)), ((), ())), preferred_element_type=F32)


def device(zh, y, core, x, zl):
    return (((zh * 4 + y) * 2 + core) * 4 + x) * 4 + zl


def scatter_pairs(half):
    return [
        (
            device(zh, y, core, zh, zl),
            device(zh, zl, half, (core ^ half) * 2 + (y >> 1), 1 + (y & 1)),
        )
        for zh in range(2)
        for y in range(4)
        for core in range(2)
        for zl in range(4)
    ]


def shards(output_grad, gate_preact, up_preact, gate_weight, up_weight, down_weight):
    zh, y, core, x, zl = (lax.axis_index(a) for a in AXES)
    units = gate_preact.shape[1]
    half_units = units // 2
    width = output_grad.shape[1]

    def at_zl(buf, block, which):
        start = ((which & 1) ^ core, which >> 1, 0, 0)
        return lax.dynamic_update_slice(buf, block[None, None], start)

    down_far = swap(down_weight, "core", 1)
    run = at_zl(jnp.zeros((2, 2, 64, width), BF), output_grad, zl)
    for k in (1, 2, 3):
        run = at_zl(run, swap(output_grad, "zl", k), zl ^ k)
    pre_a = jnp.stack([gate_preact[:ROWS], up_preact[:ROWS]])
    pre_b = jnp.stack([gate_preact[ROWS:], up_preact[ROWS:]])
    weights = jnp.concatenate([gate_weight, up_weight], 1)
    run, pre_a = after((run, pre_a), down_far)
    pre_far_a = swap(pre_a, "zh", 1)
    cot = put(jnp.zeros((2, 4, 2, 64, width), BF), run, x, 1)
    for k in (1, 3, 2):
        cot = put(cot, swap(run, "x", k), x ^ k, 1)
    far = swap(cot[1], "core", 1)
    near, far, pre_b = after((cot[0], far, pre_b), pre_far_a)
    pre_far_b = swap(pre_b, "zh", 1)

    def part_of(c):
        rows = slice(c * ROWS, (c + 1) * ROWS)
        part = contract_last(near[:, :, rows].reshape(8 * ROWS, width), down_weight)
        part = part + contract_last(far[:, :, rows].reshape(8 * ROWS, width), down_far)
        return part.reshape(2, 4, ROWS, units)

    def over_y(part, *deps):
        sends = tuple(pick(part, y ^ k, 1).astype(BF) for k in (1, 3, 2))
        sends = after(sends, *deps)
        return [swap(s, "y", k) for s, k in zip(sends, (1, 3, 2))]

    def add_up(part, got):
        hidden = pick(part, y, 1)
        for block in got:
            hidden = hidden + block.astype(F32)
        return hidden

    def grads(hidden, far_hidden, pre, pre_far):
        hidden = hidden + far_hidden.astype(F32)
        low = jnp.where(zh == 0, pre, pre_far)
        high = jnp.where(zh == 0, pre_far, pre)
        gate_tok = jnp.stack([low[0], high[0]])
        up_tok = jnp.stack([low[1], high[1]])
        return jnp.concatenate(swiglu_grads(hidden, gate_tok, up_tok), 2)

    part_a = part_of(0)
    part_b = part_of(1)
    got_a = over_y(part_a)
    hidden_a = add_up(part_a, got_a)
    got_b = over_y(part_b, *got_a, pre_far_b)
    hfar_a = swap(hidden_a.astype(BF), "zh", 1)
    both_a = grads(hidden_a, hfar_a, pre_a, pre_far_a)
    hidden_b = add_up(part_b, got_b)
    hfar_b = swap(hidden_b.astype(BF), "zh", 1)
    both_b = grads(hidden_b, hfar_b, pre_b, pre_far_b)
    both = jnp.concatenate([both_a, both_b], 1)

    pieces = [
        lax.ppermute(
            both[:, :, half * half_units : (half + 1) * half_units], AXES, scatter_pairs(half)
        )
        for half in range(2)
    ]
    one = swap(both, "y", 1)
    three = swap(both, "y", 3)
    one, three, *pieces = lax.optimization_barrier((one, three, *pieces))
    two0 = swap(one[0], "y", 3)
    two1 = swap(three[1], "y", 1)
    piece = jnp.where(core == 0, pieces[0], pieces[1])
    edge = lax.ppermute(piece, "zl", [(1, 0), (2, 3)])
    mid = lax.ppermute(piece, "zl", [(1, 2), (2, 1)])
    cross = lax.ppermute(piece, "zl", [(1, 3), (2, 0)])
    srun = jnp.stack(
        [lax.select_n(zl, edge, piece, mid, cross), lax.select_n(zl, cross, mid, piece, edge)]
    )
    two0, two1, srun = lax.optimization_barrier((two0, two1, srun))
    got = [swap(srun, "x", k) for k in (1, 3, 2)]
    ring = jnp.stack([one, three])
    two = jnp.stack([two0, two1])
    both_other = swap(both, "core", 1)
    ring_other = swap(ring, "core", 1)
    two_other = swap(two, "core", 1)

    def assemble(both, ring, two):
        full = jnp.zeros((4, 2, 64, 2 * units), BF)
        for block, k in ((both, 0), (ring[0], 1), (ring[1], 3), (two, 2)):
            full = put(full, block, y ^ k, 0)
        return full

    full = assemble(both, ring, two)
    full_other = assemble(both_other, ring_other, two_other)

    partial = jnp.stack(
        [contract_last(f.reshape(512, 2 * units), weights) for f in (full, full_other)]
    )
    partial = partial.reshape(2, 2, 2, 2, 64, width).transpose(3, 1, 2, 0, 4, 5)
    partial = partial.reshape(4, 4, 64, width)

    slab = put(jnp.zeros((4, 2, 2, 64, half_units), BF), srun, x, 0)
    for block, k in zip(got, (1, 3, 2)):
        slab = put(slab, block, x ^ k, 0)
    gate_all = jnp.stack([full[..., :units], full_other[..., :units]])
    gate_factor = (
        lax.dot_general(
            slab.reshape(TOKENS, half_units),
            gate_all.reshape(TOKENS, units),
            (((0,), (0,)), ((), ())),
            preferred_element_type=F32,
        )
        / TOKENS
    )

    mine = pick(partial, x, 0)
    got = [swap(pick(partial, x ^ k, 0).astype(BF), "x", k) for k in (1, 3, 2)]
    for block in got:
        mine = mine + block.astype(F32)
    mine = after(mine, gate_factor)

    def for_zl(column):
        return pick(mine, (column >> 1) * 2 + ((column & 1) ^ core), 0)

    result = for_zl(zl)
    for k in (1, 2, 3):
        result = result + swap(for_zl(zl ^ k).astype(BF), "zl", k).astype(F32)
    return (result.astype(BF), gate_factor)


def solution(mesh):
    fine = Mesh(mesh.devices.reshape(SIZES), AXES)
    return jax.shard_map(
        shards,
        mesh=fine,
        in_specs=(P(COL, ROW), P(ROW, COL), P(ROW, COL), P(ROW, COL), P(ROW, COL), P(COL, ROW)),
        out_specs=(P(COL, ROW), P(ROW, COL)),
        check_vma=False,
    )
```

time: 193 us -> 181 us (0.938); the launches traced: 190 us -> 181 us
  starting transfers between devices: 84.1 us -> 75.9 us
  waiting for transfers between devices: 80.7 us -> 83.1 us
    ppermute x5, waiting for transfers between devices: 10.6 us -> 28.3 us  [the longest x1 16.9 us: shards(): cross = lax.ppermute(piece, 'zl', [(1, 3), (2, 0)])]
    ppermute x38 -> x34, waiting for transfers between devices: 70.1 us -> 54.8 us  [swap(): return lax.ppermute(block, axis, [(i, i ^ k) for i in range(n)])]
    ppermute x5, starting transfers between devices: 20.2 us -> 12.9 us  [the longest x2 9.62 us: shards(): lax.ppermute(both[:, :, half * half_units:(half + 1) * half_units], AXES,...]
    dot_general x12 -> x6, matrix products: 8.13 us -> 6.97 us  [contract_last(): lax.dot_general(left, right, (((1,), (1,)), ((), ())), preferred_element_...]
    ppermute x38 -> x34, starting transfers between devices: 63.9 us -> 63 us  [swap(): return lax.ppermute(block, axis, [(i, i ^ k) for i in range(n)])]
  transfers between devices with their start and end apart: 43 -> 39, of which waited for: 24 -> 18; matrix products, arithmetic and copies ran while one was open for 8% -> 8% of each run, Pallas kernels for 0% -> 0%
where the time goes in v3:
time: 181 us
  waiting for transfers between devices  83.1 us (46%)
  starting transfers between devices  75.9 us (42%)
  matrix products  13.3 us (7%)
  local copies, waits for them, and re-layouts  4.7 us (3%)
  other arithmetic  2.86 us (2%)
    ppermute x34, starting transfers between devices, swap(): return lax.ppermute(block, axis, [(i, i ^ k) for i in range(n)])  63 us
    ppermute x34, waiting for transfers between devices, swap(): return lax.ppermute(block, axis, [(i, i ^ k) for i in range(n)])  54.8 us
    ppermute x1, waiting for transfers between devices, shards(): cross = lax.ppermute(piece, 'zl', [(1, 3), (2, 0)])  16.9 us
    ppermute x2, starting transfers between devices, shards(): lax.ppermute(both[:, :, half * half_units:(half + 1) * half_units], AXES,...  9.62 us
    ppermute x2, waiting for transfers between devices, shards(): lax.ppermute(both[:, :, half * half_units:(half + 1) * half_units], AXES,...  8.63 us
    dot_general x6, matrix products, contract_last(): lax.dot_general(left, right, (((1,), (1,)), ((), ())), preferred_element_...  6.97 us
    dot_general x1, matrix products, shards(): lax.dot_general(slab.reshape(TOKENS, half_units), gate_all.reshape(TOKENS...  6.29 us
  transfers between devices with their start and end apart: 39, of which 18 were waited for; matrix products, arithmetic and copies ran while one was open for 8% of the time, Pallas kernels for 0%

profile of v3, /device:TPU:8, one launch (start us, length us, event | category | flops | bytes accessed | tf_op | source)
XLA Modules:
  0.0 181.3 jit_solution(17669845638580243405)
XLA Ops:
  0.6 2.0 %collective-permute-start = (bf16[64,512]{1,0:T(8,128)(2,1)}, bf16[64,512]{1,0:T(8,128)(2,1)S(1)}, u32[]{:S(2)}, u32[]{:S(2)}) collective-permute-start(bf16[64,512]{1,0:T(8,128)(2,1)} %param.6), channel_id=1, source_target_pairs={{0,1},{1,0},{2,3},{3,2},{4,5},{5,4},{6,7},{7,6},{8,9},{9,8},{10,11... | collective-permute-start | bytes 196616 | tf_op jit(solution)/shard_map/ppermute | solution.py:19
  2.6 3.3 %collective-permute-start.1 = (bf16[64,512]{1,0:T(8,128)(2,1)}, bf16[64,512]{1,0:T(8,128)(2,1)S(1)}, u32[]{:S(2)}, u32[]{:S(2)}) collective-permute-start(bf16[64,512]{1,0:T(8,128)(2,1)} %param.6), channel_id=1, source_target_pairs={{0,2},{1,3},{2,0},{3,1},{4,6},{5,7},{6,4},{7,5},{8,10},{9,11},{10,... | collective-permute-start | bytes 196616 | tf_op jit(solution)/shard_map/ppermute | solution.py:19
  7.3 3.5 %collective-permute-done.1 = bf16[64,512]{1,0:T(8,128)(2,1)S(1)} collective-permute-done((bf16[64,512]{1,0:T(8,128)(2,1)}, bf16[64,512]{1,0:T(8,128)(2,1)S(1)}, u32[]{:S(2)}, u32[]{:S(2)}) %collective-permute-start.1) | collective-permute-done | bytes 65568 | tf_op jit(solution)/shard_map/ppermute | solution.py:19
  13.8 2.1 %collective-permute-start.5 = (bf16[2,2,64,512]{3,2,1,0:T(8,128)(2,1)S(1)}, bf16[2,2,64,512]{3,2,1,0:T(8,128)(2,1)S(1)}, u32[]{:S(2)}, u32[]{:S(2)}) collective-permute-start(bf16[2,2,64,512]{3,2,1,0:T(8,128)(2,1)S(1)} %bitcast_dynamic-update-slice_fusion.12), channel_id=1, source_target_pairs={{0,12},{4,8},{8,4},{12,0},{1,13},{5,9},{9,5},{13,1},{2,14},{6,10},... | collective-permute-start | bytes 786440 | tf_op jit(solution)/shard_map/ppermute | solution.py:19
  16.5 5.0 %collective-permute-start.8 = (bf16[2,32,1792]{2,1,0:T(8,128)(2,1)S(1)}, bf16[2,32,1792]{2,1,0:T(8,128)(2,1)S(1)}, u32[]{:S(2)}, u32[]{:S(2)}) collective-permute-start(bf16[2,32,1792]{2,1,0:T(8,128)(2,1)S(1)} %pad_maximum_fusion.4), channel_id=1, source_target_pairs={{0,128},{128,0},{1,129},{129,1},{2,130},{130,2},{3,131},{131,3},{4... | collective-permute-start | bytes 688136 | tf_op jit(solution)/shard_map/ppermute | solution.py:19
  21.6 6.1 %collective-permute-done.8 = bf16[2,32,1792]{2,1,0:T(8,128)(2,1)S(1)} collective-permute-done((bf16[2,32,1792]{2,1,0:T(8,128)(2,1)S(1)}, bf16[2,32,1792]{2,1,0:T(8,128)(2,1)S(1)}, u32[]{:S(2)}, u32[]{:S(2)}) %collective-permute-start.8) | collective-permute-done | bytes 229408 | tf_op jit(solution)/shard_map/ppermute | solution.py:19
  32.8 2.4 %collective-permute-start.10 = (bf16[2,32,1792]{2,1,0:T(8,128)(2,1)S(1)}, bf16[2,32,1792]{2,1,0:T(8,128)(2,1)S(1)}, u32[]{:S(2)}, u32[]{:S(2)}) collective-permute-start(bf16[2,32,1792]{2,1,0:T(8,128)(2,1)S(1)} %get-tuple-element.26), channel_id=1, source_target_pairs={{0,96},{32,64},{64,32},{96,0},{1,97},{33,65},{65,33},{97,1},{2,98}... | collective-permute-start | bytes 688136 | tf_op jit(solution)/shard_map/ppermute | solution.py:19
  36.4 8.1 %collective-permute-start.13 = (bf16[2,32,1792]{2,1,0:T(8,128)(2,1)S(1)}, bf16[2,32,1792]{2,1,0:T(8,128)(2,1)S(1)}, u32[]{:S(2)}, u32[]{:S(2)}) collective-permute-start(bf16[2,32,1792]{2,1,0:T(8,128)(2,1)S(1)} %pad_maximum_fusion.5), channel_id=1, source_target_pairs={{0,128},{128,0},{1,129},{129,1},{2,130},{130,2},{3,131},{131,3},{4... | collective-permute-start | bytes 688136 | tf_op jit(solution)/shard_map/ppermute | solution.py:19
  45.9 7.8 %collective-permute-done.13 = bf16[2,32,1792]{2,1,0:T(8,128)(2,1)S(1)} collective-permute-done((bf16[2,32,1792]{2,1,0:T(8,128)(2,1)S(1)}, bf16[2,32,1792]{2,1,0:T(8,128)(2,1)S(1)}, u32[]{:S(2)}, u32[]{:S(2)}) %collective-permute-start.13) | collective-permute-done | bytes 229408 | tf_op jit(solution)/shard_map/ppermute | solution.py:19
  53.8 2.3 %collective-permute-start.16 = (bf16[2,32,1792]{2,1,0:T(8,128)(2,1)S(1)}, bf16[2,32,1792]{2,1,0:T(8,128)(2,1)S(1)}, u32[]{:S(2)}, u32[]{:S(2)}) collective-permute-start(bf16[2,32,1792]{2,1,0:T(8,128)(2,1)S(1)} %get-tuple-element.31), channel_id=1, source_target_pairs={{0,64},{32,96},{64,0},{96,32},{1,65},{33,97},{65,1},{97,33},{2,66}... | collective-permute-start | bytes 688136 | tf_op jit(solution)/shard_map/ppermute | solution.py:19
  56.4 2.1 %collective-permute-start.14 = (bf16[2,32,1792]{2,1,0:T(8,128)(2,1)S(1)}, bf16[2,32,1792]{2,1,0:T(8,128)(2,1)S(1)}, u32[]{:S(2)}, u32[]{:S(2)}) collective-permute-start(bf16[2,32,1792]{2,1,0:T(8,128)(2,1)S(1)} %get-tuple-element.29), channel_id=1, source_target_pairs={{0,32},{32,0},{64,96},{96,64},{1,33},{33,1},{65,97},{97,65},{2,34}... | collective-permute-start | bytes 688136 | tf_op jit(solution)/shard_map/ppermute | solution.py:19
  58.7 6.6 %collective-permute-start.12 = (bf16[2,32,1792]{2,1,0:T(8,128)(2,1)S(1)}, bf16[2,32,1792]{2,1,0:T(8,128)(2,1)S(1)}, u32[]{:S(2)}, u32[]{:S(2)}) collective-permute-start(bf16[2,32,1792]{2,1,0:T(8,128)(2,1)S(1)} %get-tuple-element.40), channel_id=1, source_target_pairs={{0,128},{128,0},{1,129},{129,1},{2,130},{130,2},{3,131},{131,3},{4... | collective-permute-start | bytes 688136 | tf_op jit(solution)/shard_map/ppermute | solution.py:19
  65.4 5.0 %collective-permute-start.17 = (bf16[2,32,1792]{2,1,0:T(8,128)(2,1)S(1)}, bf16[2,32,1792]{2,1,0:T(8,128)(2,1)S(1)}, u32[]{:S(2)}, u32[]{:S(2)}) collective-permute-start(bf16[2,32,1792]{2,1,0:T(8,128)(2,1)S(1)} %get-tuple-element.42), channel_id=1, source_target_pairs={{0,128},{128,0},{1,129},{129,1},{2,130},{130,2},{3,131},{131,3},{4... | collective-permute-start | bytes 688136 | tf_op jit(solution)/shard_map/ppermute | solution.py:19
  70.7 8.5 %collective-permute-done.17 = bf16[2,32,1792]{2,1,0:T(8,128)(2,1)S(1)} collective-permute-done((bf16[2,32,1792]{2,1,0:T(8,128)(2,1)S(1)}, bf16[2,32,1792]{2,1,0:T(8,128)(2,1)S(1)}, u32[]{:S(2)}, u32[]{:S(2)}) %collective-permute-start.17) | collective-permute-done | bytes 229408 | tf_op jit(solution)/shard_map/ppermute | solution.py:19
  80.2 2.6 %collective-permute-start.18 = (bf16[2,64,3584]{2,1,0:T(8,128)(2,1)S(1)}, bf16[2,64,3584]{2,1,0:T(8,128)(2,1)S(1)}, u32[]{:S(2)}, u32[]{:S(2)}) collective-permute-start(bf16[2,64,3584]{2,1,0:T(8,128)(2,1)S(1)} %maximum_maximum_fusion), channel_id=1, source_target_pairs={{0,32},{32,0},{64,96},{96,64},{1,33},{33,1},{65,97},{97,65},{2,34}... | collective-permute-start | bytes 2752520 | tf_op jit(solution)/shard_map/ppermute | solution.py:19
  84.3 6.7 %collective-permute-start.20 = (bf16[2,64,896]{2,1,0:T(8,128)(2,1)S(1)}, bf16[2,64,896]{2,1,0:T(8,128)(2,1)S(1)}, u32[]{:S(2)}, u32[]{:S(2)}) collective-permute-start(bf16[2,64,896]{2,1,0:T(8,128)(2,1)S(1)} %get-tuple-element.58), channel_id=1, source_target_pairs={{0,1},{1,33},{2,65},{3,97},{16,9},{17,41},{18,73},{19,105},{32,2},... | collective-permute-start | bytes 688136 | tf_op jit(solution)/shard_map/ppermute | solution.py:131
  91.0 3.0 %collective-permute-start.21 = (bf16[2,64,896]{2,1,0:T(8,128)(2,1)S(1)}, bf16[2,64,896]{2,1,0:T(8,128)(2,1)S(1)}, u32[]{:S(2)}, u32[]{:S(2)}) collective-permute-start(bf16[2,64,896]{2,1,0:T(8,128)(2,1)S(1)} %get-tuple-element.57), channel_id=1, source_target_pairs={{0,25},{1,57},{2,89},{3,121},{16,17},{17,49},{18,81},{19,113},{32,... | collective-permute-start | bytes 688136 | tf_op jit(solution)/shard_map/ppermute | solution.py:131
  95.9 7.0 %collective-permute-done.21 = bf16[2,64,896]{2,1,0:T(8,128)(2,1)S(1)} collective-permute-done((bf16[2,64,896]{2,1,0:T(8,128)(2,1)S(1)}, bf16[2,64,896]{2,1,0:T(8,128)(2,1)S(1)}, u32[]{:S(2)}, u32[]{:S(2)}) %collective-permute-start.21) | collective-permute-done | bytes 229408 | tf_op jit(solution)/shard_map/ppermute | solution.py:131
  106.7 2.8 %collective-permute-start.23 = (bf16[64,3584]{1,0:T(8,128)(2,1)S(1)}, bf16[64,3584]{1,0:T(8,128)(2,1)S(1)}, u32[]{:S(2)}, u32[]{:S(2)}) collective-permute-start(bf16[64,3584]{1,0:T(8,128)(2,1)S(1)} %slice_bitcast_fusion.4), channel_id=1, source_target_pairs={{0,32},{32,0},{64,96},{96,64},{1,33},{33,1},{65,97},{97,65},{2,34}... | collective-permute-start | bytes 1376264 | tf_op jit(solution)/shard_map/ppermute | solution.py:19
  110.4 16.9 %collective-permute-done.26 = bf16[2,64,896]{2,1,0:T(8,128)(2,1)S(1)} collective-permute-done((bf16[2,64,896]{2,1,0:T(8,128)(2,1)S(1)}, bf16[2,64,896]{2,1,0:T(8,128)(2,1)S(1)}, u32[]{:S(2)}, u32[]{:S(2)}) %collective-permute-start.26) | collective-permute-done | bytes 229408 | tf_op jit(solution)/shard_map/ppermute | solution.py:144
  127.2 2.8 %collective-permute-done.24 = bf16[2,64,896]{2,1,0:T(8,128)(2,1)S(1)} collective-permute-done((bf16[2,64,896]{2,1,0:T(8,128)(2,1)S(1)}, bf16[2,64,896]{2,1,0:T(8,128)(2,1)S(1)}, u32[]{:S(2)}, u32[]{:S(2)}) %collective-permute-start.24) | collective-permute-done | bytes 229408 | tf_op jit(solution)/shard_map/ppermute | solution.py:142
  130.3 2.4 %collective-permute-start.34 = (bf16[2,2,64,896]{3,2,1,0:T(8,128)(2,1)S(1)}, bf16[2,2,64,896]{3,2,1,0:T(8,128)(2,1)S(1)}, u32[]{:S(2)}, u32[]{:S(2)}) collective-permute-start(bf16[2,2,64,896]{3,2,1,0:T(8,128)(2,1)S(1)} %pad_maximum_fusion.3), channel_id=1, source_target_pairs={{0,12},{4,8},{8,4},{12,0},{1,13},{5,9},{9,5},{13,1},{2,14},{6,10},... | collective-permute-start | bytes 1376264 | tf_op jit(solution)/shard_map/ppermute | solution.py:19
  134.5 2.1 %fusion.2 = f32[1,2,2,2,64,512]{5,4,3,2,1,0:T(8,128)S(1)} fusion(bf16[2,2,2,64,3584]{4,3,2,1,0:T(8,128)(2,1)S(1)} %bitcast.177, bf16[512,1792]{1,0:T(8,128)(2,1)S(1)} %copy-done.4, bf16[512,1792]{1,0:T(8,128)(2,1)S(1)} %copy-done.5), kind=kOutput, calls=%fused_computation.11 | convolution fusion | flops 1886388224 | bytes 8388608 | tf_op jit(solution)/shard_map/dot_general | solution.py:47
  137.4 6.3 %collective-permute-done.33 = bf16[2,2,64,896]{3,2,1,0:T(8,128)(2,1)S(1)} collective-permute-done((bf16[2,2,64,896]{3,2,1,0:T(8,128)(2,1)S(1)}, bf16[2,2,64,896]{3,2,1,0:T(8,128)(2,1)S(1)}, u32[]{:S(2)}, u32[]{:S(2)}) %collective-permute-start.33) | collective-permute-done | bytes 458784 | tf_op jit(solution)/shard_map/ppermute | solution.py:19
  143.8 7.6 %collective-permute-done.34 = bf16[2,2,64,896]{3,2,1,0:T(8,128)(2,1)S(1)} collective-permute-done((bf16[2,2,64,896]{3,2,1,0:T(8,128)(2,1)S(1)}, bf16[2,2,64,896]{3,2,1,0:T(8,128)(2,1)S(1)}, u32[]{:S(2)}, u32[]{:S(2)}) %collective-permute-start.34) | collective-permute-done | bytes 458784 | tf_op jit(solution)/shard_map/ppermute | solution.py:19
  153.3 2.1 %fusion.3 = f32[1,2,2,2,64,512]{5,4,3,2,1,0:T(8,128)S(1)} fusion(bf16[2,2,2,64,3584]{4,3,2,1,0:T(8,128)(2,1)S(1)} %bitcast.178, bf16[512,1792]{1,0:T(8,128)(2,1)S(1)} %copy-done.4, bf16[512,1792]{1,0:T(8,128)(2,1)S(1)} %copy-done.5), kind=kOutput, calls=%fused_computation.12 | convolution fusion | flops 1886388224 | bytes 8388608 | tf_op jit(solution)/shard_map/dot_general | solution.py:47
  156.0 1.9 %collective-permute-start.32 = (bf16[4,64,512]{2,1,0:T(8,128)(2,1)S(1)}, bf16[4,64,512]{2,1,0:T(8,128)(2,1)S(1)}, u32[]{:S(2)}, u32[]{:S(2)}) collective-permute-start(bf16[4,64,512]{2,1,0:T(8,128)(2,1)S(1)} %get-tuple-element.45), channel_id=1, source_target_pairs={{0,8},{4,12},{8,0},{12,4},{1,9},{5,13},{9,1},{13,5},{2,10},{6,14},... | collective-permute-start | bytes 786440 | tf_op jit(solution)/shard_map/ppermute | solution.py:19
  159.9 6.3 %convolution_multiply_fusion = f32[896,1792]{1,0:T(8,128)} fusion(bf16[1024,896]{1,0:T(8,128)(2,1)S(1)} %bitcast.188, bf16[1024,1792]{1,0:T(8,128)(2,1)S(1)} %bitcast.187), kind=kOutput, calls=%fused_computation | convolution fusion | flops 3289939968 | bytes 11927552 | tf_op jit(solution)/shard_map/dot_general | solution.py:176
  166.8 4.2 %collective-permute-done.31 = bf16[4,64,512]{2,1,0:T(8,128)(2,1)S(1)} collective-permute-done((bf16[4,64,512]{2,1,0:T(8,128)(2,1)S(1)}, bf16[4,64,512]{2,1,0:T(8,128)(2,1)S(1)}, u32[]{:S(2)}, u32[]{:S(2)}) %collective-permute-start.31) | collective-permute-done | bytes 262176 | tf_op jit(solution)/shard_map/ppermute | solution.py:19
  171.2 2.5 %collective-permute-start.38 = (bf16[64,512]{1,0:T(8,128)(2,1)S(1)}, bf16[64,512]{1,0:T(8,128)(2,1)S(1)}, u32[]{:S(2)}, u32[]{:S(2)}) collective-permute-start(bf16[64,512]{1,0:T(8,128)(2,1)S(1)} %get-tuple-element.64), channel_id=1, source_target_pairs={{0,3},{1,2},{2,1},{3,0},{4,7},{5,6},{6,5},{7,4},{8,11},{9,10},{10,... | collective-permute-start | bytes 196616 | tf_op jit(solution)/shard_map/ppermute | solution.py:19
  175.7 2.2 %collective-permute-done.38 = bf16[64,512]{1,0:T(8,128)(2,1)S(1)} collective-permute-done((bf16[64,512]{1,0:T(8,128)(2,1)S(1)}, bf16[64,512]{1,0:T(8,128)(2,1)S(1)}, u32[]{:S(2)}, u32[]{:S(2)}) %collective-permute-start.38) | collective-permute-done | bytes 65568 | tf_op jit(solution)/shard_map/ppermute | solution.py:19
  177.9 2.7 %collective-permute-done.37 = bf16[64,512]{1,0:T(8,128)(2,1)S(1)} collective-permute-done((bf16[64,512]{1,0:T(8,128)(2,1)S(1)}, bf16[64,512]{1,0:T(8,128)(2,1)S(1)}, u32[]{:S(2)}, u32[]{:S(2)}) %collective-permute-start.37) | collective-permute-done | bytes 65568 | tf_op jit(solution)/shard_map/ppermute | solution.py:19
  (126 shorter events, 33.0 us)
Async XLA Ops:
  2.6 8.1 %collective-permute-start.1 = (bf16[64,512]{1,0:T(8,128)(2,1)}, bf16[64,512]{1,0:T(8,128)(2,1)S(1)}, u32[]{:S(2)}, u32[]{:S(2)}) collective-permute-start(bf16[64,512]{1,0:T(8,128)(2,1)} %param.6), channel_id=1, source_target_pairs={{0,2},{1,3},{2,0},{3,1},{4,6},{5,7},{6,4},{7,5},{8,10},{9,11},{10,... | collective-permute-start | bytes 196616 | tf_op jit(solution)/shard_map/ppermute | solution.py:19
  12.2 15.6 %collective-permute-start.4 = (bf16[2,2,64,512]{3,2,1,0:T(8,128)(2,1)S(1)}, bf16[2,2,64,512]{3,2,1,0:T(8,128)(2,1)S(1)}, u32[]{:S(2)}, u32[]{:S(2)}) collective-permute-start(bf16[2,2,64,512]{3,2,1,0:T(8,128)(2,1)S(1)} %bitcast_dynamic-update-slice_fusion.12), channel_id=1, source_target_pairs={{0,4},{4,0},{8,12},{12,8},{1,5},{5,1},{9,13},{13,9},{2,6},{6,2},{1... | collective-permute-start | bytes 786440 | tf_op jit(solution)/shard_map/ppermute | solution.py:19
  13.8 14.0 %collective-permute-start.5 = (bf16[2,2,64,512]{3,2,1,0:T(8,128)(2,1)S(1)}, bf16[2,2,64,512]{3,2,1,0:T(8,128)(2,1)S(1)}, u32[]{:S(2)}, u32[]{:S(2)}) collective-permute-start(bf16[2,2,64,512]{3,2,1,0:T(8,128)(2,1)S(1)} %bitcast_dynamic-update-slice_fusion.12), channel_id=1, source_target_pairs={{0,12},{4,8},{8,4},{12,0},{1,13},{5,9},{9,5},{13,1},{2,14},{6,10},... | collective-permute-start | bytes 786440 | tf_op jit(solution)/shard_map/ppermute | solution.py:19
  15.9 12.0 %collective-permute-start.6 = (bf16[2,2,64,512]{3,2,1,0:T(8,128)(2,1)S(1)}, bf16[2,2,64,512]{3,2,1,0:T(8,128)(2,1)S(1)}, u32[]{:S(2)}, u32[]{:S(2)}) collective-permute-start(bf16[2,2,64,512]{3,2,1,0:T(8,128)(2,1)S(1)} %bitcast_dynamic-update-slice_fusion.12), channel_id=1, source_target_pairs={{0,8},{4,12},{8,0},{12,4},{1,9},{5,13},{9,1},{13,5},{2,10},{6,14},... | collective-permute-start | bytes 786440 | tf_op jit(solution)/shard_map/ppermute | solution.py:19
  16.5 11.2 %collective-permute-start.8 = (bf16[2,32,1792]{2,1,0:T(8,128)(2,1)S(1)}, bf16[2,32,1792]{2,1,0:T(8,128)(2,1)S(1)}, u32[]{:S(2)}, u32[]{:S(2)}) collective-permute-start(bf16[2,32,1792]{2,1,0:T(8,128)(2,1)S(1)} %pad_maximum_fusion.4), channel_id=1, source_target_pairs={{0,128},{128,0},{1,129},{129,1},{2,130},{130,2},{3,131},{131,3},{4... | collective-permute-start | bytes 688136 | tf_op jit(solution)/shard_map/ppermute | solution.py:19
  32.3 13.1 %collective-permute-start.9 = (bf16[2,32,1792]{2,1,0:T(8,128)(2,1)S(1)}, bf16[2,32,1792]{2,1,0:T(8,128)(2,1)S(1)}, u32[]{:S(2)}, u32[]{:S(2)}) collective-permute-start(bf16[2,32,1792]{2,1,0:T(8,128)(2,1)S(1)} %get-tuple-element.25), channel_id=1, source_target_pairs={{0,32},{32,0},{64,96},{96,64},{1,33},{33,1},{65,97},{97,65},{2,34}... | collective-permute-start | bytes 688136 | tf_op jit(solution)/shard_map/ppermute | solution.py:19
  32.8 12.6 %collective-permute-start.10 = (bf16[2,32,1792]{2,1,0:T(8,128)(2,1)S(1)}, bf16[2,32,1792]{2,1,0:T(8,128)(2,1)S(1)}, u32[]{:S(2)}, u32[]{:S(2)}) collective-permute-start(bf16[2,32,1792]{2,1,0:T(8,128)(2,1)S(1)} %get-tuple-element.26), channel_id=1, source_target_pairs={{0,96},{32,64},{64,32},{96,0},{1,97},{33,65},{65,33},{97,1},{2,98}... | collective-permute-start | bytes 688136 | tf_op jit(solution)/shard_map/ppermute | solution.py:19
  35.2 10.7 %collective-permute-start.11 = (bf16[2,32,1792]{2,1,0:T(8,128)(2,1)S(1)}, bf16[2,32,1792]{2,1,0:T(8,128)(2,1)S(1)}, u32[]{:S(2)}, u32[]{:S(2)}) collective-permute-start(bf16[2,32,1792]{2,1,0:T(8,128)(2,1)S(1)} %get-tuple-element.27), channel_id=1, source_target_pairs={{0,64},{32,96},{64,0},{96,32},{1,65},{33,97},{65,1},{97,33},{2,66}... | collective-permute-start | bytes 688136 | tf_op jit(solution)/shard_map/ppermute | solution.py:19
  36.4 17.3 %collective-permute-start.13 = (bf16[2,32,1792]{2,1,0:T(8,128)(2,1)S(1)}, bf16[2,32,1792]{2,1,0:T(8,128)(2,1)S(1)}, u32[]{:S(2)}, u32[]{:S(2)}) collective-permute-start(bf16[2,32,1792]{2,1,0:T(8,128)(2,1)S(1)} %pad_maximum_fusion.5), channel_id=1, source_target_pairs={{0,128},{128,0},{1,129},{129,1},{2,130},{130,2},{3,131},{131,3},{4... | collective-permute-start | bytes 688136 | tf_op jit(solution)/shard_map/ppermute | solution.py:19
  53.8 11.5 %collective-permute-start.16 = (bf16[2,32,1792]{2,1,0:T(8,128)(2,1)S(1)}, bf16[2,32,1792]{2,1,0:T(8,128)(2,1)S(1)}, u32[]{:S(2)}, u32[]{:S(2)}) collective-permute-start(bf16[2,32,1792]{2,1,0:T(8,128)(2,1)S(1)} %get-tuple-element.31), channel_id=1, source_target_pairs={{0,64},{32,96},{64,0},{96,32},{1,65},{33,97},{65,1},{97,33},{2,66}... | collective-permute-start | bytes 688136 | tf_op jit(solution)/shard_map/ppermute | solution.py:19
  56.1 9.2 %collective-permute-start.15 = (bf16[2,32,1792]{2,1,0:T(8,128)(2,1)S(1)}, bf16[2,32,1792]{2,1,0:T(8,128)(2,1)S(1)}, u32[]{:S(2)}, u32[]{:S(2)}) collective-permute-start(bf16[2,32,1792]{2,1,0:T(8,128)(2,1)S(1)} %get-tuple-element.30), channel_id=1, source_target_pairs={{0,96},{32,64},{64,32},{96,0},{1,97},{33,65},{65,33},{97,1},{2,98}... | collective-permute-start | bytes 688136 | tf_op jit(solution)/shard_map/ppermute | solution.py:19
  56.4 9.0 %collective-permute-start.14 = (bf16[2,32,1792]{2,1,0:T(8,128)(2,1)S(1)}, bf16[2,32,1792]{2,1,0:T(8,128)(2,1)S(1)}, u32[]{:S(2)}, u32[]{:S(2)}) collective-permute-start(bf16[2,32,1792]{2,1,0:T(8,128)(2,1)S(1)} %get-tuple-element.29), channel_id=1, source_target_pairs={{0,32},{32,0},{64,96},{96,64},{1,33},{33,1},{65,97},{97,65},{2,34}... | collective-permute-start | bytes 688136 | tf_op jit(solution)/shard_map/ppermute | solution.py:19
  58.7 11.8 %collective-permute-start.12 = (bf16[2,32,1792]{2,1,0:T(8,128)(2,1)S(1)}, bf16[2,32,1792]{2,1,0:T(8,128)(2,1)S(1)}, u32[]{:S(2)}, u32[]{:S(2)}) collective-permute-start(bf16[2,32,1792]{2,1,0:T(8,128)(2,1)S(1)} %get-tuple-element.40), channel_id=1, source_target_pairs={{0,128},{128,0},{1,129},{129,1},{2,130},{130,2},{3,131},{131,3},{4... | collective-permute-start | bytes 688136 | tf_op jit(solution)/shard_map/ppermute | solution.py:19
  65.4 13.8 %collective-permute-start.17 = (bf16[2,32,1792]{2,1,0:T(8,128)(2,1)S(1)}, bf16[2,32,1792]{2,1,0:T(8,128)(2,1)S(1)}, u32[]{:S(2)}, u32[]{:S(2)}) collective-permute-start(bf16[2,32,1792]{2,1,0:T(8,128)(2,1)S(1)} %get-tuple-element.42), channel_id=1, source_target_pairs={{0,128},{128,0},{1,129},{129,1},{2,130},{130,2},{3,131},{131,3},{4... | collective-permute-start | bytes 688136 | tf_op jit(solution)/shard_map/ppermute | solution.py:19
  80.2 22.8 %collective-permute-start.18 = (bf16[2,64,3584]{2,1,0:T(8,128)(2,1)S(1)}, bf16[2,64,3584]{2,1,0:T(8,128)(2,1)S(1)}, u32[]{:S(2)}, u32[]{:S(2)}) collective-permute-start(bf16[2,64,3584]{2,1,0:T(8,128)(2,1)S(1)} %maximum_maximum_fusion), channel_id=1, source_target_pairs={{0,32},{32,0},{64,96},{96,64},{1,33},{33,1},{65,97},{97,65},{2,34}... | collective-permute-start | bytes 2752520 | tf_op jit(solution)/shard_map/ppermute | solution.py:19
  82.8 20.2 %collective-permute-start.19 = (bf16[2,64,3584]{2,1,0:T(8,128)(2,1)S(1)}, bf16[2,64,3584]{2,1,0:T(8,128)(2,1)S(1)}, u32[]{:S(2)}, u32[]{:S(2)}) collective-permute-start(bf16[2,64,3584]{2,1,0:T(8,128)(2,1)S(1)} %maximum_maximum_fusion), channel_id=1, source_target_pairs={{0,96},{32,64},{64,32},{96,0},{1,97},{33,65},{65,33},{97,1},{2,98}... | collective-permute-start | bytes 2752520 | tf_op jit(solution)/shard_map/ppermute | solution.py:19
  84.2 22.4 %collective-permute-start.27 = (bf16[2,64,3584]{2,1,0:T(8,128)(2,1)S(1)}, bf16[2,64,3584]{2,1,0:T(8,128)(2,1)S(1)}, u32[]{:S(2)}, u32[]{:S(2)}) collective-permute-start(bf16[2,64,3584]{2,1,0:T(8,128)(2,1)S(1)} %maximum_maximum_fusion), channel_id=1, source_target_pairs={{0,16},{16,0},{1,17},{17,1},{2,18},{18,2},{3,19},{19,3},{4,20},{20... | collective-permute-start | bytes 2752520 | tf_op jit(solution)/shard_map/ppermute | solution.py:19
  84.3 11.6 %collective-permute-start.20 = (bf16[2,64,896]{2,1,0:T(8,128)(2,1)S(1)}, bf16[2,64,896]{2,1,0:T(8,128)(2,1)S(1)}, u32[]{:S(2)}, u32[]{:S(2)}) collective-permute-start(bf16[2,64,896]{2,1,0:T(8,128)(2,1)S(1)} %get-tuple-element.58), channel_id=1, source_target_pairs={{0,1},{1,33},{2,65},{3,97},{16,9},{17,41},{18,73},{19,105},{32,2},... | collective-permute-start | bytes 688136 | tf_op jit(solution)/shard_map/ppermute | solution.py:131
  91.0 12.0 %collective-permute-start.21 = (bf16[2,64,896]{2,1,0:T(8,128)(2,1)S(1)}, bf16[2,64,896]{2,1,0:T(8,128)(2,1)S(1)}, u32[]{:S(2)}, u32[]{:S(2)}) collective-permute-start(bf16[2,64,896]{2,1,0:T(8,128)(2,1)S(1)} %get-tuple-element.57), channel_id=1, source_target_pairs={{0,25},{1,57},{2,89},{3,121},{16,17},{17,49},{18,81},{19,113},{32,... | collective-permute-start | bytes 688136 | tf_op jit(solution)/shard_map/ppermute | solution.py:131
  103.0 7.1 %collective-permute-start.25 = (bf16[2,64,896]{2,1,0:T(8,128)(2,1)S(1)}, bf16[2,64,896]{2,1,0:T(8,128)(2,1)S(1)}, u32[]{:S(2)}, u32[]{:S(2)}) collective-permute-start(bf16[2,64,896]{2,1,0:T(8,128)(2,1)S(1)} %broadcast_select_fusion), channel_id=1, source_target_pairs={{1,2},{2,1},{5,6},{6,5},{9,10},{10,9},{13,14},{14,13},{17,18},{18,... | collective-permute-start | bytes 688136 | tf_op jit(solution)/shard_map/ppermute | solution.py:143
  103.7 23.5 %collective-permute-start.26 = (bf16[2,64,896]{2,1,0:T(8,128)(2,1)S(1)}, bf16[2,64,896]{2,1,0:T(8,128)(2,1)S(1)}, u32[]{:S(2)}, u32[]{:S(2)}) collective-permute-start(bf16[2,64,896]{2,1,0:T(8,128)(2,1)S(1)} %broadcast_select_fusion), channel_id=1, source_target_pairs={{1,3},{2,0},{5,7},{6,4},{9,11},{10,8},{13,15},{14,12},{17,19},{18,... | collective-permute-start | bytes 688136 | tf_op jit(solution)/shard_map/ppermute | solution.py:144
  105.0 25.0 %collective-permute-start.24 = (bf16[2,64,896]{2,1,0:T(8,128)(2,1)S(1)}, bf16[2,64,896]{2,1,0:T(8,128)(2,1)S(1)}, u32[]{:S(2)}, u32[]{:S(2)}) collective-permute-start(bf16[2,64,896]{2,1,0:T(8,128)(2,1)S(1)} %broadcast_select_fusion), channel_id=1, source_target_pairs={{1,0},{2,3},{5,4},{6,7},{9,8},{10,11},{13,12},{14,15},{17,16},{18,... | collective-permute-start | bytes 688136 | tf_op jit(solution)/shard_map/ppermute | solution.py:142
  106.3 23.8 %collective-permute-start.22 = (bf16[64,3584]{1,0:T(8,128)(2,1)S(1)}, bf16[64,3584]{1,0:T(8,128)(2,1)S(1)}, u32[]{:S(2)}, u32[]{:S(2)}) collective-permute-start(bf16[64,3584]{1,0:T(8,128)(2,1)S(1)} %slice_bitcast_fusion.5), channel_id=1, source_target_pairs={{0,96},{32,64},{64,32},{96,0},{1,97},{33,65},{65,33},{97,1},{2,98}... | collective-permute-start | bytes 1376264 | tf_op jit(solution)/shard_map/ppermute | solution.py:19
  106.7 23.5 %collective-permute-start.23 = (bf16[64,3584]{1,0:T(8,128)(2,1)S(1)}, bf16[64,3584]{1,0:T(8,128)(2,1)S(1)}, u32[]{:S(2)}, u32[]{:S(2)}) collective-permute-start(bf16[64,3584]{1,0:T(8,128)(2,1)S(1)} %slice_bitcast_fusion.4), channel_id=1, source_target_pairs={{0,32},{32,0},{64,96},{96,64},{1,33},{33,1},{65,97},{97,65},{2,34}... | collective-permute-start | bytes 1376264 | tf_op jit(solution)/shard_map/ppermute | solution.py:19
  110.1 42.8 %collective-permute-start.28 = (bf16[2,2,64,3584]{3,2,1,0:T(8,128)(2,1)S(1)}, bf16[2,2,64,3584]{3,2,1,0:T(8,128)(2,1)S(1)}, u32[]{:S(2)}, u32[]{:S(2)}) collective-permute-start(bf16[2,2,64,3584]{3,2,1,0:T(8,128)(2,1)S(1)} %pad_maximum_fusion.1), channel_id=1, source_target_pairs={{0,16},{16,0},{1,17},{17,1},{2,18},{18,2},{3,19},{19,3},{4,20},{20... | collective-permute-start | bytes 5505032 | tf_op jit(solution)/shard_map/ppermute | solution.py:19
  130.2 13.5 %collective-permute-start.33 = (bf16[2,2,64,896]{3,2,1,0:T(8,128)(2,1)S(1)}, bf16[2,2,64,896]{3,2,1,0:T(8,128)(2,1)S(1)}, u32[]{:S(2)}, u32[]{:S(2)}) collective-permute-start(bf16[2,2,64,896]{3,2,1,0:T(8,128)(2,1)S(1)} %pad_maximum_fusion.3), channel_id=1, source_target_pairs={{0,4},{4,0},{8,12},{12,8},{1,5},{5,1},{9,13},{13,9},{2,6},{6,2},{1... | collective-permute-start | bytes 1376264 | tf_op jit(solution)/shard_map/ppermute | solution.py:19
  130.3 21.1 %collective-permute-start.34 = (bf16[2,2,64,896]{3,2,1,0:T(8,128)(2,1)S(1)}, bf16[2,2,64,896]{3,2,1,0:T(8,128)(2,1)S(1)}, u32[]{:S(2)}, u32[]{:S(2)}) collective-permute-start(bf16[2,2,64,896]{3,2,1,0:T(8,128)(2,1)S(1)} %pad_maximum_fusion.3), channel_id=1, source_target_pairs={{0,12},{4,8},{8,4},{12,0},{1,13},{5,9},{9,5},{13,1},{2,14},{6,10},... | collective-permute-start | bytes 1376264 | tf_op jit(solution)/shard_map/ppermute | solution.py:19
  132.7 20.1 %collective-permute-start.35 = (bf16[2,2,64,896]{3,2,1,0:T(8,128)(2,1)S(1)}, bf16[2,2,64,896]{3,2,1,0:T(8,128)(2,1)S(1)}, u32[]{:S(2)}, u32[]{:S(2)}) collective-permute-start(bf16[2,2,64,896]{3,2,1,0:T(8,128)(2,1)S(1)} %pad_maximum_fusion.3), channel_id=1, source_target_pairs={{0,8},{4,12},{8,0},{12,4},{1,9},{5,13},{9,1},{13,5},{2,10},{6,14},... | collective-permute-start | bytes 1376264 | tf_op jit(solution)/shard_map/ppermute | solution.py:19
  136.8 16.2 %collective-permute-start.29 = (bf16[2,64,3584]{2,1,0:T(8,128)(2,1)S(1)}, bf16[2,64,3584]{2,1,0:T(8,128)(2,1)S(1)}, u32[]{:S(2)}, u32[]{:S(2)}) collective-permute-start(bf16[2,64,3584]{2,1,0:T(8,128)(2,1)S(1)} %pad_maximum_fusion.2), channel_id=1, source_target_pairs={{0,16},{16,0},{1,17},{17,1},{2,18},{18,2},{3,19},{19,3},{4,20},{20... | collective-permute-start | bytes 2752520 | tf_op jit(solution)/shard_map/ppermute | solution.py:19
  156.0 10.9 %collective-permute-start.32 = (bf16[4,64,512]{2,1,0:T(8,128)(2,1)S(1)}, bf16[4,64,512]{2,1,0:T(8,128)(2,1)S(1)}, u32[]{:S(2)}, u32[]{:S(2)}) collective-permute-start(bf16[4,64,512]{2,1,0:T(8,128)(2,1)S(1)} %get-tuple-element.45), channel_id=1, source_target_pairs={{0,8},{4,12},{8,0},{12,4},{1,9},{5,13},{9,1},{13,5},{2,10},{6,14},... | collective-permute-start | bytes 786440 | tf_op jit(solution)/shard_map/ppermute | solution.py:19
  157.9 13.1 %collective-permute-start.31 = (bf16[4,64,512]{2,1,0:T(8,128)(2,1)S(1)}, bf16[4,64,512]{2,1,0:T(8,128)(2,1)S(1)}, u32[]{:S(2)}, u32[]{:S(2)}) collective-permute-start(bf16[4,64,512]{2,1,0:T(8,128)(2,1)S(1)} %get-tuple-element.46), channel_id=1, source_target_pairs={{0,12},{4,8},{8,4},{12,0},{1,13},{5,9},{9,5},{13,1},{2,14},{6,10},... | collective-permute-start | bytes 786440 | tf_op jit(solution)/shard_map/ppermute | solution.py:19
  159.2 11.8 %collective-permute-start.30 = (bf16[4,64,512]{2,1,0:T(8,128)(2,1)S(1)}, bf16[4,64,512]{2,1,0:T(8,128)(2,1)S(1)}, u32[]{:S(2)}, u32[]{:S(2)}) collective-permute-start(bf16[4,64,512]{2,1,0:T(8,128)(2,1)S(1)} %get-tuple-element.44), channel_id=1, source_target_pairs={{0,4},{4,0},{8,12},{12,8},{1,5},{5,1},{9,13},{13,9},{2,6},{6,2},{1... | collective-permute-start | bytes 786440 | tf_op jit(solution)/shard_map/ppermute | solution.py:19
  (13 other events, 102.1 us)

commit v4 on v3

--- a/solution.py
+++ b/solution.py
@@ -55,7 +55,7 @@
     return [
         (
             device(zh, y, core, zh, zl),
-            device(zh, zl, half, (core ^ half) * 2 + (y >> 1), 1 + (y & 1)),
+            device(zh, zl, half, (core ^ half) * 2 + (y >> 1), 1 + ((y ^ zl) & 1)),
         )
         for zh in range(2)
         for y in range(4)
@@ -119,7 +119,7 @@
     part_b = part_of(1)
     got_a = over_y(part_a)
     hidden_a = add_up(part_a, got_a)
-    got_b = over_y(part_b, *got_a, pre_far_b)
+    got_b = over_y(part_b, *got_a)
     hfar_a = swap(hidden_a.astype(BF), "zh", 1)
     both_a = grads(hidden_a, hfar_a, pre_a, pre_far_a)
     hidden_b = add_up(part_b, got_b)
@@ -142,25 +142,29 @@
     edge = lax.ppermute(piece, "zl", [(1, 0), (2, 3)])
     mid = lax.ppermute(piece, "zl", [(1, 2), (2, 1)])
     cross = lax.ppermute(piece, "zl", [(1, 3), (2, 0)])
-    srun = jnp.stack(
-        [lax.select_n(zl, edge, piece, mid, cross), lax.select_n(zl, cross, mid, piece, edge)]
-    )
-    two0, two1, srun = lax.optimization_barrier((two0, two1, srun))
-    got = [swap(srun, "x", k) for k in (1, 3, 2)]
-    ring = jnp.stack([one, three])
-    two = jnp.stack([two0, two1])
-    both_other = swap(both, "core", 1)
-    ring_other = swap(ring, "core", 1)
-    two_other = swap(two, "core", 1)
-
-    def assemble(both, ring, two):
-        full = jnp.zeros((4, 2, 64, 2 * units), BF)
-        for block, k in ((both, 0), (ring[0], 1), (ring[1], 3), (two, 2)):
+    first = lax.select_n(zl, edge, piece, mid, cross)
+    second = lax.select_n(zl, cross, mid, piece, edge)
+    even = (y & 1) == 0
+    srun = jnp.stack([jnp.where(even, first, second), jnp.where(even, second, first)])
+
+    def fill(full, blocks):
+        for block, k in blocks:
             full = put(full, block, y ^ k, 0)
         return full
 
-    full = assemble(both, ring, two)
-    full_other = assemble(both_other, ring_other, two_other)
+    ring = jnp.stack([both, one, three])
+    ring_other = swap(ring, "core", 1)
+    empty = jnp.zeros((4, 2, 64, 2 * units), BF)
+    full = fill(empty, ((both, 0), (one, 1), (three, 3)))
+    two0, two1, srun, full = lax.optimization_barrier((two0, two1, srun, full))
+    near_1 = swap(srun, "x", 1)
+    near_3 = swap(srun, "x", 3)
+    two = jnp.stack([two0, two1])
+    full = fill(full, ((two, 2),))
+    two_other = swap(two, "core", 1)
+    full_other = fill(
+        empty, ((ring_other[0], 0), (ring_other[1], 1), (ring_other[2], 3), (two_other, 2))
+    )
 
     partial = jnp.stack(
         [contract_last(f.reshape(512, 2 * units), weights) for f in (full, full_other)]
@@ -168,8 +172,10 @@
     partial = partial.reshape(2, 2, 2, 2, 64, width).transpose(3, 1, 2, 0, 4, 5)
     partial = partial.reshape(4, 4, 64, width)
 
+    near_1, near_3, partial = lax.optimization_barrier((near_1, near_3, partial))
+    across = jnp.stack([swap(near_1[0], "x", 3), swap(near_3[1], "x", 1)])
     slab = put(jnp.zeros((4, 2, 2, 64, half_units), BF), srun, x, 0)
-    for block, k in zip(got, (1, 3, 2)):
+    for block, k in ((near_1, 1), (near_3, 3), (across, 2)):
         slab = put(slab, block, x ^ k, 0)
     gate_all = jnp.stack([full[..., :units], full_other[..., :units]])
     gate_factor = (
@@ -186,7 +192,6 @@
     got = [swap(pick(partial, x ^ k, 0).astype(BF), "x", k) for k in (1, 3, 2)]
     for block in got:
         mine = mine + block.astype(F32)
-    mine = after(mine, gate_factor)
 
     def for_zl(column):
         return pick(mine, (column >> 1) * 2 + ((column & 1) ^ core), 0)

time: 181 us -> 171 us (0.945); the launches traced: 181 us -> 169 us
  waiting for transfers between devices: 83.1 us -> 68.9 us
  local copies, waits for them, and re-layouts: 4.7 us -> 6.97 us
    ppermute x1, waiting for transfers between devices: 16.9 us -> 9.33 us  [shards(): cross = lax.ppermute(piece, 'zl', [(1, 3), (2, 0)])]
    ppermute x2, starting transfers between devices: 9.62 us -> 4.79 us  [shards(): lax.ppermute(both[:, :, half * half_units:(half + 1) * half_units], AXES,...]
    ppermute x34, waiting for transfers between devices: 54.8 us -> 50.1 us  [swap(): return lax.ppermute(block, axis, [(i, i ^ k) for i in range(n)])]
    ppermute x34, starting transfers between devices: 63 us -> 66.4 us  [swap(): return lax.ppermute(block, axis, [(i, i ^ k) for i in range(n)])]
  transfers between devices with their start and end apart: 39 -> 39, of which waited for: 18 -> 17; matrix products, arithmetic and copies ran while one was open for 8% -> 11% of each run, Pallas kernels for 0% -> 0%
where the time goes in v4:
time: 171 us; the launch traced here: 169 us
  starting transfers between devices  74.5 us (44%)
  waiting for transfers between devices  68.9 us (40%)
  matrix products  13.3 us (8%)
  local copies, waits for them, and re-layouts  6.97 us (4%)
  other arithmetic  4.08 us (2%)
    ppermute x34, starting transfers between devices, swap(): return lax.ppermute(block, axis, [(i, i ^ k) for i in range(n)])  66.4 us
    ppermute x34, waiting for transfers between devices, swap(): return lax.ppermute(block, axis, [(i, i ^ k) for i in range(n)])  50.1 us
    ppermute x1, waiting for transfers between devices, shards(): cross = lax.ppermute(piece, 'zl', [(1, 3), (2, 0)])  9.33 us
    ppermute x2, waiting for transfers between devices, shards(): lax.ppermute(both[:, :, half * half_units:(half + 1) * half_units], AXES,...  7.52 us
    dot_general x6, matrix products, contract_last(): lax.dot_general(left, right, (((1,), (1,)), ((), ())), preferred_element_...  6.96 us
    dot_general x1, matrix products, shards(): lax.dot_general(slab.reshape(TOKENS, half_units), gate_all.reshape(TOKENS...  6.29 us
    ppermute x2, starting transfers between devices, shards(): lax.ppermute(both[:, :, half * half_units:(half + 1) * half_units], AXES,...  4.79 us
  transfers between devices with their start and end apart: 39, of which 17 were waited for; matrix products, arithmetic and copies ran while one was open for 11% of the time, Pallas kernels for 0%

profile of v4, /device:TPU:8, one launch (start us, length us, event | category | flops | bytes accessed | tf_op | source)
XLA Modules:
  0.0 169.1 jit_solution(5743962493959457631)
XLA Ops:
  0.6 2.0 %collective-permute-start = (bf16[64,512]{1,0:T(8,128)(2,1)}, bf16[64,512]{1,0:T(8,128)(2,1)S(1)}, u32[]{:S(2)}, u32[]{:S(2)}) collective-permute-start(bf16[64,512]{1,0:T(8,128)(2,1)} %param.6), channel_id=1, source_target_pairs={{0,1},{1,0},{2,3},{3,2},{4,5},{5,4},{6,7},{7,6},{8,9},{9,8},{10,11... | collective-permute-start | bytes 196616 | tf_op jit(solution)/shard_map/ppermute | solution.py:19
  2.6 3.3 %collective-permute-start.1 = (bf16[64,512]{1,0:T(8,128)(2,1)}, bf16[64,512]{1,0:T(8,128)(2,1)S(1)}, u32[]{:S(2)}, u32[]{:S(2)}) collective-permute-start(bf16[64,512]{1,0:T(8,128)(2,1)} %param.6), channel_id=1, source_target_pairs={{0,2},{1,3},{2,0},{3,1},{4,6},{5,7},{6,4},{7,5},{8,10},{9,11},{10,... | collective-permute-start | bytes 196616 | tf_op jit(solution)/shard_map/ppermute | solution.py:19
  7.3 3.5 %collective-permute-done.1 = bf16[64,512]{1,0:T(8,128)(2,1)S(1)} collective-permute-done((bf16[64,512]{1,0:T(8,128)(2,1)}, bf16[64,512]{1,0:T(8,128)(2,1)S(1)}, u32[]{:S(2)}, u32[]{:S(2)}) %collective-permute-start.1) | collective-permute-done | bytes 65568 | tf_op jit(solution)/shard_map/ppermute | solution.py:19
  12.2 1.6 collective-permute-start.4
  13.8 2.1 %collective-permute-start.5 = (bf16[2,2,64,512]{3,2,1,0:T(8,128)(2,1)S(1)}, bf16[2,2,64,512]{3,2,1,0:T(8,128)(2,1)S(1)}, u32[]{:S(2)}, u32[]{:S(2)}) collective-permute-start(bf16[2,2,64,512]{3,2,1,0:T(8,128)(2,1)S(1)} %bitcast_dynamic-update-slice_fusion.9), channel_id=1, source_target_pairs={{0,12},{4,8},{8,4},{12,0},{1,13},{5,9},{9,5},{13,1},{2,14},{6,10},... | collective-permute-start | bytes 786440 | tf_op jit(solution)/shard_map/ppermute | solution.py:19
  16.5 5.0 %collective-permute-start.8 = (bf16[2,32,1792]{2,1,0:T(8,128)(2,1)S(1)}, bf16[2,32,1792]{2,1,0:T(8,128)(2,1)S(1)}, u32[]{:S(2)}, u32[]{:S(2)}) collective-permute-start(bf16[2,32,1792]{2,1,0:T(8,128)(2,1)S(1)} %pad_maximum_fusion.4), channel_id=1, source_target_pairs={{0,128},{128,0},{1,129},{129,1},{2,130},{130,2},{3,131},{131,3},{4... | collective-permute-start | bytes 688136 | tf_op jit(solution)/shard_map/ppermute | solution.py:19
  21.6 6.1 %collective-permute-done.8 = bf16[2,32,1792]{2,1,0:T(8,128)(2,1)S(1)} collective-permute-done((bf16[2,32,1792]{2,1,0:T(8,128)(2,1)S(1)}, bf16[2,32,1792]{2,1,0:T(8,128)(2,1)S(1)}, u32[]{:S(2)}, u32[]{:S(2)}) %collective-permute-start.8) | collective-permute-done | bytes 229408 | tf_op jit(solution)/shard_map/ppermute | solution.py:19
  28.1 1.8 %collective-permute-done.7 = bf16[4,2,64,512]{3,2,1,0:T(8,128)(2,1)S(1)} collective-permute-done((bf16[4,2,64,512]{3,2,1,0:T(8,128)(2,1)S(1)}, bf16[4,2,64,512]{3,2,1,0:T(8,128)(2,1)S(1)}, u32[]{:S(2)}, u32[]{:S(2)}) %collective-permute-start.7) | collective-permute-done | bytes 524320 | tf_op jit(solution)/shard_map/ppermute | solution.py:19
  32.8 2.4 %collective-permute-start.10 = (bf16[2,32,1792]{2,1,0:T(8,128)(2,1)S(1)}, bf16[2,32,1792]{2,1,0:T(8,128)(2,1)S(1)}, u32[]{:S(2)}, u32[]{:S(2)}) collective-permute-start(bf16[2,32,1792]{2,1,0:T(8,128)(2,1)S(1)} %get-tuple-element.29), channel_id=1, source_target_pairs={{0,96},{32,64},{64,32},{96,0},{1,97},{33,65},{65,33},{97,1},{2,98}... | collective-permute-start | bytes 688136 | tf_op jit(solution)/shard_map/ppermute | solution.py:19
  36.4 8.1 %collective-permute-start.17 = (bf16[2,32,1792]{2,1,0:T(8,128)(2,1)S(1)}, bf16[2,32,1792]{2,1,0:T(8,128)(2,1)S(1)}, u32[]{:S(2)}, u32[]{:S(2)}) collective-permute-start(bf16[2,32,1792]{2,1,0:T(8,128)(2,1)S(1)} %pad_maximum_fusion.5), channel_id=1, source_target_pairs={{0,128},{128,0},{1,129},{129,1},{2,130},{130,2},{3,131},{131,3},{4... | collective-permute-start | bytes 688136 | tf_op jit(solution)/shard_map/ppermute | solution.py:19
  45.9 3.0 %collective-permute-start.15 = (bf16[2,32,1792]{2,1,0:T(8,128)(2,1)S(1)}, bf16[2,32,1792]{2,1,0:T(8,128)(2,1)S(1)}, u32[]{:S(2)}, u32[]{:S(2)}) collective-permute-start(bf16[2,32,1792]{2,1,0:T(8,128)(2,1)S(1)} %get-tuple-element.33), channel_id=1, source_target_pairs={{0,64},{32,96},{64,0},{96,32},{1,65},{33,97},{65,1},{97,33},{2,66}... | collective-permute-start | bytes 688136 | tf_op jit(solution)/shard_map/ppermute | solution.py:19
  50.6 3.1 %collective-permute-done.17 = bf16[2,32,1792]{2,1,0:T(8,128)(2,1)S(1)} collective-permute-done((bf16[2,32,1792]{2,1,0:T(8,128)(2,1)S(1)}, bf16[2,32,1792]{2,1,0:T(8,128)(2,1)S(1)}, u32[]{:S(2)}, u32[]{:S(2)}) %collective-permute-start.17) | collective-permute-done | bytes 229408 | tf_op jit(solution)/shard_map/ppermute | solution.py:19
  54.0 6.6 %collective-permute-start.12 = (bf16[2,32,1792]{2,1,0:T(8,128)(2,1)S(1)}, bf16[2,32,1792]{2,1,0:T(8,128)(2,1)S(1)}, u32[]{:S(2)}, u32[]{:S(2)}) collective-permute-start(bf16[2,32,1792]{2,1,0:T(8,128)(2,1)S(1)} %get-tuple-element.49), channel_id=1, source_target_pairs={{0,128},{128,0},{1,129},{129,1},{2,130},{130,2},{3,131},{131,3},{4... | collective-permute-start | bytes 688136 | tf_op jit(solution)/shard_map/ppermute | solution.py:19
  60.7 6.7 %collective-permute-start.16 = (bf16[2,32,1792]{2,1,0:T(8,128)(2,1)S(1)}, bf16[2,32,1792]{2,1,0:T(8,128)(2,1)S(1)}, u32[]{:S(2)}, u32[]{:S(2)}) collective-permute-start(bf16[2,32,1792]{2,1,0:T(8,128)(2,1)S(1)} %get-tuple-element.51), channel_id=1, source_target_pairs={{0,128},{128,0},{1,129},{129,1},{2,130},{130,2},{3,131},{131,3},{4... | collective-permute-start | bytes 688136 | tf_op jit(solution)/shard_map/ppermute | solution.py:19
  68.1 13.4 %collective-permute-done.16 = bf16[2,32,1792]{2,1,0:T(8,128)(2,1)S(1)} collective-permute-done((bf16[2,32,1792]{2,1,0:T(8,128)(2,1)S(1)}, bf16[2,32,1792]{2,1,0:T(8,128)(2,1)S(1)}, u32[]{:S(2)}, u32[]{:S(2)}) %collective-permute-start.16) | collective-permute-done | bytes 229408 | tf_op jit(solution)/shard_map/ppermute | solution.py:19
  85.3 3.4 %collective-permute-start.20 = (bf16[2,64,896]{2,1,0:T(8,128)(2,1)S(1)}, bf16[2,64,896]{2,1,0:T(8,128)(2,1)S(1)}, u32[]{:S(2)}, u32[]{:S(2)}) collective-permute-start(bf16[2,64,896]{2,1,0:T(8,128)(2,1)S(1)} %get-tuple-element.67), channel_id=1, source_target_pairs={{0,1},{1,34},{2,65},{3,98},{16,9},{17,42},{18,73},{19,106},{32,2},... | collective-permute-start | bytes 688136 | tf_op jit(solution)/shard_map/ppermute | solution.py:131
  90.5 2.6 %collective-permute-done.20 = bf16[2,64,896]{2,1,0:T(8,128)(2,1)S(1)} collective-permute-done((bf16[2,64,896]{2,1,0:T(8,128)(2,1)S(1)}, bf16[2,64,896]{2,1,0:T(8,128)(2,1)S(1)}, u32[]{:S(2)}, u32[]{:S(2)}) %collective-permute-start.20) | collective-permute-done | bytes 229408 | tf_op jit(solution)/shard_map/ppermute | solution.py:131
  93.1 4.9 %collective-permute-done.21 = bf16[2,64,896]{2,1,0:T(8,128)(2,1)S(1)} collective-permute-done((bf16[2,64,896]{2,1,0:T(8,128)(2,1)S(1)}, bf16[2,64,896]{2,1,0:T(8,128)(2,1)S(1)}, u32[]{:S(2)}, u32[]{:S(2)}) %collective-permute-start.21) | collective-permute-done | bytes 229408 | tf_op jit(solution)/shard_map/ppermute | solution.py:131
  98.1 5.9 %collective-permute-done.18 = bf16[2,64,3584]{2,1,0:T(8,128)(2,1)S(1)} collective-permute-done((bf16[2,64,3584]{2,1,0:T(8,128)(2,1)}, bf16[2,64,3584]{2,1,0:T(8,128)(2,1)S(1)}, u32[]{:S(2)}, u32[]{:S(2)}) %collective-permute-start.18) | collective-permute-done | bytes 917536 | tf_op jit(solution)/shard_map/ppermute | solution.py:19
  108.5 2.3 %collective-permute-start.23 = (bf16[64,3584]{1,0:T(8,128)(2,1)S(1)}, bf16[64,3584]{1,0:T(8,128)(2,1)S(1)}, u32[]{:S(2)}, u32[]{:S(2)}) collective-permute-start(bf16[64,3584]{1,0:T(8,128)(2,1)S(1)} %slice_bitcast_fusion.4), channel_id=1, source_target_pairs={{0,32},{32,0},{64,96},{96,64},{1,33},{33,1},{65,97},{97,65},{2,34}... | collective-permute-start | bytes 1376264 | tf_op jit(solution)/shard_map/ppermute | solution.py:19
  111.4 9.3 %collective-permute-done.26 = bf16[2,64,896]{2,1,0:T(8,128)(2,1)S(1)} collective-permute-done((bf16[2,64,896]{2,1,0:T(8,128)(2,1)S(1)}, bf16[2,64,896]{2,1,0:T(8,128)(2,1)S(1)}, u32[]{:S(2)}, u32[]{:S(2)}) %collective-permute-start.26) | collective-permute-done | bytes 229408 | tf_op jit(solution)/shard_map/ppermute | solution.py:144
  120.7 1.9 %collective-permute-done.24 = bf16[2,64,896]{2,1,0:T(8,128)(2,1)S(1)} collective-permute-done((bf16[2,64,896]{2,1,0:T(8,128)(2,1)S(1)}, bf16[2,64,896]{2,1,0:T(8,128)(2,1)S(1)}, u32[]{:S(2)}, u32[]{:S(2)}) %collective-permute-start.24) | collective-permute-done | bytes 229408 | tf_op jit(solution)/shard_map/ppermute | solution.py:142
  122.9 2.2 %collective-permute-start.27 = (bf16[2,2,64,896]{3,2,1,0:T(8,128)(2,1)S(1)}, bf16[2,2,64,896]{3,2,1,0:T(8,128)(2,1)S(1)}, u32[]{:S(2)}, u32[]{:S(2)}) collective-permute-start(bf16[2,2,64,896]{3,2,1,0:T(8,128)(2,1)S(1)} %pad_maximum_fusion.3), channel_id=1, source_target_pairs={{0,4},{4,0},{8,12},{12,8},{1,5},{5,1},{9,13},{13,9},{2,6},{6,2},{1... | collective-permute-start | bytes 1376264 | tf_op jit(solution)/shard_map/ppermute | solution.py:19
  129.1 2.1 %fusion.2 = f32[1,2,2,2,64,512]{5,4,3,2,1,0:T(8,128)S(1)} fusion(bf16[2,2,2,64,3584]{4,3,2,1,0:T(8,128)(2,1)S(1)} %bitcast.184, bf16[512,1792]{1,0:T(8,128)(2,1)S(1)} %copy-done.4, bf16[512,1792]{1,0:T(8,128)(2,1)S(1)} %copy-done.5), kind=kOutput, calls=%fused_computation.11 | convolution fusion | flops 1886388224 | bytes 8388608 | tf_op jit(solution)/shard_map/dot_general | solution.py:47
  131.8 2.1 %fusion.3 = f32[1,2,2,2,64,512]{5,4,3,2,1,0:T(8,128)S(1)} fusion(bf16[2,2,2,64,3584]{4,3,2,1,0:T(8,128)(2,1)S(1)} %bitcast.185, bf16[512,1792]{1,0:T(8,128)(2,1)S(1)} %copy-done.4, bf16[512,1792]{1,0:T(8,128)(2,1)S(1)} %copy-done.5), kind=kOutput, calls=%fused_computation.12 | convolution fusion | flops 1886388224 | bytes 8388608 | tf_op jit(solution)/shard_map/dot_general | solution.py:47
  134.5 2.5 %collective-permute-done.28 = bf16[2,2,64,896]{3,2,1,0:T(8,128)(2,1)S(1)} collective-permute-done((bf16[2,2,64,896]{3,2,1,0:T(8,128)(2,1)S(1)}, bf16[2,2,64,896]{3,2,1,0:T(8,128)(2,1)S(1)}, u32[]{:S(2)}, u32[]{:S(2)}) %collective-permute-start.28) | collective-permute-done | bytes 458784 | tf_op jit(solution)/shard_map/ppermute | solution.py:19
  137.1 1.6 collective-permute-start.33
  141.8 2.3 %collective-permute-start.37 = (bf16[2,64,896]{2,1,0:T(8,128)(2,1)S(1)}, bf16[2,64,896]{2,1,0:T(8,128)(2,1)S(1)}, u32[]{:S(2)}, u32[]{:S(2)}) collective-permute-start(bf16[2,64,896]{2,1,0:T(8,128)(2,1)S(1)} %slice_bitcast_fusion.7), channel_id=1, source_target_pairs={{0,12},{4,8},{8,4},{12,0},{1,13},{5,9},{9,5},{13,1},{2,14},{6,10},... | collective-permute-start | bytes 688136 | tf_op jit(solution)/shard_map/ppermute | solution.py:19
  144.6 10.1 %collective-permute-done.38 = bf16[2,64,896]{2,1,0:T(8,128)(2,1)S(1)} collective-permute-done((bf16[2,64,896]{2,1,0:T(8,128)(2,1)S(1)}, bf16[2,64,896]{2,1,0:T(8,128)(2,1)S(1)}, u32[]{:S(2)}, u32[]{:S(2)}) %collective-permute-start.38) | collective-permute-done | bytes 229408 | tf_op jit(solution)/shard_map/ppermute | solution.py:19
  155.8 2.1 %collective-permute-start.36 = (bf16[64,512]{1,0:T(8,128)(2,1)S(1)}, bf16[64,512]{1,0:T(8,128)(2,1)S(1)}, u32[]{:S(2)}, u32[]{:S(2)}) collective-permute-start(bf16[64,512]{1,0:T(8,128)(2,1)S(1)} %get-tuple-element.73), channel_id=1, source_target_pairs={{0,3},{1,2},{2,1},{3,0},{4,7},{5,6},{6,5},{7,4},{8,11},{9,10},{10,... | collective-permute-start | bytes 196616 | tf_op jit(solution)/shard_map/ppermute | solution.py:19
  157.9 3.9 %collective-permute-start.35 = (bf16[64,512]{1,0:T(8,128)(2,1)S(1)}, bf16[64,512]{1,0:T(8,128)(2,1)S(1)}, u32[]{:S(2)}, u32[]{:S(2)}) collective-permute-start(bf16[64,512]{1,0:T(8,128)(2,1)S(1)} %get-tuple-element.74), channel_id=1, source_target_pairs={{0,2},{1,3},{2,0},{3,1},{4,6},{5,7},{6,4},{7,5},{8,10},{9,11},{10,... | collective-permute-start | bytes 196616 | tf_op jit(solution)/shard_map/ppermute | solution.py:19
  162.1 6.3 %convolution_multiply_fusion = f32[896,1792]{1,0:T(8,128)} fusion(bf16[1024,896]{1,0:T(8,128)(2,1)S(1)} %bitcast.195, bf16[1024,1792]{1,0:T(8,128)(2,1)S(1)} %bitcast.194), kind=kOutput, calls=%fused_computation | convolution fusion | flops 3289939968 | bytes 11927552 | tf_op jit(solution)/shard_map/dot_general | solution.py:182
  (129 shorter events, 33.5 us)
Async XLA Ops:
  2.6 8.1 %collective-permute-start.1 = (bf16[64,512]{1,0:T(8,128)(2,1)}, bf16[64,512]{1,0:T(8,128)(2,1)S(1)}, u32[]{:S(2)}, u32[]{:S(2)}) collective-permute-start(bf16[64,512]{1,0:T(8,128)(2,1)} %param.6), channel_id=1, source_target_pairs={{0,2},{1,3},{2,0},{3,1},{4,6},{5,7},{6,4},{7,5},{8,10},{9,11},{10,... | collective-permute-start | bytes 196616 | tf_op jit(solution)/shard_map/ppermute | solution.py:19
  12.2 15.6 %collective-permute-start.4 = (bf16[2,2,64,512]{3,2,1,0:T(8,128)(2,1)S(1)}, bf16[2,2,64,512]{3,2,1,0:T(8,128)(2,1)S(1)}, u32[]{:S(2)}, u32[]{:S(2)}) collective-permute-start(bf16[2,2,64,512]{3,2,1,0:T(8,128)(2,1)S(1)} %bitcast_dynamic-update-slice_fusion.9), channel_id=1, source_target_pairs={{0,4},{4,0},{8,12},{12,8},{1,5},{5,1},{9,13},{13,9},{2,6},{6,2},{1... | collective-permute-start | bytes 786440 | tf_op jit(solution)/shard_map/ppermute | solution.py:19
  13.8 14.0 %collective-permute-start.5 = (bf16[2,2,64,512]{3,2,1,0:T(8,128)(2,1)S(1)}, bf16[2,2,64,512]{3,2,1,0:T(8,128)(2,1)S(1)}, u32[]{:S(2)}, u32[]{:S(2)}) collective-permute-start(bf16[2,2,64,512]{3,2,1,0:T(8,128)(2,1)S(1)} %bitcast_dynamic-update-slice_fusion.9), channel_id=1, source_target_pairs={{0,12},{4,8},{8,4},{12,0},{1,13},{5,9},{9,5},{13,1},{2,14},{6,10},... | collective-permute-start | bytes 786440 | tf_op jit(solution)/shard_map/ppermute | solution.py:19
  15.9 12.0 %collective-permute-start.6 = (bf16[2,2,64,512]{3,2,1,0:T(8,128)(2,1)S(1)}, bf16[2,2,64,512]{3,2,1,0:T(8,128)(2,1)S(1)}, u32[]{:S(2)}, u32[]{:S(2)}) collective-permute-start(bf16[2,2,64,512]{3,2,1,0:T(8,128)(2,1)S(1)} %bitcast_dynamic-update-slice_fusion.9), channel_id=1, source_target_pairs={{0,8},{4,12},{8,0},{12,4},{1,9},{5,13},{9,1},{13,5},{2,10},{6,14},... | collective-permute-start | bytes 786440 | tf_op jit(solution)/shard_map/ppermute | solution.py:19
  16.5 11.2 %collective-permute-start.8 = (bf16[2,32,1792]{2,1,0:T(8,128)(2,1)S(1)}, bf16[2,32,1792]{2,1,0:T(8,128)(2,1)S(1)}, u32[]{:S(2)}, u32[]{:S(2)}) collective-permute-start(bf16[2,32,1792]{2,1,0:T(8,128)(2,1)S(1)} %pad_maximum_fusion.4), channel_id=1, source_target_pairs={{0,128},{128,0},{1,129},{129,1},{2,130},{130,2},{3,131},{131,3},{4... | collective-permute-start | bytes 688136 | tf_op jit(solution)/shard_map/ppermute | solution.py:19
  32.3 13.1 %collective-permute-start.9 = (bf16[2,32,1792]{2,1,0:T(8,128)(2,1)S(1)}, bf16[2,32,1792]{2,1,0:T(8,128)(2,1)S(1)}, u32[]{:S(2)}, u32[]{:S(2)}) collective-permute-start(bf16[2,32,1792]{2,1,0:T(8,128)(2,1)S(1)} %get-tuple-element.28), channel_id=1, source_target_pairs={{0,32},{32,0},{64,96},{96,64},{1,33},{33,1},{65,97},{97,65},{2,34}... | collective-permute-start | bytes 688136 | tf_op jit(solution)/shard_map/ppermute | solution.py:19
  32.8 12.6 %collective-permute-start.10 = (bf16[2,32,1792]{2,1,0:T(8,128)(2,1)S(1)}, bf16[2,32,1792]{2,1,0:T(8,128)(2,1)S(1)}, u32[]{:S(2)}, u32[]{:S(2)}) collective-permute-start(bf16[2,32,1792]{2,1,0:T(8,128)(2,1)S(1)} %get-tuple-element.29), channel_id=1, source_target_pairs={{0,96},{32,64},{64,32},{96,0},{1,97},{33,65},{65,33},{97,1},{2,98}... | collective-permute-start | bytes 688136 | tf_op jit(solution)/shard_map/ppermute | solution.py:19
  35.2 10.7 %collective-permute-start.11 = (bf16[2,32,1792]{2,1,0:T(8,128)(2,1)S(1)}, bf16[2,32,1792]{2,1,0:T(8,128)(2,1)S(1)}, u32[]{:S(2)}, u32[]{:S(2)}) collective-permute-start(bf16[2,32,1792]{2,1,0:T(8,128)(2,1)S(1)} %get-tuple-element.30), channel_id=1, source_target_pairs={{0,64},{32,96},{64,0},{96,32},{1,65},{33,97},{65,1},{97,33},{2,66}... | collective-permute-start | bytes 688136 | tf_op jit(solution)/shard_map/ppermute | solution.py:19
  36.4 17.3 %collective-permute-start.17 = (bf16[2,32,1792]{2,1,0:T(8,128)(2,1)S(1)}, bf16[2,32,1792]{2,1,0:T(8,128)(2,1)S(1)}, u32[]{:S(2)}, u32[]{:S(2)}) collective-permute-start(bf16[2,32,1792]{2,1,0:T(8,128)(2,1)S(1)} %pad_maximum_fusion.5), channel_id=1, source_target_pairs={{0,128},{128,0},{1,129},{129,1},{2,130},{130,2},{3,131},{131,3},{4... | collective-permute-start | bytes 688136 | tf_op jit(solution)/shard_map/ppermute | solution.py:19
  45.9 14.7 %collective-permute-start.15 = (bf16[2,32,1792]{2,1,0:T(8,128)(2,1)S(1)}, bf16[2,32,1792]{2,1,0:T(8,128)(2,1)S(1)}, u32[]{:S(2)}, u32[]{:S(2)}) collective-permute-start(bf16[2,32,1792]{2,1,0:T(8,128)(2,1)S(1)} %get-tuple-element.33), channel_id=1, source_target_pairs={{0,64},{32,96},{64,0},{96,32},{1,65},{33,97},{65,1},{97,33},{2,66}... | collective-permute-start | bytes 688136 | tf_op jit(solution)/shard_map/ppermute | solution.py:19
  48.9 11.7 %collective-permute-start.14 = (bf16[2,32,1792]{2,1,0:T(8,128)(2,1)S(1)}, bf16[2,32,1792]{2,1,0:T(8,128)(2,1)S(1)}, u32[]{:S(2)}, u32[]{:S(2)}) collective-permute-start(bf16[2,32,1792]{2,1,0:T(8,128)(2,1)S(1)} %get-tuple-element.32), channel_id=1, source_target_pairs={{0,96},{32,64},{64,32},{96,0},{1,97},{33,65},{65,33},{97,1},{2,98}... | collective-permute-start | bytes 688136 | tf_op jit(solution)/shard_map/ppermute | solution.py:19
  49.3 11.3 %collective-permute-start.13 = (bf16[2,32,1792]{2,1,0:T(8,128)(2,1)S(1)}, bf16[2,32,1792]{2,1,0:T(8,128)(2,1)S(1)}, u32[]{:S(2)}, u32[]{:S(2)}) collective-permute-start(bf16[2,32,1792]{2,1,0:T(8,128)(2,1)S(1)} %get-tuple-element.31), channel_id=1, source_target_pairs={{0,32},{32,0},{64,96},{96,64},{1,33},{33,1},{65,97},{97,65},{2,34}... | collective-permute-start | bytes 688136 | tf_op jit(solution)/shard_map/ppermute | solution.py:19
  54.0 13.9 %collective-permute-start.12 = (bf16[2,32,1792]{2,1,0:T(8,128)(2,1)S(1)}, bf16[2,32,1792]{2,1,0:T(8,128)(2,1)S(1)}, u32[]{:S(2)}, u32[]{:S(2)}) collective-permute-start(bf16[2,32,1792]{2,1,0:T(8,128)(2,1)S(1)} %get-tuple-element.49), channel_id=1, source_target_pairs={{0,128},{128,0},{1,129},{129,1},{2,130},{130,2},{3,131},{131,3},{4... | collective-permute-start | bytes 688136 | tf_op jit(solution)/shard_map/ppermute | solution.py:19
  60.7 20.8 %collective-permute-start.16 = (bf16[2,32,1792]{2,1,0:T(8,128)(2,1)S(1)}, bf16[2,32,1792]{2,1,0:T(8,128)(2,1)S(1)}, u32[]{:S(2)}, u32[]{:S(2)}) collective-permute-start(bf16[2,32,1792]{2,1,0:T(8,128)(2,1)S(1)} %get-tuple-element.51), channel_id=1, source_target_pairs={{0,128},{128,0},{1,129},{129,1},{2,130},{130,2},{3,131},{131,3},{4... | collective-permute-start | bytes 688136 | tf_op jit(solution)/shard_map/ppermute | solution.py:19
  82.8 21.1 %collective-permute-start.18 = (bf16[2,64,3584]{2,1,0:T(8,128)(2,1)}, bf16[2,64,3584]{2,1,0:T(8,128)(2,1)S(1)}, u32[]{:S(2)}, u32[]{:S(2)}) collective-permute-start(bf16[2,64,3584]{2,1,0:T(8,128)(2,1)} %get-tuple-element.65), channel_id=1, source_target_pairs={{0,32},{32,0},{64,96},{96,64},{1,33},{33,1},{65,97},{97,65},{2,34}... | collective-permute-start | bytes 2752520 | tf_op jit(solution)/shard_map/ppermute | solution.py:19
  84.2 20.0 %collective-permute-start.19 = (bf16[2,64,3584]{2,1,0:T(8,128)(2,1)}, bf16[2,64,3584]{2,1,0:T(8,128)(2,1)S(1)}, u32[]{:S(2)}, u32[]{:S(2)}) collective-permute-start(bf16[2,64,3584]{2,1,0:T(8,128)(2,1)} %get-tuple-element.65), channel_id=1, source_target_pairs={{0,96},{32,64},{64,32},{96,0},{1,97},{33,65},{65,33},{97,1},{2,98}... | collective-permute-start | bytes 2752520 | tf_op jit(solution)/shard_map/ppermute | solution.py:19
  85.3 7.8 %collective-permute-start.20 = (bf16[2,64,896]{2,1,0:T(8,128)(2,1)S(1)}, bf16[2,64,896]{2,1,0:T(8,128)(2,1)S(1)}, u32[]{:S(2)}, u32[]{:S(2)}) collective-permute-start(bf16[2,64,896]{2,1,0:T(8,128)(2,1)S(1)} %get-tuple-element.67), channel_id=1, source_target_pairs={{0,1},{1,34},{2,65},{3,98},{16,9},{17,42},{18,73},{19,106},{32,2},... | collective-permute-start | bytes 688136 | tf_op jit(solution)/shard_map/ppermute | solution.py:131
  88.7 9.4 %collective-permute-start.21 = (bf16[2,64,896]{2,1,0:T(8,128)(2,1)S(1)}, bf16[2,64,896]{2,1,0:T(8,128)(2,1)S(1)}, u32[]{:S(2)}, u32[]{:S(2)}) collective-permute-start(bf16[2,64,896]{2,1,0:T(8,128)(2,1)S(1)} %get-tuple-element.66), channel_id=1, source_target_pairs={{0,25},{1,58},{2,89},{3,122},{16,17},{17,50},{18,81},{19,114},{32,... | collective-permute-start | bytes 688136 | tf_op jit(solution)/shard_map/ppermute | solution.py:131
  104.9 15.8 %collective-permute-start.26 = (bf16[2,64,896]{2,1,0:T(8,128)(2,1)S(1)}, bf16[2,64,896]{2,1,0:T(8,128)(2,1)S(1)}, u32[]{:S(2)}, u32[]{:S(2)}) collective-permute-start(bf16[2,64,896]{2,1,0:T(8,128)(2,1)S(1)} %broadcast_select_fusion), channel_id=1, source_target_pairs={{1,3},{2,0},{5,7},{6,4},{9,11},{10,8},{13,15},{14,12},{17,19},{18,... | collective-permute-start | bytes 688136 | tf_op jit(solution)/shard_map/ppermute | solution.py:144
  106.2 16.4 %collective-permute-start.24 = (bf16[2,64,896]{2,1,0:T(8,128)(2,1)S(1)}, bf16[2,64,896]{2,1,0:T(8,128)(2,1)S(1)}, u32[]{:S(2)}, u32[]{:S(2)}) collective-permute-start(bf16[2,64,896]{2,1,0:T(8,128)(2,1)S(1)} %broadcast_select_fusion), channel_id=1, source_target_pairs={{1,0},{2,3},{5,4},{6,7},{9,8},{10,11},{13,12},{14,15},{17,16},{18,... | collective-permute-start | bytes 688136 | tf_op jit(solution)/shard_map/ppermute | solution.py:142
  107.6 15.3 %collective-permute-start.22 = (bf16[64,3584]{1,0:T(8,128)(2,1)S(1)}, bf16[64,3584]{1,0:T(8,128)(2,1)S(1)}, u32[]{:S(2)}, u32[]{:S(2)}) collective-permute-start(bf16[64,3584]{1,0:T(8,128)(2,1)S(1)} %slice_bitcast_fusion.5), channel_id=1, source_target_pairs={{0,96},{32,64},{64,32},{96,0},{1,97},{33,65},{65,33},{97,1},{2,98}... | collective-permute-start | bytes 1376264 | tf_op jit(solution)/shard_map/ppermute | solution.py:19
  108.5 14.4 %collective-permute-start.23 = (bf16[64,3584]{1,0:T(8,128)(2,1)S(1)}, bf16[64,3584]{1,0:T(8,128)(2,1)S(1)}, u32[]{:S(2)}, u32[]{:S(2)}) collective-permute-start(bf16[64,3584]{1,0:T(8,128)(2,1)S(1)} %slice_bitcast_fusion.4), channel_id=1, source_target_pairs={{0,32},{32,0},{64,96},{96,64},{1,33},{33,1},{65,97},{97,65},{2,34}... | collective-permute-start | bytes 1376264 | tf_op jit(solution)/shard_map/ppermute | solution.py:19
  111.3 19.9 %collective-permute-start.29 = (bf16[3,2,64,3584]{3,2,1,0:T(8,128)(2,1)S(1)}, bf16[3,2,64,3584]{3,2,1,0:T(8,128)(2,1)S(1)}, u32[]{:S(2)}, u32[]{:S(2)}) collective-permute-start(bf16[3,2,64,3584]{3,2,1,0:T(8,128)(2,1)S(1)} %pad_maximum_fusion.1), channel_id=1, source_target_pairs={{0,16},{16,0},{1,17},{17,1},{2,18},{18,2},{3,19},{19,3},{4,20},{20... | collective-permute-start | bytes 8257544 | tf_op jit(solution)/shard_map/ppermute | solution.py:19
  122.9 11.7 %collective-permute-start.27 = (bf16[2,2,64,896]{3,2,1,0:T(8,128)(2,1)S(1)}, bf16[2,2,64,896]{3,2,1,0:T(8,128)(2,1)S(1)}, u32[]{:S(2)}, u32[]{:S(2)}) collective-permute-start(bf16[2,2,64,896]{3,2,1,0:T(8,128)(2,1)S(1)} %pad_maximum_fusion.3), channel_id=1, source_target_pairs={{0,4},{4,0},{8,12},{12,8},{1,5},{5,1},{9,13},{13,9},{2,6},{6,2},{1... | collective-permute-start | bytes 1376264 | tf_op jit(solution)/shard_map/ppermute | solution.py:19
  125.1 12.0 %collective-permute-start.28 = (bf16[2,2,64,896]{3,2,1,0:T(8,128)(2,1)S(1)}, bf16[2,2,64,896]{3,2,1,0:T(8,128)(2,1)S(1)}, u32[]{:S(2)}, u32[]{:S(2)}) collective-permute-start(bf16[2,2,64,896]{3,2,1,0:T(8,128)(2,1)S(1)} %pad_maximum_fusion.3), channel_id=1, source_target_pairs={{0,12},{4,8},{8,4},{12,0},{1,13},{5,9},{9,5},{13,1},{2,14},{6,10},... | collective-permute-start | bytes 1376264 | tf_op jit(solution)/shard_map/ppermute | solution.py:19
  137.1 18.4 %collective-permute-start.33 = (bf16[4,64,512]{2,1,0:T(8,128)(2,1)S(1)}, bf16[4,64,512]{2,1,0:T(8,128)(2,1)S(1)}, u32[]{:S(2)}, u32[]{:S(2)}) collective-permute-start(bf16[4,64,512]{2,1,0:T(8,128)(2,1)S(1)} %get-tuple-element.54), channel_id=1, source_target_pairs={{0,8},{4,12},{8,0},{12,4},{1,9},{5,13},{9,1},{13,5},{2,10},{6,14},... | collective-permute-start | bytes 786440 | tf_op jit(solution)/shard_map/ppermute | solution.py:19
  138.7 16.9 %collective-permute-start.32 = (bf16[4,64,512]{2,1,0:T(8,128)(2,1)S(1)}, bf16[4,64,512]{2,1,0:T(8,128)(2,1)S(1)}, u32[]{:S(2)}, u32[]{:S(2)}) collective-permute-start(bf16[4,64,512]{2,1,0:T(8,128)(2,1)S(1)} %get-tuple-element.55), channel_id=1, source_target_pairs={{0,12},{4,8},{8,4},{12,0},{1,13},{5,9},{9,5},{13,1},{2,14},{6,10},... | collective-permute-start | bytes 786440 | tf_op jit(solution)/shard_map/ppermute | solution.py:19
  139.6 16.0 %collective-permute-start.31 = (bf16[4,64,512]{2,1,0:T(8,128)(2,1)S(1)}, bf16[4,64,512]{2,1,0:T(8,128)(2,1)S(1)}, u32[]{:S(2)}, u32[]{:S(2)}) collective-permute-start(bf16[4,64,512]{2,1,0:T(8,128)(2,1)S(1)} %get-tuple-element.53), channel_id=1, source_target_pairs={{0,4},{4,0},{8,12},{12,8},{1,5},{5,1},{9,13},{13,9},{2,6},{6,2},{1... | collective-permute-start | bytes 786440 | tf_op jit(solution)/shard_map/ppermute | solution.py:19
  140.8 13.9 %collective-permute-start.38 = (bf16[2,64,896]{2,1,0:T(8,128)(2,1)S(1)}, bf16[2,64,896]{2,1,0:T(8,128)(2,1)S(1)}, u32[]{:S(2)}, u32[]{:S(2)}) collective-permute-start(bf16[2,64,896]{2,1,0:T(8,128)(2,1)S(1)} %slice_bitcast_fusion.6), channel_id=1, source_target_pairs={{0,4},{4,0},{8,12},{12,8},{1,5},{5,1},{9,13},{13,9},{2,6},{6,2},{1... | collective-permute-start | bytes 688136 | tf_op jit(solution)/shard_map/ppermute | solution.py:19
  141.8 13.7 %collective-permute-start.37 = (bf16[2,64,896]{2,1,0:T(8,128)(2,1)S(1)}, bf16[2,64,896]{2,1,0:T(8,128)(2,1)S(1)}, u32[]{:S(2)}, u32[]{:S(2)}) collective-permute-start(bf16[2,64,896]{2,1,0:T(8,128)(2,1)S(1)} %slice_bitcast_fusion.7), channel_id=1, source_target_pairs={{0,12},{4,8},{8,4},{12,0},{1,13},{5,9},{9,5},{13,1},{2,14},{6,10},... | collective-permute-start | bytes 688136 | tf_op jit(solution)/shard_map/ppermute | solution.py:19
  155.8 12.6 %collective-permute-start.36 = (bf16[64,512]{1,0:T(8,128)(2,1)S(1)}, bf16[64,512]{1,0:T(8,128)(2,1)S(1)}, u32[]{:S(2)}, u32[]{:S(2)}) collective-permute-start(bf16[64,512]{1,0:T(8,128)(2,1)S(1)} %get-tuple-element.73), channel_id=1, source_target_pairs={{0,3},{1,2},{2,1},{3,0},{4,7},{5,6},{6,5},{7,4},{8,11},{9,10},{10,... | collective-permute-start | bytes 196616 | tf_op jit(solution)/shard_map/ppermute | solution.py:19
  157.9 10.5 %collective-permute-start.35 = (bf16[64,512]{1,0:T(8,128)(2,1)S(1)}, bf16[64,512]{1,0:T(8,128)(2,1)S(1)}, u32[]{:S(2)}, u32[]{:S(2)}) collective-permute-start(bf16[64,512]{1,0:T(8,128)(2,1)S(1)} %get-tuple-element.74), channel_id=1, source_target_pairs={{0,2},{1,3},{2,0},{3,1},{4,6},{5,7},{6,4},{7,5},{8,10},{9,11},{10,... | collective-permute-start | bytes 196616 | tf_op jit(solution)/shard_map/ppermute | solution.py:19
  (13 other events, 55.0 us)

commit v5 on v4

--- a/solution.py
+++ b/solution.py
@@ -175,18 +175,17 @@
     near_1, near_3, partial = lax.optimization_barrier((near_1, near_3, partial))
     across = jnp.stack([swap(near_1[0], "x", 3), swap(near_3[1], "x", 1)])
     slab = put(jnp.zeros((4, 2, 2, 64, half_units), BF), srun, x, 0)
-    for block, k in ((near_1, 1), (near_3, 3), (across, 2)):
+    for block, k in ((near_1, 1), (near_3, 3)):
         slab = put(slab, block, x ^ k, 0)
     gate_all = jnp.stack([full[..., :units], full_other[..., :units]])
-    gate_factor = (
-        lax.dot_general(
-            slab.reshape(TOKENS, half_units),
-            gate_all.reshape(TOKENS, units),
-            (((0,), (0,)), ((), ())),
-            preferred_element_type=F32,
-        )
-        / TOKENS
-    )
+    gate_last = pick(gate_all.reshape(4, 256, units), x ^ 2, 0)
+
+    def contract_first(left, right):
+        return lax.dot_general(left, right, (((0,), (0,)), ((), ())), preferred_element_type=F32)
+
+    early = contract_first(slab.reshape(TOKENS, half_units), gate_all.reshape(TOKENS, units))
+    late = contract_first(across.reshape(256, half_units), gate_last)
+    gate_factor = (early + late) / TOKENS
 
     mine = pick(partial, x, 0)
     got = [swap(pick(partial, x ^ k, 0).astype(BF), "x", k) for k in (1, 3, 2)]

time: 171 us -> 169 us (0.988)
  waiting for transfers between devices: 68.9 us -> 65.8 us
    ppermute x34, waiting for transfers between devices: 50.1 us -> 46.8 us  [swap(): return lax.ppermute(block, axis, [(i, i ^ k) for i in range(n)])]
    dot_general x1 -> x2, matrix products: 6.29 us -> 7.5 us  [contract_first(): lax.dot_general(left, right, (((0,), (0,)), ((), ())), preferred_element_...]
  transfers between devices with their start and end apart: 39 -> 39, of which waited for: 17 -> 19; matrix products, arithmetic and copies ran while one was open for 11% -> 11% of each run, Pallas kernels for 0% -> 0%
where the time goes in v5:
time: 169 us; the launch traced here: 167 us
  starting transfers between devices  74.3 us (44%)
  waiting for transfers between devices  65.8 us (39%)
  matrix products  14.5 us (9%)
  local copies, waits for them, and re-layouts  7.01 us (4%)
  other arithmetic  4.08 us (2%)
    ppermute x34, starting transfers between devices, swap(): return lax.ppermute(block, axis, [(i, i ^ k) for i in range(n)])  66.4 us
    ppermute x34, waiting for transfers between devices, swap(): return lax.ppermute(block, axis, [(i, i ^ k) for i in range(n)])  46.8 us
    ppermute x1, waiting for transfers between devices, shards(): cross = lax.ppermute(piece, 'zl', [(1, 3), (2, 0)])  9.33 us
    ppermute x2, waiting for transfers between devices, shards(): lax.ppermute(both[:, :, half * half_units:(half + 1) * half_units], AXES,...  7.66 us
    dot_general x2, matrix products, contract_first(): lax.dot_general(left, right, (((0,), (0,)), ((), ())), preferred_element_...  7.5 us
    dot_general x6, matrix products, contract_last(): lax.dot_general(left, right, (((1,), (1,)), ((), ())), preferred_element_...  6.96 us
    ppermute x2, starting transfers between devices, shards(): lax.ppermute(both[:, :, half * half_units:(half + 1) * half_units], AXES,...  4.66 us
  transfers between devices with their start and end apart: 39, of which 19 were waited for; matrix products, arithmetic and copies ran while one was open for 11% of the time, Pallas kernels for 0%

profile of v5, /device:TPU:8, one launch (start us, length us, event | category | flops | bytes accessed | tf_op | source)
XLA Modules:
  0.0 167.1 jit_solution(7568462062867173440)
XLA Ops:
  0.6 2.0 %collective-permute-start = (bf16[64,512]{1,0:T(8,128)(2,1)}, bf16[64,512]{1,0:T(8,128)(2,1)S(1)}, u32[]{:S(2)}, u32[]{:S(2)}) collective-permute-start(bf16[64,512]{1,0:T(8,128)(2,1)} %param.6), channel_id=1, source_target_pairs={{0,1},{1,0},{2,3},{3,2},{4,5},{5,4},{6,7},{7,6},{8,9},{9,8},{10,11... | collective-permute-start | bytes 196616 | tf_op jit(solution)/shard_map/ppermute | solution.py:19
  2.6 3.3 %collective-permute-start.1 = (bf16[64,512]{1,0:T(8,128)(2,1)}, bf16[64,512]{1,0:T(8,128)(2,1)S(1)}, u32[]{:S(2)}, u32[]{:S(2)}) collective-permute-start(bf16[64,512]{1,0:T(8,128)(2,1)} %param.6), channel_id=1, source_target_pairs={{0,2},{1,3},{2,0},{3,1},{4,6},{5,7},{6,4},{7,5},{8,10},{9,11},{10,... | collective-permute-start | bytes 196616 | tf_op jit(solution)/shard_map/ppermute | solution.py:19
  7.3 3.5 %collective-permute-done.1 = bf16[64,512]{1,0:T(8,128)(2,1)S(1)} collective-permute-done((bf16[64,512]{1,0:T(8,128)(2,1)}, bf16[64,512]{1,0:T(8,128)(2,1)S(1)}, u32[]{:S(2)}, u32[]{:S(2)}) %collective-permute-start.1) | collective-permute-done | bytes 65568 | tf_op jit(solution)/shard_map/ppermute | solution.py:19
  13.8 2.1 %collective-permute-start.5 = (bf16[2,2,64,512]{3,2,1,0:T(8,128)(2,1)S(1)}, bf16[2,2,64,512]{3,2,1,0:T(8,128)(2,1)S(1)}, u32[]{:S(2)}, u32[]{:S(2)}) collective-permute-start(bf16[2,2,64,512]{3,2,1,0:T(8,128)(2,1)S(1)} %bitcast_dynamic-update-slice_fusion.9), channel_id=1, source_target_pairs={{0,12},{4,8},{8,4},{12,0},{1,13},{5,9},{9,5},{13,1},{2,14},{6,10},... | collective-permute-start | bytes 786440 | tf_op jit(solution)/shard_map/ppermute | solution.py:19
  16.5 5.0 %collective-permute-start.8 = (bf16[2,32,1792]{2,1,0:T(8,128)(2,1)S(1)}, bf16[2,32,1792]{2,1,0:T(8,128)(2,1)S(1)}, u32[]{:S(2)}, u32[]{:S(2)}) collective-permute-start(bf16[2,32,1792]{2,1,0:T(8,128)(2,1)S(1)} %pad_maximum_fusion.5), channel_id=1, source_target_pairs={{0,128},{128,0},{1,129},{129,1},{2,130},{130,2},{3,131},{131,3},{4... | collective-permute-start | bytes 688136 | tf_op jit(solution)/shard_map/ppermute | solution.py:19
  21.6 6.1 %collective-permute-done.8 = bf16[2,32,1792]{2,1,0:T(8,128)(2,1)S(1)} collective-permute-done((bf16[2,32,1792]{2,1,0:T(8,128)(2,1)S(1)}, bf16[2,32,1792]{2,1,0:T(8,128)(2,1)S(1)}, u32[]{:S(2)}, u32[]{:S(2)}) %collective-permute-start.8) | collective-permute-done | bytes 229408 | tf_op jit(solution)/shard_map/ppermute | solution.py:19
  28.1 1.8 %collective-permute-done.7 = bf16[4,2,64,512]{3,2,1,0:T(8,128)(2,1)S(1)} collective-permute-done((bf16[4,2,64,512]{3,2,1,0:T(8,128)(2,1)S(1)}, bf16[4,2,64,512]{3,2,1,0:T(8,128)(2,1)S(1)}, u32[]{:S(2)}, u32[]{:S(2)}) %collective-permute-start.7) | collective-permute-done | bytes 524320 | tf_op jit(solution)/shard_map/ppermute | solution.py:19
  32.8 2.4 %collective-permute-start.10 = (bf16[2,32,1792]{2,1,0:T(8,128)(2,1)S(1)}, bf16[2,32,1792]{2,1,0:T(8,128)(2,1)S(1)}, u32[]{:S(2)}, u32[]{:S(2)}) collective-permute-start(bf16[2,32,1792]{2,1,0:T(8,128)(2,1)S(1)} %get-tuple-element.29), channel_id=1, source_target_pairs={{0,96},{32,64},{64,32},{96,0},{1,97},{33,65},{65,33},{97,1},{2,98}... | collective-permute-start | bytes 688136 | tf_op jit(solution)/shard_map/ppermute | solution.py:19
  36.4 8.1 %collective-permute-start.17 = (bf16[2,32,1792]{2,1,0:T(8,128)(2,1)S(1)}, bf16[2,32,1792]{2,1,0:T(8,128)(2,1)S(1)}, u32[]{:S(2)}, u32[]{:S(2)}) collective-permute-start(bf16[2,32,1792]{2,1,0:T(8,128)(2,1)S(1)} %pad_maximum_fusion.6), channel_id=1, source_target_pairs={{0,128},{128,0},{1,129},{129,1},{2,130},{130,2},{3,131},{131,3},{4... | collective-permute-start | bytes 688136 | tf_op jit(solution)/shard_map/ppermute | solution.py:19
  45.9 3.0 %collective-permute-start.15 = (bf16[2,32,1792]{2,1,0:T(8,128)(2,1)S(1)}, bf16[2,32,1792]{2,1,0:T(8,128)(2,1)S(1)}, u32[]{:S(2)}, u32[]{:S(2)}) collective-permute-start(bf16[2,32,1792]{2,1,0:T(8,128)(2,1)S(1)} %get-tuple-element.33), channel_id=1, source_target_pairs={{0,64},{32,96},{64,0},{96,32},{1,65},{33,97},{65,1},{97,33},{2,66}... | collective-permute-start | bytes 688136 | tf_op jit(solution)/shard_map/ppermute | solution.py:19
  50.6 3.1 %collective-permute-done.17 = bf16[2,32,1792]{2,1,0:T(8,128)(2,1)S(1)} collective-permute-done((bf16[2,32,1792]{2,1,0:T(8,128)(2,1)S(1)}, bf16[2,32,1792]{2,1,0:T(8,128)(2,1)S(1)}, u32[]{:S(2)}, u32[]{:S(2)}) %collective-permute-start.17) | collective-permute-done | bytes 229408 | tf_op jit(solution)/shard_map/ppermute | solution.py:19
  54.0 6.6 %collective-permute-start.12 = (bf16[2,32,1792]{2,1,0:T(8,128)(2,1)S(1)}, bf16[2,32,1792]{2,1,0:T(8,128)(2,1)S(1)}, u32[]{:S(2)}, u32[]{:S(2)}) collective-permute-start(bf16[2,32,1792]{2,1,0:T(8,128)(2,1)S(1)} %get-tuple-element.49), channel_id=1, source_target_pairs={{0,128},{128,0},{1,129},{129,1},{2,130},{130,2},{3,131},{131,3},{4... | collective-permute-start | bytes 688136 | tf_op jit(solution)/shard_map/ppermute | solution.py:19
  60.7 6.7 %collective-permute-start.16 = (bf16[2,32,1792]{2,1,0:T(8,128)(2,1)S(1)}, bf16[2,32,1792]{2,1,0:T(8,128)(2,1)S(1)}, u32[]{:S(2)}, u32[]{:S(2)}) collective-permute-start(bf16[2,32,1792]{2,1,0:T(8,128)(2,1)S(1)} %get-tuple-element.51), channel_id=1, source_target_pairs={{0,128},{128,0},{1,129},{129,1},{2,130},{130,2},{3,131},{131,3},{4... | collective-permute-start | bytes 688136 | tf_op jit(solution)/shard_map/ppermute | solution.py:19
  68.1 13.4 %collective-permute-done.16 = bf16[2,32,1792]{2,1,0:T(8,128)(2,1)S(1)} collective-permute-done((bf16[2,32,1792]{2,1,0:T(8,128)(2,1)S(1)}, bf16[2,32,1792]{2,1,0:T(8,128)(2,1)S(1)}, u32[]{:S(2)}, u32[]{:S(2)}) %collective-permute-start.16) | collective-permute-done | bytes 229408 | tf_op jit(solution)/shard_map/ppermute | solution.py:19
  85.4 3.4 %collective-permute-start.20 = (bf16[2,64,896]{2,1,0:T(8,128)(2,1)S(1)}, bf16[2,64,896]{2,1,0:T(8,128)(2,1)S(1)}, u32[]{:S(2)}, u32[]{:S(2)}) collective-permute-start(bf16[2,64,896]{2,1,0:T(8,128)(2,1)S(1)} %get-tuple-element.67), channel_id=1, source_target_pairs={{0,1},{1,34},{2,65},{3,98},{16,9},{17,42},{18,73},{19,106},{32,2},... | collective-permute-start | bytes 688136 | tf_op jit(solution)/shard_map/ppermute | solution.py:131
  90.4 2.7 %collective-permute-done.20 = bf16[2,64,896]{2,1,0:T(8,128)(2,1)S(1)} collective-permute-done((bf16[2,64,896]{2,1,0:T(8,128)(2,1)S(1)}, bf16[2,64,896]{2,1,0:T(8,128)(2,1)S(1)}, u32[]{:S(2)}, u32[]{:S(2)}) %collective-permute-start.20) | collective-permute-done | bytes 229408 | tf_op jit(solution)/shard_map/ppermute | solution.py:131
  93.2 4.9 %collective-permute-done.21 = bf16[2,64,896]{2,1,0:T(8,128)(2,1)S(1)} collective-permute-done((bf16[2,64,896]{2,1,0:T(8,128)(2,1)S(1)}, bf16[2,64,896]{2,1,0:T(8,128)(2,1)S(1)}, u32[]{:S(2)}, u32[]{:S(2)}) %collective-permute-start.21) | collective-permute-done | bytes 229408 | tf_op jit(solution)/shard_map/ppermute | solution.py:131
  98.1 5.9 %collective-permute-done.18 = bf16[2,64,3584]{2,1,0:T(8,128)(2,1)S(1)} collective-permute-done((bf16[2,64,3584]{2,1,0:T(8,128)(2,1)}, bf16[2,64,3584]{2,1,0:T(8,128)(2,1)S(1)}, u32[]{:S(2)}, u32[]{:S(2)}) %collective-permute-start.18) | collective-permute-done | bytes 917536 | tf_op jit(solution)/shard_map/ppermute | solution.py:19
  108.5 2.3 %collective-permute-start.23 = (bf16[64,3584]{1,0:T(8,128)(2,1)S(1)}, bf16[64,3584]{1,0:T(8,128)(2,1)S(1)}, u32[]{:S(2)}, u32[]{:S(2)}) collective-permute-start(bf16[64,3584]{1,0:T(8,128)(2,1)S(1)} %slice_bitcast_fusion.4), channel_id=1, source_target_pairs={{0,32},{32,0},{64,96},{96,64},{1,33},{33,1},{65,97},{97,65},{2,34}... | collective-permute-start | bytes 1376264 | tf_op jit(solution)/shard_map/ppermute | solution.py:19
  111.4 9.3 %collective-permute-done.26 = bf16[2,64,896]{2,1,0:T(8,128)(2,1)S(1)} collective-permute-done((bf16[2,64,896]{2,1,0:T(8,128)(2,1)S(1)}, bf16[2,64,896]{2,1,0:T(8,128)(2,1)S(1)}, u32[]{:S(2)}, u32[]{:S(2)}) %collective-permute-start.26) | collective-permute-done | bytes 229408 | tf_op jit(solution)/shard_map/ppermute | solution.py:144
  120.7 1.9 %collective-permute-done.24 = bf16[2,64,896]{2,1,0:T(8,128)(2,1)S(1)} collective-permute-done((bf16[2,64,896]{2,1,0:T(8,128)(2,1)S(1)}, bf16[2,64,896]{2,1,0:T(8,128)(2,1)S(1)}, u32[]{:S(2)}, u32[]{:S(2)}) %collective-permute-start.24) | collective-permute-done | bytes 229408 | tf_op jit(solution)/shard_map/ppermute | solution.py:142
  122.9 2.2 %collective-permute-start.27 = (bf16[2,2,64,896]{3,2,1,0:T(8,128)(2,1)S(1)}, bf16[2,2,64,896]{3,2,1,0:T(8,128)(2,1)S(1)}, u32[]{:S(2)}, u32[]{:S(2)}) collective-permute-start(bf16[2,2,64,896]{3,2,1,0:T(8,128)(2,1)S(1)} %pad_maximum_fusion.3), channel_id=1, source_target_pairs={{0,4},{4,0},{8,12},{12,8},{1,5},{5,1},{9,13},{13,9},{2,6},{6,2},{1... | collective-permute-start | bytes 1376264 | tf_op jit(solution)/shard_map/ppermute | solution.py:19
  129.1 2.1 %fusion.2 = f32[1,2,2,2,64,512]{5,4,3,2,1,0:T(8,128)S(1)} fusion(bf16[2,2,2,64,3584]{4,3,2,1,0:T(8,128)(2,1)S(1)} %bitcast.186, bf16[512,1792]{1,0:T(8,128)(2,1)S(1)} %copy-done.4, bf16[512,1792]{1,0:T(8,128)(2,1)S(1)} %copy-done.5), kind=kOutput, calls=%fused_computation.11 | convolution fusion | flops 1886388224 | bytes 8388608 | tf_op jit(solution)/shard_map/dot_general | solution.py:47
  131.8 2.1 %fusion.3 = f32[1,2,2,2,64,512]{5,4,3,2,1,0:T(8,128)S(1)} fusion(bf16[2,2,2,64,3584]{4,3,2,1,0:T(8,128)(2,1)S(1)} %bitcast.187, bf16[512,1792]{1,0:T(8,128)(2,1)S(1)} %copy-done.4, bf16[512,1792]{1,0:T(8,128)(2,1)S(1)} %copy-done.5), kind=kOutput, calls=%fused_computation.12 | convolution fusion | flops 1886388224 | bytes 8388608 | tf_op jit(solution)/shard_map/dot_general | solution.py:47
  134.5 2.5 %collective-permute-done.28 = bf16[2,2,64,896]{3,2,1,0:T(8,128)(2,1)S(1)} collective-permute-done((bf16[2,2,64,896]{3,2,1,0:T(8,128)(2,1)S(1)}, bf16[2,2,64,896]{3,2,1,0:T(8,128)(2,1)S(1)}, u32[]{:S(2)}, u32[]{:S(2)}) %collective-permute-start.28) | collective-permute-done | bytes 458784 | tf_op jit(solution)/shard_map/ppermute | solution.py:19
  137.1 1.6 collective-permute-start.33
  141.9 2.3 %collective-permute-start.37 = (bf16[2,64,896]{2,1,0:T(8,128)(2,1)S(1)}, bf16[2,64,896]{2,1,0:T(8,128)(2,1)S(1)}, u32[]{:S(2)}, u32[]{:S(2)}) collective-permute-start(bf16[2,64,896]{2,1,0:T(8,128)(2,1)S(1)} %slice_bitcast_fusion.7), channel_id=1, source_target_pairs={{0,12},{4,8},{8,4},{12,0},{1,13},{5,9},{9,5},{13,1},{2,14},{6,10},... | collective-permute-start | bytes 688136 | tf_op jit(solution)/shard_map/ppermute | solution.py:19
  144.6 3.6 %fusion.62 = f32[896,1792]{1,0:T(8,128)S(1)} fusion(bf16[1024,896]{1,0:T(8,128)(2,1)S(1)} %bitcast.199, bf16[1024,1792]{1,0:T(8,128)(2,1)S(1)} %bitcast.188), kind=kOutput, calls=%fused_computation.139 | convolution fusion | flops 3288334336 | bytes 11927552 | tf_op jit(solution)/shard_map/dot_general | solution.py:184
  148.2 6.5 %collective-permute-done.38 = bf16[2,64,896]{2,1,0:T(8,128)(2,1)S(1)} collective-permute-done((bf16[2,64,896]{2,1,0:T(8,128)(2,1)S(1)}, bf16[2,64,896]{2,1,0:T(8,128)(2,1)S(1)}, u32[]{:S(2)}, u32[]{:S(2)}) %collective-permute-start.38) | collective-permute-done | bytes 229408 | tf_op jit(solution)/shard_map/ppermute | solution.py:19
  155.8 2.1 %collective-permute-start.36 = (bf16[64,512]{1,0:T(8,128)(2,1)S(1)}, bf16[64,512]{1,0:T(8,128)(2,1)S(1)}, u32[]{:S(2)}, u32[]{:S(2)}) collective-permute-start(bf16[64,512]{1,0:T(8,128)(2,1)S(1)} %get-tuple-element.73), channel_id=1, source_target_pairs={{0,3},{1,2},{2,1},{3,0},{4,7},{5,6},{6,5},{7,4},{8,11},{9,10},{10,... | collective-permute-start | bytes 196616 | tf_op jit(solution)/shard_map/ppermute | solution.py:19
  157.9 3.9 %collective-permute-start.35 = (bf16[64,512]{1,0:T(8,128)(2,1)S(1)}, bf16[64,512]{1,0:T(8,128)(2,1)S(1)}, u32[]{:S(2)}, u32[]{:S(2)}) collective-permute-start(bf16[64,512]{1,0:T(8,128)(2,1)S(1)} %get-tuple-element.74), channel_id=1, source_target_pairs={{0,2},{1,3},{2,0},{3,1},{4,6},{5,7},{6,4},{7,5},{8,10},{9,11},{10,... | collective-permute-start | bytes 196616 | tf_op jit(solution)/shard_map/ppermute | solution.py:19
  162.1 3.9 %add_multiply_fusion = f32[896,1792]{1,0:T(8,128)} fusion(f32[896,1792]{1,0:T(8,128)S(1)} %fusion.62, bf16[256,896]{1,0:T(8,128)(2,1)S(1)} %bitcast.198, bf16[4,256,1792]{2,1,0:T(8,128)(2,1)S(1)} %bitcast.189, s32[]{:T(128)S(6)} %select_n.175), kind=kOutput, calls=%fused_computation | convolution fusion | flops 825294848 | bytes 14221316 | tf_op jit(solution)/shard_map/dot_general | solution.py:184
  (130 shorter events, 35.4 us)
Async XLA Ops:
  2.6 8.1 %collective-permute-start.1 = (bf16[64,512]{1,0:T(8,128)(2,1)}, bf16[64,512]{1,0:T(8,128)(2,1)S(1)}, u32[]{:S(2)}, u32[]{:S(2)}) collective-permute-start(bf16[64,512]{1,0:T(8,128)(2,1)} %param.6), channel_id=1, source_target_pairs={{0,2},{1,3},{2,0},{3,1},{4,6},{5,7},{6,4},{7,5},{8,10},{9,11},{10,... | collective-permute-start | bytes 196616 | tf_op jit(solution)/shard_map/ppermute | solution.py:19
  12.2 15.6 %collective-permute-start.4 = (bf16[2,2,64,512]{3,2,1,0:T(8,128)(2,1)S(1)}, bf16[2,2,64,512]{3,2,1,0:T(8,128)(2,1)S(1)}, u32[]{:S(2)}, u32[]{:S(2)}) collective-permute-start(bf16[2,2,64,512]{3,2,1,0:T(8,128)(2,1)S(1)} %bitcast_dynamic-update-slice_fusion.9), channel_id=1, source_target_pairs={{0,4},{4,0},{8,12},{12,8},{1,5},{5,1},{9,13},{13,9},{2,6},{6,2},{1... | collective-permute-start | bytes 786440 | tf_op jit(solution)/shard_map/ppermute | solution.py:19
  13.8 14.0 %collective-permute-start.5 = (bf16[2,2,64,512]{3,2,1,0:T(8,128)(2,1)S(1)}, bf16[2,2,64,512]{3,2,1,0:T(8,128)(2,1)S(1)}, u32[]{:S(2)}, u32[]{:S(2)}) collective-permute-start(bf16[2,2,64,512]{3,2,1,0:T(8,128)(2,1)S(1)} %bitcast_dynamic-update-slice_fusion.9), channel_id=1, source_target_pairs={{0,12},{4,8},{8,4},{12,0},{1,13},{5,9},{9,5},{13,1},{2,14},{6,10},... | collective-permute-start | bytes 786440 | tf_op jit(solution)/shard_map/ppermute | solution.py:19
  15.9 12.0 %collective-permute-start.6 = (bf16[2,2,64,512]{3,2,1,0:T(8,128)(2,1)S(1)}, bf16[2,2,64,512]{3,2,1,0:T(8,128)(2,1)S(1)}, u32[]{:S(2)}, u32[]{:S(2)}) collective-permute-start(bf16[2,2,64,512]{3,2,1,0:T(8,128)(2,1)S(1)} %bitcast_dynamic-update-slice_fusion.9), channel_id=1, source_target_pairs={{0,8},{4,12},{8,0},{12,4},{1,9},{5,13},{9,1},{13,5},{2,10},{6,14},... | collective-permute-start | bytes 786440 | tf_op jit(solution)/shard_map/ppermute | solution.py:19
  16.5 11.2 %collective-permute-start.8 = (bf16[2,32,1792]{2,1,0:T(8,128)(2,1)S(1)}, bf16[2,32,1792]{2,1,0:T(8,128)(2,1)S(1)}, u32[]{:S(2)}, u32[]{:S(2)}) collective-permute-start(bf16[2,32,1792]{2,1,0:T(8,128)(2,1)S(1)} %pad_maximum_fusion.5), channel_id=1, source_target_pairs={{0,128},{128,0},{1,129},{129,1},{2,130},{130,2},{3,131},{131,3},{4... | collective-permute-start | bytes 688136 | tf_op jit(solution)/shard_map/ppermute | solution.py:19
  32.3 13.1 %collective-permute-start.9 = (bf16[2,32,1792]{2,1,0:T(8,128)(2,1)S(1)}, bf16[2,32,1792]{2,1,0:T(8,128)(2,1)S(1)}, u32[]{:S(2)}, u32[]{:S(2)}) collective-permute-start(bf16[2,32,1792]{2,1,0:T(8,128)(2,1)S(1)} %get-tuple-element.28), channel_id=1, source_target_pairs={{0,32},{32,0},{64,96},{96,64},{1,33},{33,1},{65,97},{97,65},{2,34}... | collective-permute-start | bytes 688136 | tf_op jit(solution)/shard_map/ppermute | solution.py:19
  32.8 12.6 %collective-permute-start.10 = (bf16[2,32,1792]{2,1,0:T(8,128)(2,1)S(1)}, bf16[2,32,1792]{2,1,0:T(8,128)(2,1)S(1)}, u32[]{:S(2)}, u32[]{:S(2)}) collective-permute-start(bf16[2,32,1792]{2,1,0:T(8,128)(2,1)S(1)} %get-tuple-element.29), channel_id=1, source_target_pairs={{0,96},{32,64},{64,32},{96,0},{1,97},{33,65},{65,33},{97,1},{2,98}... | collective-permute-start | bytes 688136 | tf_op jit(solution)/shard_map/ppermute | solution.py:19
  35.2 10.7 %collective-permute-start.11 = (bf16[2,32,1792]{2,1,0:T(8,128)(2,1)S(1)}, bf16[2,32,1792]{2,1,0:T(8,128)(2,1)S(1)}, u32[]{:S(2)}, u32[]{:S(2)}) collective-permute-start(bf16[2,32,1792]{2,1,0:T(8,128)(2,1)S(1)} %get-tuple-element.30), channel_id=1, source_target_pairs={{0,64},{32,96},{64,0},{96,32},{1,65},{33,97},{65,1},{97,33},{2,66}... | collective-permute-start | bytes 688136 | tf_op jit(solution)/shard_map/ppermute | solution.py:19
  36.4 17.3 %collective-permute-start.17 = (bf16[2,32,1792]{2,1,0:T(8,128)(2,1)S(1)}, bf16[2,32,1792]{2,1,0:T(8,128)(2,1)S(1)}, u32[]{:S(2)}, u32[]{:S(2)}) collective-permute-start(bf16[2,32,1792]{2,1,0:T(8,128)(2,1)S(1)} %pad_maximum_fusion.6), channel_id=1, source_target_pairs={{0,128},{128,0},{1,129},{129,1},{2,130},{130,2},{3,131},{131,3},{4... | collective-permute-start | bytes 688136 | tf_op jit(solution)/shard_map/ppermute | solution.py:19
  45.9 14.7 %collective-permute-start.15 = (bf16[2,32,1792]{2,1,0:T(8,128)(2,1)S(1)}, bf16[2,32,1792]{2,1,0:T(8,128)(2,1)S(1)}, u32[]{:S(2)}, u32[]{:S(2)}) collective-permute-start(bf16[2,32,1792]{2,1,0:T(8,128)(2,1)S(1)} %get-tuple-element.33), channel_id=1, source_target_pairs={{0,64},{32,96},{64,0},{96,32},{1,65},{33,97},{65,1},{97,33},{2,66}... | collective-permute-start | bytes 688136 | tf_op jit(solution)/shard_map/ppermute | solution.py:19
  48.9 11.7 %collective-permute-start.14 = (bf16[2,32,1792]{2,1,0:T(8,128)(2,1)S(1)}, bf16[2,32,1792]{2,1,0:T(8,128)(2,1)S(1)}, u32[]{:S(2)}, u32[]{:S(2)}) collective-permute-start(bf16[2,32,1792]{2,1,0:T(8,128)(2,1)S(1)} %get-tuple-element.32), channel_id=1, source_target_pairs={{0,96},{32,64},{64,32},{96,0},{1,97},{33,65},{65,33},{97,1},{2,98}... | collective-permute-start | bytes 688136 | tf_op jit(solution)/shard_map/ppermute | solution.py:19
  49.3 11.3 %collective-permute-start.13 = (bf16[2,32,1792]{2,1,0:T(8,128)(2,1)S(1)}, bf16[2,32,1792]{2,1,0:T(8,128)(2,1)S(1)}, u32[]{:S(2)}, u32[]{:S(2)}) collective-permute-start(bf16[2,32,1792]{2,1,0:T(8,128)(2,1)S(1)} %get-tuple-element.31), channel_id=1, source_target_pairs={{0,32},{32,0},{64,96},{96,64},{1,33},{33,1},{65,97},{97,65},{2,34}... | collective-permute-start | bytes 688136 | tf_op jit(solution)/shard_map/ppermute | solution.py:19
  54.0 13.9 %collective-permute-start.12 = (bf16[2,32,1792]{2,1,0:T(8,128)(2,1)S(1)}, bf16[2,32,1792]{2,1,0:T(8,128)(2,1)S(1)}, u32[]{:S(2)}, u32[]{:S(2)}) collective-permute-start(bf16[2,32,1792]{2,1,0:T(8,128)(2,1)S(1)} %get-tuple-element.49), channel_id=1, source_target_pairs={{0,128},{128,0},{1,129},{129,1},{2,130},{130,2},{3,131},{131,3},{4... | collective-permute-start | bytes 688136 | tf_op jit(solution)/shard_map/ppermute | solution.py:19
  60.7 20.8 %collective-permute-start.16 = (bf16[2,32,1792]{2,1,0:T(8,128)(2,1)S(1)}, bf16[2,32,1792]{2,1,0:T(8,128)(2,1)S(1)}, u32[]{:S(2)}, u32[]{:S(2)}) collective-permute-start(bf16[2,32,1792]{2,1,0:T(8,128)(2,1)S(1)} %get-tuple-element.51), channel_id=1, source_target_pairs={{0,128},{128,0},{1,129},{129,1},{2,130},{130,2},{3,131},{131,3},{4... | collective-permute-start | bytes 688136 | tf_op jit(solution)/shard_map/ppermute | solution.py:19
  82.8 21.1 %collective-permute-start.18 = (bf16[2,64,3584]{2,1,0:T(8,128)(2,1)}, bf16[2,64,3584]{2,1,0:T(8,128)(2,1)S(1)}, u32[]{:S(2)}, u32[]{:S(2)}) collective-permute-start(bf16[2,64,3584]{2,1,0:T(8,128)(2,1)} %get-tuple-element.65), channel_id=1, source_target_pairs={{0,32},{32,0},{64,96},{96,64},{1,33},{33,1},{65,97},{97,65},{2,34}... | collective-permute-start | bytes 2752520 | tf_op jit(solution)/shard_map/ppermute | solution.py:19
  84.2 20.0 %collective-permute-start.19 = (bf16[2,64,3584]{2,1,0:T(8,128)(2,1)}, bf16[2,64,3584]{2,1,0:T(8,128)(2,1)S(1)}, u32[]{:S(2)}, u32[]{:S(2)}) collective-permute-start(bf16[2,64,3584]{2,1,0:T(8,128)(2,1)} %get-tuple-element.65), channel_id=1, source_target_pairs={{0,96},{32,64},{64,32},{96,0},{1,97},{33,65},{65,33},{97,1},{2,98}... | collective-permute-start | bytes 2752520 | tf_op jit(solution)/shard_map/ppermute | solution.py:19
  85.4 7.8 %collective-permute-start.20 = (bf16[2,64,896]{2,1,0:T(8,128)(2,1)S(1)}, bf16[2,64,896]{2,1,0:T(8,128)(2,1)S(1)}, u32[]{:S(2)}, u32[]{:S(2)}) collective-permute-start(bf16[2,64,896]{2,1,0:T(8,128)(2,1)S(1)} %get-tuple-element.67), channel_id=1, source_target_pairs={{0,1},{1,34},{2,65},{3,98},{16,9},{17,42},{18,73},{19,106},{32,2},... | collective-permute-start | bytes 688136 | tf_op jit(solution)/shard_map/ppermute | solution.py:131
  88.7 9.4 %collective-permute-start.21 = (bf16[2,64,896]{2,1,0:T(8,128)(2,1)S(1)}, bf16[2,64,896]{2,1,0:T(8,128)(2,1)S(1)}, u32[]{:S(2)}, u32[]{:S(2)}) collective-permute-start(bf16[2,64,896]{2,1,0:T(8,128)(2,1)S(1)} %get-tuple-element.66), channel_id=1, source_target_pairs={{0,25},{1,58},{2,89},{3,122},{16,17},{17,50},{18,81},{19,114},{32,... | collective-permute-start | bytes 688136 | tf_op jit(solution)/shard_map/ppermute | solution.py:131
  104.9 15.8 %collective-permute-start.26 = (bf16[2,64,896]{2,1,0:T(8,128)(2,1)S(1)}, bf16[2,64,896]{2,1,0:T(8,128)(2,1)S(1)}, u32[]{:S(2)}, u32[]{:S(2)}) collective-permute-start(bf16[2,64,896]{2,1,0:T(8,128)(2,1)S(1)} %broadcast_select_fusion), channel_id=1, source_target_pairs={{1,3},{2,0},{5,7},{6,4},{9,11},{10,8},{13,15},{14,12},{17,19},{18,... | collective-permute-start | bytes 688136 | tf_op jit(solution)/shard_map/ppermute | solution.py:144
  106.2 16.4 %collective-permute-start.24 = (bf16[2,64,896]{2,1,0:T(8,128)(2,1)S(1)}, bf16[2,64,896]{2,1,0:T(8,128)(2,1)S(1)}, u32[]{:S(2)}, u32[]{:S(2)}) collective-permute-start(bf16[2,64,896]{2,1,0:T(8,128)(2,1)S(1)} %broadcast_select_fusion), channel_id=1, source_target_pairs={{1,0},{2,3},{5,4},{6,7},{9,8},{10,11},{13,12},{14,15},{17,16},{18,... | collective-permute-start | bytes 688136 | tf_op jit(solution)/shard_map/ppermute | solution.py:142
  107.6 15.3 %collective-permute-start.22 = (bf16[64,3584]{1,0:T(8,128)(2,1)S(1)}, bf16[64,3584]{1,0:T(8,128)(2,1)S(1)}, u32[]{:S(2)}, u32[]{:S(2)}) collective-permute-start(bf16[64,3584]{1,0:T(8,128)(2,1)S(1)} %slice_bitcast_fusion.5), channel_id=1, source_target_pairs={{0,96},{32,64},{64,32},{96,0},{1,97},{33,65},{65,33},{97,1},{2,98}... | collective-permute-start | bytes 1376264 | tf_op jit(solution)/shard_map/ppermute | solution.py:19
  108.5 14.4 %collective-permute-start.23 = (bf16[64,3584]{1,0:T(8,128)(2,1)S(1)}, bf16[64,3584]{1,0:T(8,128)(2,1)S(1)}, u32[]{:S(2)}, u32[]{:S(2)}) collective-permute-start(bf16[64,3584]{1,0:T(8,128)(2,1)S(1)} %slice_bitcast_fusion.4), channel_id=1, source_target_pairs={{0,32},{32,0},{64,96},{96,64},{1,33},{33,1},{65,97},{97,65},{2,34}... | collective-permute-start | bytes 1376264 | tf_op jit(solution)/shard_map/ppermute | solution.py:19
  111.3 19.9 %collective-permute-start.29 = (bf16[3,2,64,3584]{3,2,1,0:T(8,128)(2,1)S(1)}, bf16[3,2,64,3584]{3,2,1,0:T(8,128)(2,1)S(1)}, u32[]{:S(2)}, u32[]{:S(2)}) collective-permute-start(bf16[3,2,64,3584]{3,2,1,0:T(8,128)(2,1)S(1)} %pad_maximum_fusion.1), channel_id=1, source_target_pairs={{0,16},{16,0},{1,17},{17,1},{2,18},{18,2},{3,19},{19,3},{4,20},{20... | collective-permute-start | bytes 8257544 | tf_op jit(solution)/shard_map/ppermute | solution.py:19
  122.9 11.7 %collective-permute-start.27 = (bf16[2,2,64,896]{3,2,1,0:T(8,128)(2,1)S(1)}, bf16[2,2,64,896]{3,2,1,0:T(8,128)(2,1)S(1)}, u32[]{:S(2)}, u32[]{:S(2)}) collective-permute-start(bf16[2,2,64,896]{3,2,1,0:T(8,128)(2,1)S(1)} %pad_maximum_fusion.3), channel_id=1, source_target_pairs={{0,4},{4,0},{8,12},{12,8},{1,5},{5,1},{9,13},{13,9},{2,6},{6,2},{1... | collective-permute-start | bytes 1376264 | tf_op jit(solution)/shard_map/ppermute | solution.py:19
  125.1 12.0 %collective-permute-start.28 = (bf16[2,2,64,896]{3,2,1,0:T(8,128)(2,1)S(1)}, bf16[2,2,64,896]{3,2,1,0:T(8,128)(2,1)S(1)}, u32[]{:S(2)}, u32[]{:S(2)}) collective-permute-start(bf16[2,2,64,896]{3,2,1,0:T(8,128)(2,1)S(1)} %pad_maximum_fusion.3), channel_id=1, source_target_pairs={{0,12},{4,8},{8,4},{12,0},{1,13},{5,9},{9,5},{13,1},{2,14},{6,10},... | collective-permute-start | bytes 1376264 | tf_op jit(solution)/shard_map/ppermute | solution.py:19
  137.1 18.4 %collective-permute-start.33 = (bf16[4,64,512]{2,1,0:T(8,128)(2,1)S(1)}, bf16[4,64,512]{2,1,0:T(8,128)(2,1)S(1)}, u32[]{:S(2)}, u32[]{:S(2)}) collective-permute-start(bf16[4,64,512]{2,1,0:T(8,128)(2,1)S(1)} %get-tuple-element.54), channel_id=1, source_target_pairs={{0,8},{4,12},{8,0},{12,4},{1,9},{5,13},{9,1},{13,5},{2,10},{6,14},... | collective-permute-start | bytes 786440 | tf_op jit(solution)/shard_map/ppermute | solution.py:19
  138.7 16.8 %collective-permute-start.32 = (bf16[4,64,512]{2,1,0:T(8,128)(2,1)S(1)}, bf16[4,64,512]{2,1,0:T(8,128)(2,1)S(1)}, u32[]{:S(2)}, u32[]{:S(2)}) collective-permute-start(bf16[4,64,512]{2,1,0:T(8,128)(2,1)S(1)} %get-tuple-element.55), channel_id=1, source_target_pairs={{0,12},{4,8},{8,4},{12,0},{1,13},{5,9},{9,5},{13,1},{2,14},{6,10},... | collective-permute-start | bytes 786440 | tf_op jit(solution)/shard_map/ppermute | solution.py:19
  139.6 16.0 %collective-permute-start.31 = (bf16[4,64,512]{2,1,0:T(8,128)(2,1)S(1)}, bf16[4,64,512]{2,1,0:T(8,128)(2,1)S(1)}, u32[]{:S(2)}, u32[]{:S(2)}) collective-permute-start(bf16[4,64,512]{2,1,0:T(8,128)(2,1)S(1)} %get-tuple-element.53), channel_id=1, source_target_pairs={{0,4},{4,0},{8,12},{12,8},{1,5},{5,1},{9,13},{13,9},{2,6},{6,2},{1... | collective-permute-start | bytes 786440 | tf_op jit(solution)/shard_map/ppermute | solution.py:19
  140.9 13.8 %collective-permute-start.38 = (bf16[2,64,896]{2,1,0:T(8,128)(2,1)S(1)}, bf16[2,64,896]{2,1,0:T(8,128)(2,1)S(1)}, u32[]{:S(2)}, u32[]{:S(2)}) collective-permute-start(bf16[2,64,896]{2,1,0:T(8,128)(2,1)S(1)} %slice_bitcast_fusion.6), channel_id=1, source_target_pairs={{0,4},{4,0},{8,12},{12,8},{1,5},{5,1},{9,13},{13,9},{2,6},{6,2},{1... | collective-permute-start | bytes 688136 | tf_op jit(solution)/shard_map/ppermute | solution.py:19
  141.9 13.6 %collective-permute-start.37 = (bf16[2,64,896]{2,1,0:T(8,128)(2,1)S(1)}, bf16[2,64,896]{2,1,0:T(8,128)(2,1)S(1)}, u32[]{:S(2)}, u32[]{:S(2)}) collective-permute-start(bf16[2,64,896]{2,1,0:T(8,128)(2,1)S(1)} %slice_bitcast_fusion.7), channel_id=1, source_target_pairs={{0,12},{4,8},{8,4},{12,0},{1,13},{5,9},{9,5},{13,1},{2,14},{6,10},... | collective-permute-start | bytes 688136 | tf_op jit(solution)/shard_map/ppermute | solution.py:19
  155.8 10.2 %collective-permute-start.36 = (bf16[64,512]{1,0:T(8,128)(2,1)S(1)}, bf16[64,512]{1,0:T(8,128)(2,1)S(1)}, u32[]{:S(2)}, u32[]{:S(2)}) collective-permute-start(bf16[64,512]{1,0:T(8,128)(2,1)S(1)} %get-tuple-element.73), channel_id=1, source_target_pairs={{0,3},{1,2},{2,1},{3,0},{4,7},{5,6},{6,5},{7,4},{8,11},{9,10},{10,... | collective-permute-start | bytes 196616 | tf_op jit(solution)/shard_map/ppermute | solution.py:19
  157.9 8.1 %collective-permute-start.35 = (bf16[64,512]{1,0:T(8,128)(2,1)S(1)}, bf16[64,512]{1,0:T(8,128)(2,1)S(1)}, u32[]{:S(2)}, u32[]{:S(2)}) collective-permute-start(bf16[64,512]{1,0:T(8,128)(2,1)S(1)} %get-tuple-element.74), channel_id=1, source_target_pairs={{0,2},{1,3},{2,0},{3,1},{4,6},{5,7},{6,4},{7,5},{8,10},{9,11},{10,... | collective-permute-start | bytes 196616 | tf_op jit(solution)/shard_map/ppermute | solution.py:19
  (13 other events, 57.4 us)
